TPU v7x, 512 devices: a whole 4x8x8 slice. The times are simulated.
512 devices in a mesh: dp: 64 (over x, y, core), frame: 8 (over z).
Axes of the slice: x: 4, y: 8, z: 8, core: 2. Of those that a mesh axis runs over, the one named last changes fastest.
Arguments:
- video_tokens: bfloat16 [64, 8, 256, 1024], P('dp', 'frame'), may hold values from -6 to 6
- text_states: bfloat16 [64, 77, 768], P('dp'), may hold values from -6 to 6
- caption_ids: int32 [64, 77], P('dp'), may hold values from 0 to 49407, as said below
- pair_index: int32 [64], replicated, may hold values from 0 to 63, each once
- logit_scale: float32 [1], replicated, may hold values from 10 to 100
- gain_spatial: float32 [1024], replicated, may hold values from 0.25 to 1.75
- gain_temporal: float32 [1024], replicated, may hold values from 0.25 to 1.75
- gain_video: float32 [1024], replicated, may hold values from 0.25 to 1.75
- gain_text: float32 [768], replicated, may hold values from 0.25 to 1.75
- w_qkv_spatial: bfloat16 [1024, 1536], P('dp'), may hold values from -0.1875 to 0.1875
- w_out_spatial: bfloat16 [512, 1024], P('dp'), may hold values from -0.25 to 0.25
- w_qkv_temporal: bfloat16 [1024, 1536], P('dp'), may hold values from -0.1875 to 0.1875
- w_out_temporal: bfloat16 [512, 1024], P('dp'), may hold values from -0.25 to 0.25
- w_video: bfloat16 [1024, 768], P('dp'), may hold values from -0.1875 to 0.1875
- w_text: bfloat16 [768, 768], P('dp'), may hold values from -0.21875 to 0.21875
Outputs:
- layer_out: bfloat16 [64, 8, 256, 1024], P('dp', None, 'frame')
- video_loss: float32 [64], P('dp')
- text_loss: float32 [64], P('dp')
- grad_pooled: float32 [64, 1024], P('dp')
- grad_text: float32 [64, 768], P('dp')
Inputs may be any that keep to these rules, and one draw needn't show every extreme that they name: `caption_ids`: in each row the ids before the end token lie in 1 to 49406, exactly one entry is the end token 49407, at position 1 to 75, and every entry after it is 0. `pair_index`: every number below 64 appears once.
All inputs are finite; a program needn't handle non-finite values.
Results may differ from a plain program's by a relative error of at most 0.012.
Values may be sent and summed in bfloat16 or wider, within the bound.
No kernel may reach another device: no remote copies, remote signals or barrier semaphores. Data moves between devices by JAX's collectives and lax.ppermute only.
A program may use at most 64 MiB of HBM per device.

v0:
```python
import jax
import jax.numpy as jnp
from jax import lax
from jax.sharding import PartitionSpec as P

HEADS = 8
HD = 64


norm_eps = 1e-05
unit_eps = 1e-06


def layer_norm(values, gain):
    values = values.astype(jnp.float32)
    center = values - jnp.mean(values, axis=-1, keepdims=True)
    spread = jnp.mean(center * center, axis=-1, keepdims=True)
    return center * lax.rsqrt(spread + norm_eps) * gain


def unit_rows(values):
    return values * lax.rsqrt(jnp.sum(values * values, axis=-1, keepdims=True) + unit_eps)


def project(values, weight):
    flat = values.reshape(-1, values.shape[-1])
    result = jnp.dot(flat, weight, preferred_element_type=jnp.float32)
    return result.reshape(values.shape[:-1] + (weight.shape[1],))


def embed_head(values, gain, weight):
    mapped = jnp.dot(
        layer_norm(values, gain), weight.astype(jnp.float32), precision=lax.Precision.HIGHEST
    )
    return unit_rows(mapped)


def on_device(
    video_tokens,
    text_states,
    caption_ids,
    pair_index,
    logit_scale,
    gain_spatial,
    gain_temporal,
    gain_video,
    gain_text,
    w_qkv_spatial,
    w_out_spatial,
    w_qkv_temporal,
    w_out_temporal,
    w_video,
    w_text,
):
    clips = video_tokens.shape[0]
    frames_local = video_tokens.shape[1]
    patches = video_tokens.shape[2]
    gathered_weights = (
        lax.all_gather(w_qkv_spatial, "dp", axis=0, tiled=True),
        lax.all_gather(w_out_spatial, "dp", axis=0, tiled=True),
        lax.all_gather(w_qkv_temporal, "dp", axis=0, tiled=True),
        lax.all_gather(w_out_temporal, "dp", axis=0, tiled=True),
        lax.all_gather(w_video, "dp", axis=0, tiled=True),
        lax.all_gather(w_text, "dp", axis=0, tiled=True),
    )
    qkv_spatial, out_spatial, qkv_temporal, out_temporal, video_weight, text_weight = (
        gathered_weights
    )
    scaling = 1.0 / float(HD) ** 0.5
    normed = layer_norm(video_tokens, gain_spatial).astype(jnp.bfloat16)
    packed = (
        project(normed, qkv_spatial)
        .astype(jnp.bfloat16)
        .reshape(clips, frames_local, patches, 3, HEADS, HD)
    )
    scores = (
        jnp.einsum(
            "cfqhe,cfkhe->cfhqk",
            packed[:, :, :, 0],
            packed[:, :, :, 1],
            preferred_element_type=jnp.float32,
        )
        * scaling
    )
    probs = jax.nn.softmax(scores, axis=-1).astype(jnp.bfloat16)
    mixed = jnp.einsum(
        "cfhqk,cfkhe->cfqhe", probs, packed[:, :, :, 2], preferred_element_type=jnp.float32
    ).astype(jnp.bfloat16)
    mixed = mixed.reshape(clips, frames_local, patches, HEADS * HD)
    spatial = (video_tokens.astype(jnp.float32) + project(mixed, out_spatial)).astype(jnp.bfloat16)
    gathered = lax.all_to_all(spatial, "frame", split_axis=2, concat_axis=1, tiled=True)
    count = gathered.shape[0]
    frames = gathered.shape[1]
    owned = gathered.shape[2]
    normed_time = layer_norm(gathered, gain_temporal).astype(jnp.bfloat16)
    packed_time = (
        project(normed_time, qkv_temporal)
        .astype(jnp.bfloat16)
        .reshape(count, frames, owned, 3, HEADS, HD)
    )
    scores_time = (
        jnp.einsum(
            "cqphe,ckphe->cphqk",
            packed_time[:, :, :, 0],
            packed_time[:, :, :, 1],
            preferred_element_type=jnp.float32,
        )
        * scaling
    )
    probs_time = jax.nn.softmax(scores_time, axis=-1).astype(jnp.bfloat16)
    mixed_time = jnp.einsum(
        "cphqk,ckphe->cqphe",
        probs_time,
        packed_time[:, :, :, 2],
        preferred_element_type=jnp.float32,
    ).astype(jnp.bfloat16)
    mixed_time = mixed_time.reshape(count, frames, owned, HEADS * HD)
    output = (gathered.astype(jnp.float32) + project(mixed_time, out_temporal)).astype(jnp.bfloat16)
    partial_pool = jnp.sum(output.astype(jnp.float32), axis=(1, 2))
    layer_out, partial_pool = (output, partial_pool)
    divisor = float(layer_out.shape[1] * patches)
    end_place = jnp.argmax(caption_ids, axis=1)
    picker = (
        jnp.arange(caption_ids.shape[1], dtype=jnp.int32)[None, :] == end_place[:, None]
    ).astype(jnp.bfloat16)
    text_pool = jnp.einsum("cl,cld->cd", picker, text_states, preferred_element_type=jnp.float32)
    here = lax.axis_index("dp") * clips

    def video_side(values):
        return embed_head(values, gain_video, video_weight)

    def text_side(values):
        return embed_head(values, gain_text, text_weight)

    pooled = lax.psum(partial_pool, "frame") / divisor
    video_mine, video_back = jax.vjp(video_side, pooled)
    text_mine, text_back = jax.vjp(text_side, text_pool)
    video_every, text_every = (
        lax.all_gather(video_mine, "dp", axis=0, tiled=True),
        lax.all_gather(text_mine, "dp", axis=0, tiled=True),
    )
    scale = logit_scale[0]
    total = video_every.shape[0]
    columns = jnp.arange(total, dtype=jnp.int32)
    mine_index = here + jnp.arange(clips, dtype=jnp.int32)
    mine_pairs = lax.dynamic_slice_in_dim(pair_index, here, clips, 0)
    rows_logits = scale * jnp.dot(video_mine, text_every.T, precision=lax.Precision.HIGHEST)
    cols_logits = scale * jnp.dot(video_every, text_mine.T, precision=lax.Precision.HIGHEST)
    mask_rows = (mine_pairs[:, None] == columns[None, :]).astype(jnp.float32)
    mask_cols = (pair_index[:, None] == mine_index[None, :]).astype(jnp.float32)
    row_lse = jax.nn.logsumexp(rows_logits, axis=1)
    col_lse = jax.nn.logsumexp(cols_logits, axis=0)
    video_loss = 0.5 * (row_lse - jnp.sum(mask_rows * rows_logits, axis=1))
    text_loss = 0.5 * (col_lse - jnp.sum(mask_cols * cols_logits, axis=0))
    rows_part = 0.5 * (jnp.exp(rows_logits - row_lse[:, None]) - mask_rows)
    cols_part = 0.5 * (jnp.exp(cols_logits - col_lse[None, :]) - mask_cols)
    video_term = scale * jnp.dot(cols_part, text_mine, precision=lax.Precision.HIGHEST)
    text_term = scale * jnp.dot(rows_part.T, video_mine, precision=lax.Precision.HIGHEST)
    video_got, text_got = (
        lax.psum_scatter(video_term, "dp", scatter_dimension=0, tiled=True),
        lax.psum_scatter(text_term, "dp", scatter_dimension=0, tiled=True),
    )
    grad_video = scale * jnp.dot(rows_part, text_every, precision=lax.Precision.HIGHEST) + video_got
    grad_caption = (
        scale * jnp.dot(cols_part.T, video_every, precision=lax.Precision.HIGHEST) + text_got
    )
    grad_pooled = video_back(grad_video)[0]
    grad_text = text_back(grad_caption)[0]
    return (layer_out, video_loss, text_loss, grad_pooled, grad_text)


def solution(mesh):
    placed = (
        P("dp", "frame", None, None),
        P("dp", None, None),
        P("dp", None),
        P(),
        P(),
        P(),
        P(),
        P(),
        P(),
        P("dp", None),
        P("dp", None),
        P("dp", None),
        P("dp", None),
        P("dp", None),
        P("dp", None),
    )
    return jax.shard_map(
        on_device,
        mesh=mesh,
        in_specs=placed,
        out_specs=(P("dp", None, "frame", None), P("dp"), P("dp"), P("dp", None), P("dp", None)),
        check_vma=False,
    )
```

profile of v0, /device:TPU:1, one launch (start us, length us, event | category | flops | bytes accessed | tf_op | source)
XLA Modules:
  0.0 785.0 jit_solution(3189090102826812938)
XLA Ops:
  7.2 0.7 all-gather.12.cloned.1.call-update
  8.0 0.7 all-gather.14.cloned.1.call-update
  8.7 0.7 all-gather.22.cloned.1.call-update
  9.4 0.5 all-gather.16.cloned.1.call-update
  10.0 0.5 all-gather.18.cloned.1.call-update
  11.1 1.2 convert_reduce_fusion
  12.3 1.3 fusion.17
  13.7 1.3 iota_reduce_fusion
  15.0 0.8 convolution_reduce_fusion.2
  15.8 0.6 reduce_sum.248
  17.0 83.7 %all-gather.12.cloned.1.call-done = bf16[1024,1536]{1,0:T(8,128)(2,1)} async-done(((bf16[16,1536]{1,0:T(8,128)(2,1)}), bf16[1024,1536]{1,0:T(8,128)(2,1)}) %all-gather.12.cloned.1.call-update) | async-done | bytes 3145744 | tf_op jit(solution)/shard_map/all_gather | solution.py:59
  100.7 3.1 convolution_convert_fusion
  104.2 0.8 fusion.80
  105.0 1.1 convolution_convert_fusion.2
  106.1 77.5 %all-gather.14.cloned.1.call-done = bf16[512,1024]{1,0:T(8,128)(2,1)} async-done(((bf16[8,1024]{1,0:T(8,128)(2,1)}), bf16[512,1024]{1,0:T(8,128)(2,1)}) %all-gather.14.cloned.1.call-update) | async-done | bytes 1048592 | tf_op jit(solution)/shard_map/all_gather | solution.py:60
  183.5 1.7 fusion.11
  185.2 0.8 copy.90
  186.6 3.7 reduce.77
  190.3 1.2 reshape.505
  191.5 7.1 all-to-all-start
  198.6 0.6 multiply_reduce_fusion.5
  200.7 0.6 dynamic_slice.3
  201.3 1.3 dynamic-slice
  202.6 64.6 %all-gather.22.cloned.1.call-done = bf16[64,12,768]{2,1,0:T(8,128)(2,1)} async-done(((bf16[1,12,768]{2,1,0:T(8,128)(2,1)}), bf16[64,12,768]{2,1,0:T(8,128)(2,1)}) %all-gather.22.cloned.1.call-update) | async-done | bytes 1179664 | tf_op jit(solution)/shard_map/all_gather | solution.py:64
  267.2 2.2 reshape.466
  269.4 0.6 fusion.83
  270.0 0.6 multiply_reduce_fusion.4
  271.4 39.5 %all-gather.3 = f32[64,1,768]{2,1,0:T(1,128)} all-gather(f32[1,1,768]{2,1,0:T(1,128)S(1)} %reshape.467), channel_id=2, replica_groups=mesh['dp'=64,'frame'=8] {'dp'}, dimensions={0}, use_global_device_ids=true | all-gather | bytes 199680 | tf_op jit(solution)/shard_map/all_gather | solution.py:140
  310.9 0.5 reshape.506
  311.4 1.4 convert_reduce_fusion.2
  312.9 3.9 multiply_reduce_fusion.1
  317.2 34.7 %all-gather.16.cloned.1.call-done = bf16[1024,1536]{1,0:T(8,128)(2,1)} async-done(((bf16[16,1536]{1,0:T(8,128)(2,1)}), bf16[1024,1536]{1,0:T(8,128)(2,1)}) %all-gather.16.cloned.1.call-update) | async-done | bytes 3145744 | tf_op jit(solution)/shard_map/all_gather | solution.py:61
  351.8 3.8 fusion.4
  355.7 2.4 reshape.450
  358.0 1.5 fusion.79
  359.5 3.3 fusion.81
  362.8 1.9 fusion.14
  365.1 69.3 %all-gather.18.cloned.1.call-done = bf16[512,1024]{1,0:T(8,128)(2,1)} async-done(((bf16[8,1024]{1,0:T(8,128)(2,1)}), bf16[512,1024]{1,0:T(8,128)(2,1)}) %all-gather.18.cloned.1.call-update) | async-done | bytes 1048592 | tf_op jit(solution)/shard_map/all_gather | solution.py:62
  434.5 2.5 convert_reduce_fusion.1
  436.9 14.4 %psum.7 = f32[1,1024]{1,0:T(1,128)S(1)} all-reduce(f32[1,1024]{1,0:T(1,128)S(1)} %bitcast.201), channel_id=1, replica_groups=mesh['dp'=64,'frame'=8] {'frame'}, use_global_device_ids=true, to_apply=%region_9.0 | all-reduce | flops 1024 | bytes 8192 | tf_op jit(solution)/shard_map/psum | solution.py:135
  451.3 0.6 multiply_reduce_fusion.10
  452.6 0.6 multiply_reduce_fusion.7
  453.9 64.0 %all-gather.20.cloned.1.call-done = bf16[1024,768]{1,0:T(8,128)(2,1)} async-done(((bf16[16,768]{1,0:T(8,128)(2,1)}), bf16[1024,768]{1,0:T(8,128)(2,1)}) %all-gather.20.cloned.1.call-update) | async-done | bytes 1572880 | tf_op jit(solution)/shard_map/all_gather | solution.py:63
  517.9 2.3 fusion.82
  520.2 0.6 multiply_reduce_fusion.6
  521.6 0.9 fusion.84
  523.8 1.3 fusion.61
  525.7 0.6 fusion.63
  526.6 37.4 %all-gather.4 = f32[64,1,768]{2,1,0:T(1,128)S(1)} all-gather(f32[1,1,768]{2,1,0:T(1,128)S(1)} %reshape.469), channel_id=3, replica_groups=mesh['dp'=64,'frame'=8] {'dp'}, dimensions={0}, use_global_device_ids=true | all-gather | bytes 199680 | tf_op jit(solution)/shard_map/all_gather | solution.py:139
  564.0 1.0 fusion.85
  566.3 0.7 fusion.64
  567.9 0.8 multiply_multiply_fusion
  568.6 0.8 multiply_multiply_fusion.1
  570.8 188.4 %all-reduce.5.cloned.1.call-done = (f32[64,768]{1,0:T(8,128)}, f32[64,768]{1,0:T(8,128)}) async-done(((f32[64,768]{1,0:T(8,128)}, f32[64,768]{1,0:T(8,128)}), (f32[64,768]{1,0:T(8,128)}, f32[64,768]{1,0:T(8,128)})) %all-reduce.5.cloned.1.call-update) | async-done | bytes 393232
  759.2 2.0 multiply_reduce_fusion.8
  761.8 2.4 convolution_reduce_fusion.3
  764.2 0.6 multiply_reduce_fusion.2
  765.5 0.6 fusion.77
  766.7 0.6 add_any.45
  767.3 2.0 multiply_reduce_fusion.9
  770.0 2.7 fusion.50
  772.6 0.6 multiply_reduce_fusion.3
  773.9 0.7 fusion.78
  775.3 0.6 broadcast_add_fusion.1
  (59 shorter events, 3.0 us)
Async XLA Ops:
  7.2 7.8 copy-start
  7.2 93.6 %all-gather.12.cloned.1.call-start = ((), (), s32[]{:S(2)}) async-start(), calls=%async_computation.1 | async-start | bytes 3194880 | tf_op jit(solution)/shard_map/all_gather | solution.py:59
  7.9 175.6 %all-gather.14.cloned.1.call-start = ((), (), s32[]{:S(2)}) async-start(), calls=%async_computation.2 | async-start | bytes 1064960 | tf_op jit(solution)/shard_map/all_gather | solution.py:60
  8.7 258.5 %all-gather.22.cloned.1.call-start = ((), (), s32[]{:S(2)}) async-start(), calls=%async_computation.6 | async-start | bytes 1597440 | tf_op jit(solution)/shard_map/all_gather | solution.py:64
  9.4 342.4 %all-gather.16.cloned.1.call-start = ((), (), s32[]{:S(2)}) async-start(), calls=%async_computation.3 | async-start | bytes 3194880 | tf_op jit(solution)/shard_map/all_gather | solution.py:61
  10.0 424.5 %all-gather.18.cloned.1.call-start = ((), (), s32[]{:S(2)}) async-start(), calls=%async_computation.4 | async-start | bytes 1064960 | tf_op jit(solution)/shard_map/all_gather | solution.py:62
  10.6 507.4 %all-gather.20.cloned.1.call-start = ((), (), s32[]{:S(2)}) async-start(), calls=%async_computation.5 | async-start | bytes 1597440 | tf_op jit(solution)/shard_map/all_gather | solution.py:63
  105.0 78.6 %copy-start.2 = (bf16[1,1,256,1024]{3,2,1,0:T(8,128)(2,1)S(1)}, bf16[1,1,256,1024]{3,2,1,0:T(8,128)(2,1)}, u32[]{:S(2)}) copy-start(bf16[1,1,256,1024]{3,2,1,0:T(8,128)(2,1)} %param.15) | copy-start | bytes 1572868
  186.1 13.9 %copy-start.6 = (f32[768]{0:T(1024)S(1)}, f32[768]{0:T(1024)}, u32[]{:S(2)}) copy-start(f32[768]{0:T(1024)} %param.23) | copy-start | bytes 9220
  186.1 14.6 %copy-start.8 = (s32[64]{0:T(128)S(1)}, s32[64]{0:T(128)}, u32[]{:S(2)}) copy-start(s32[64]{0:T(128)} %param.18) | copy-start | bytes 772
  191.5 119.4 %all-to-all-start = ((bf16[8,2,16384]{2,1,0:T(2,128)(2,1)}), bf16[8,2,16384]{2,1,0:T(2,128)(2,1)S(1)}, u32[]{:S(2)}, u32[]{:S(2)}) async-start(bf16[8,2,16384]{2,1,0:T(2,128)(2,1)} %reshape.505), calls=%async_computation | async-start | bytes 1048576 | tf_op jit(solution)/shard_map/all_to_all | solution.py:91
  198.6 560.6 %all-reduce.5.cloned.1.call-start = ((), (), s32[]{:S(2)}) async-start(), calls=%async_computation.7 | async-start | bytes 786432
  311.4 40.4 %copy-start.9 = (f32[1024]{0:T(1024)S(1)}, f32[1024]{0:T(1024)}, u32[]{:S(2)}) copy-start(f32[1024]{0:T(1024)} %param.21) | copy-start | bytes 12292
  317.1 34.7 %copy-start.3 = (f32[1,1,256,1024]{3,2,0,1:T(8,128)}, f32[1,1,256,1024]{3,2,0,1:T(8,128)S(1)}, u32[]{:S(2)}) copy-start(f32[1,1,256,1024]{3,2,0,1:T(8,128)S(1)} %copy.45) | copy-start | bytes 3145732
  362.8 71.7 %copy-start.4 = (f32[1,1,256,1024]{3,2,0,1:T(8,128)S(1)}, f32[1,1,256,1024]{3,2,0,1:T(8,128)}, u32[]{:S(2)}) copy-start(f32[1,1,256,1024]{3,2,0,1:T(8,128)} %copy-done.3) | copy-start | bytes 3145732
  364.8 153.1 %copy-start.7 = (f32[1024]{0:T(1024)S(1)}, f32[1024]{0:T(1024)}, u32[]{:S(2)}) copy-start(f32[1024]{0:T(1024)} %param.22) | copy-start | bytes 12292
  365.1 156.5 %copy-start.5 = (f32[64,1,768]{2,1,0:T(1,128)S(1)}, f32[64,1,768]{2,1,0:T(1,128)}, u32[]{:S(2)}) copy-start(f32[64,1,768]{2,1,0:T(1,128)} %all-gather.3) | copy-start | bytes 589828
  517.9 252.0 %copy-start.1 = (bf16[1024,768]{1,0:T(8,128)(2,1)S(1)}, bf16[1024,768]{1,0:T(8,128)(2,1)}, u32[]{:S(2)}) copy-start(bf16[1024,768]{1,0:T(8,128)(2,1)} %all-gather.20.cloned.1.call-done) | copy-start | bytes 4718596
Sparse Core Ops, SparseCore 0:
  11.3 89.3 all-gather.11
  104.1 79.4 all-gather.13
  186.9 80.2 all-gather.21
  270.3 81.4 all-gather.15
  355.0 79.4 all-gather.17
  437.7 80.2 all-gather.19
  570.9 188.2 all-reduce.4
where the time goes:
time: 788 us; the launch traced here: 785 us
  waiting for transfers between devices  586 us (74%)
  blocking collectives  91.2 us (12%)
  between operations  30.8 us (4%)
  matrix products  29.2 us (4%)
  other arithmetic  27.8 us (4%)
  local copies, waits for them, and re-layouts  12.8 us (2%)
    unnamed x8, waiting for transfers between devices  192 us
    all_gather x1, waiting for transfers between devices, on_device(): lax.all_gather(w_qkv_spatial, 'dp', axis=0, tiled=True)  83.7 us
    all_gather x1, waiting for transfers between devices, on_device(): lax.all_gather(w_out_spatial, 'dp', axis=0, tiled=True)  77.5 us
    all_gather x1, waiting for transfers between devices, on_device(): lax.all_gather(w_out_temporal, 'dp', axis=0, tiled=True)  69.3 us
    all_gather x1, waiting for transfers between devices, on_device(): lax.all_gather(w_text, 'dp', axis=0, tiled=True)  64.6 us
    all_gather x1, waiting for transfers between devices, on_device(): lax.all_gather(w_video, 'dp', axis=0, tiled=True)  64 us
    all_gather x1, blocking collectives, on_device(): lax.all_gather(text_mine, 'dp', axis=0, tiled=True)  39.5 us
    all_gather x1, blocking collectives, on_device(): lax.all_gather(video_mine, 'dp', axis=0, tiled=True)  37.4 us
  transfers between devices with their start and end apart: 8, of which 7 were waited for; matrix products, arithmetic and copies ran while one was open for 6% of the time, Pallas kernels for 0%

commit v1 on v0

v1 whole, which is shorter than its diff:
```python
import functools

import jax
import jax.numpy as jnp
from jax import lax
from jax.experimental import pallas as pl
from jax.experimental.pallas import tpu as pltpu
from jax.sharding import PartitionSpec as P

HEADS = 8
HD = 64
WIDTH = HEADS * HD
D = 1024
DT = 768
E = 768
NORM_EPS = 1e-05
UNIT_EPS = 1e-06
F32 = jnp.float32
BF16 = jnp.bfloat16
VMEM_LIMIT = 48 * 1024 * 1024

QKV_S = 0
QKV_T = 1536
W_VIDEO = 3072
W_TEXT = 3840
W_OUT = 4608
PACKED = 5632


def dot(a, b):
    return lax.dot_general(a, b, (((1,), (0,)), ((), ())), preferred_element_type=F32)


def dot_t(a, b):
    return lax.dot_general(a, b, (((1,), (1,)), ((), ())), preferred_element_type=F32)


def pieces(a):
    first = a.astype(BF16)
    rest = a - first.astype(F32)
    second = rest.astype(BF16)
    third = (rest - second.astype(F32)).astype(BF16)
    return first, second, third


def exact(dot_fn, a, weight):
    first, second, third = pieces(a)
    return dot_fn(third, weight) + dot_fn(second, weight) + dot_fn(first, weight)


def layer_norm(values, gain):
    center = values - jnp.mean(values, axis=-1, keepdims=True)
    spread = jnp.mean(center * center, axis=-1, keepdims=True)
    return center * lax.rsqrt(spread + NORM_EPS) * gain


def attend(packed_ref, mixed_ref, mask):
    rows = packed_ref.shape[0]
    low = lax.broadcasted_iota(jnp.int32, (rows, 2 * HD), 1) < HD
    for pair in range(HEADS // 2):
        at = pair * 2 * HD
        query = packed_ref[:, at : at + 2 * HD]
        key = packed_ref[:, WIDTH + at : WIDTH + at + 2 * HD]
        value = packed_ref[:, 2 * WIDTH + at : 2 * WIDTH + at + 2 * HD]
        mixed = []
        for lanes in (low, ~low):
            scores = dot_t(jnp.where(lanes, query, jnp.zeros_like(query)), key) * (HD**-0.5)
            if mask is not None:
                scores = jnp.where(mask, scores, -1e30)
            weight = jnp.exp(scores - jnp.max(scores, axis=-1, keepdims=True))
            probs = weight * (1.0 / jnp.sum(weight, axis=-1, keepdims=True))
            mixed.append(dot(probs.astype(BF16), value))
        mixed_ref[:, at : at + 2 * HD] = jnp.where(low, mixed[0], mixed[1]).astype(BF16)


def spatial_kernel(tokens_ref, gain_ref, weights_ref, mixed_ref, qkv, packed, sem):
    copy = pltpu.make_async_copy(weights_ref.at[:, QKV_S : QKV_S + 3 * WIDTH], qkv, sem)
    copy.start()
    normed = layer_norm(tokens_ref[...].astype(F32), gain_ref[...]).astype(BF16)
    copy.wait()
    packed[...] = dot(normed, qkv[...]).astype(BF16)
    attend(packed, mixed_ref, None)


def temporal_kernel(
    mixed_ref, tokens_ref, gain_ref, weights_ref, out_ref, pool_ref, qkv, outs, packed, mixed, sems
):
    copy_out = pltpu.make_async_copy(weights_ref.at[:, W_OUT : W_OUT + D], outs, sems.at[0])
    copy_qkv = pltpu.make_async_copy(
        weights_ref.at[:, QKV_T : QKV_T + 3 * WIDTH], qkv, sems.at[1]
    )
    copy_out.start()
    copy_qkv.start()
    copy_out.wait()
    both = outs[...].astype(F32).reshape(64, 2, 8, D)
    out_spatial = both[:, 0].reshape(WIDTH, D).astype(BF16)
    out_temporal = both[:, 1].reshape(WIDTH, D).astype(BF16)
    spatial = (tokens_ref[...].astype(F32) + dot(mixed_ref[...], out_spatial)).astype(BF16)
    normed = layer_norm(spatial.astype(F32), gain_ref[...]).astype(BF16)
    copy_qkv.wait()
    packed[...] = dot(normed, qkv[...]).astype(BF16)
    rows = packed.shape[0]
    patches = 32
    place = lax.broadcasted_iota(jnp.int32, (rows, rows), 0) % patches
    other = lax.broadcasted_iota(jnp.int32, (rows, rows), 1) % patches
    attend(packed, mixed, place == other)
    output = (spatial.astype(F32) + dot(mixed[...], out_temporal)).astype(BF16)
    out_ref[...] = output
    total = jnp.sum(output.astype(F32), axis=0, keepdims=True)
    for chunk in range(D // 128):
        pool_ref[:, chunk, :] = jnp.broadcast_to(total[:, chunk * 128 : (chunk + 1) * 128], (8, 128))


def spread_kernel(parts_ref, every_ref):
    mine = jnp.sum(parts_ref[...], axis=0) * (1.0 / (8 * 256))
    every_ref[...] = jnp.broadcast_to(mine[None], every_ref.shape)


def text_kernel(gain_ref, weights_ref, pool_ref, mapped_ref, weight_ref, packed, sem):
    copy = pltpu.make_async_copy(weights_ref.at[:, W_TEXT : W_TEXT + E], packed, sem)
    copy.start()
    copy.wait()
    column = lax.broadcasted_iota(jnp.int32, (DT, D), 1)
    place = column % 16
    row = jnp.where(place < 12, (column // 16) * 12 + place, -1)
    pick = (row == lax.broadcasted_iota(jnp.int32, (DT, D), 0)).astype(BF16)
    weight = dot(pick, packed[...]).astype(BF16)
    weight_ref[...] = weight
    column = lax.broadcasted_iota(jnp.int32, (64, D), 1)
    pick = (column == 16 * lax.broadcasted_iota(jnp.int32, (64, D), 0) + 12).astype(BF16)
    pool = dot(pick, packed[...])
    pool_ref[...] = pool
    mapped_ref[...] = exact(dot, layer_norm(pool, gain_ref[...]), weight)


def unit_rows(values):
    return values * lax.rsqrt(jnp.sum(values * values, axis=-1, keepdims=True) + UNIT_EPS)


def unit_back(mapped, grad):
    scale = lax.rsqrt(jnp.sum(mapped * mapped, axis=-1, keepdims=True) + UNIT_EPS)
    along = jnp.sum(mapped * grad, axis=-1, keepdims=True)
    return scale * grad - mapped * (scale * scale * scale * along)


def norm_back(values, gain, grad):
    center = values - jnp.mean(values, axis=-1, keepdims=True)
    scale = lax.rsqrt(jnp.mean(center * center, axis=-1, keepdims=True) + NORM_EPS)
    grad = grad * gain
    unit = center * scale
    along = jnp.mean(grad * unit, axis=-1, keepdims=True)
    return scale * (grad - jnp.mean(grad, axis=-1, keepdims=True) - unit * along)


def loss_kernel(
    place_ref,
    scale_ref,
    pairs_ref,
    pooled_ref,
    text_pool_ref,
    text_mapped_ref,
    text_weight_ref,
    gain_video_ref,
    gain_text_ref,
    weights_ref,
    video_loss_ref,
    text_loss_ref,
    grad_pooled_ref,
    grad_text_ref,
    weight,
    pooled_all,
    sem,
):
    copy = pltpu.make_async_copy(weights_ref.at[:, W_VIDEO : W_VIDEO + E], weight, sem)
    copy.start()
    me = place_ref[0]
    scale = scale_ref[0]
    for chunk in range(D // 128):
        pooled_all[:, chunk * 128 : (chunk + 1) * 128] = pooled_ref[:, chunk, :]
    gain = gain_video_ref[...]
    normed = layer_norm(pooled_all[...], gain)
    copy.wait()
    mapped = exact(dot, normed, weight[...])
    video = unit_rows(mapped)
    text_mapped = text_mapped_ref[...]
    text = unit_rows(text_mapped)
    logits = scale * lax.dot_general(
        video, text, (((1,), (1,)), ((), ())), precision=lax.Precision.HIGHEST,
        preferred_element_type=F32,
    )
    count = logits.shape[0]
    rows = lax.broadcasted_iota(jnp.int32, (count, count), 0)
    columns = lax.broadcasted_iota(jnp.int32, (count, count), 1)
    match = pairs_ref[...] == columns
    row_top = jnp.max(logits, axis=1, keepdims=True)
    row_exp = jnp.exp(logits - row_top)
    row_sum = jnp.sum(row_exp, axis=1, keepdims=True)
    col_top = jnp.max(logits, axis=0, keepdims=True)
    col_exp = jnp.exp(logits - col_top)
    col_sum = jnp.sum(col_exp, axis=0, keepdims=True)
    positive = jnp.where(match, logits, 0.0)
    video_loss = 0.5 * (row_top + jnp.log(row_sum) - jnp.sum(positive, axis=1, keepdims=True))
    text_loss = 0.5 * (col_top + jnp.log(col_sum) - jnp.sum(positive, axis=0, keepdims=True))
    mine_row = lax.broadcasted_iota(jnp.int32, (count, 1), 0) == me
    mine_col = lax.broadcasted_iota(jnp.int32, (1, count), 1) == me
    video_loss_ref[0] = jnp.sum(jnp.where(mine_row, video_loss, 0.0))
    text_loss_ref[0] = jnp.sum(jnp.where(mine_col, text_loss, 0.0))
    slope = (0.5 * scale) * (row_exp / row_sum + col_exp / col_sum - 2.0 * match.astype(F32))
    row_slope = jnp.sum(jnp.where(rows == me, slope, 0.0), axis=0, keepdims=True)
    row_slope = jnp.sum(jnp.where(rows == columns, row_slope, 0.0), axis=1, keepdims=True)
    col_slope = jnp.sum(jnp.where(columns == me, slope, 0.0), axis=1, keepdims=True)
    grad_video = jnp.sum(row_slope * text, axis=0, keepdims=True)
    grad_caption = jnp.sum(col_slope * video, axis=0, keepdims=True)
    mine_mapped = jnp.sum(jnp.where(mine_row, mapped, 0.0), axis=0, keepdims=True)
    mine_text_mapped = jnp.sum(jnp.where(mine_row, text_mapped, 0.0), axis=0, keepdims=True)
    mine_pooled = jnp.sum(jnp.where(mine_row, pooled_all[...], 0.0), axis=0, keepdims=True)
    mine_text_pool = jnp.sum(jnp.where(mine_row, text_pool_ref[...], 0.0), axis=0, keepdims=True)
    back = exact(dot_t, unit_back(mine_mapped, grad_video), weight[...])
    grad_pooled_ref[...] = norm_back(mine_pooled, gain, back)
    back = exact(dot_t, unit_back(mine_text_mapped, grad_caption), text_weight_ref[...])
    grad_text_ref[...] = norm_back(mine_text_pool, gain_text_ref[...], back)


def call(kernel, out_shape, in_spaces, scratch, out_spaces=None, cost=(0, 0)):
    many = isinstance(out_shape, (tuple, list))
    out_spaces = out_spaces or ([pltpu.VMEM] * (len(out_shape) if many else 1))
    out_specs = [pl.BlockSpec(memory_space=space) for space in out_spaces]
    return pl.pallas_call(
        kernel,
        out_shape=out_shape,
        in_specs=[pl.BlockSpec(memory_space=space) for space in in_spaces],
        out_specs=out_specs if many else out_specs[0],
        scratch_shapes=scratch,
        compiler_params=pltpu.CompilerParams(vmem_limit_bytes=VMEM_LIMIT),
        cost_estimate=pl.CostEstimate(flops=cost[0], bytes_accessed=cost[1], transcendentals=0),
    )


def shape(dims, dtype):
    return jax.ShapeDtypeStruct(dims, dtype)


def on_device(
    video_tokens,
    text_states,
    caption_ids,
    pair_index,
    logit_scale,
    gain_spatial,
    gain_temporal,
    gain_video,
    gain_text,
    w_qkv_spatial,
    w_out_spatial,
    w_qkv_temporal,
    w_out_temporal,
    w_video,
    w_text,
):
    V, S, A = pltpu.VMEM, pltpu.SMEM, pl.ANY
    DMA = pltpu.SemaphoreType.DMA
    tokens = video_tokens.reshape(256, D)
    end_place = jnp.argmax(caption_ids[0])
    text_row = lax.dynamic_slice_in_dim(text_states[0], end_place, 1, 0)
    text_part = jnp.concatenate([w_text, text_row, jnp.zeros((3, E), BF16)], axis=0)
    outs = jnp.concatenate([w_out_spatial, w_out_temporal], axis=0)
    mine = jnp.concatenate([w_qkv_spatial, w_qkv_temporal, w_video, text_part, outs], axis=1)
    weights = lax.all_gather(mine, "dp", axis=0, tiled=True)
    by_patch = lax.all_to_all(tokens.reshape(8, 32, D), "frame", 0, 0, tiled=True)

    mixed = call(
        spatial_kernel,
        shape((256, WIDTH), BF16),
        (V, V, A),
        [pltpu.VMEM((D, 3 * WIDTH), BF16), pltpu.VMEM((256, 3 * WIDTH), BF16), DMA],
    )(tokens, gain_spatial.reshape(1, D), weights)
    mixed = lax.all_to_all(mixed.reshape(8, 32, WIDTH), "frame", 0, 0, tiled=True)
    layer_out, pool = call(
        temporal_kernel,
        (shape((256, D), BF16), shape((8, 8, 128), F32)),
        (V, V, V, A),
        [
            pltpu.VMEM((D, 3 * WIDTH), BF16),
            pltpu.VMEM((D, D), BF16),
            pltpu.VMEM((256, 3 * WIDTH), BF16),
            pltpu.VMEM((256, WIDTH), BF16),
            DMA((2,)),
        ],
    )(mixed.reshape(256, WIDTH), by_patch.reshape(256, D), gain_temporal.reshape(1, D), weights)
    text_pool, text_mapped, text_weight = call(
        text_kernel,
        (shape((64, DT), F32), shape((64, E), F32), shape((DT, E), BF16)),
        (V, A),
        [pltpu.VMEM((D, E), BF16), DMA],
    )(gain_text.reshape(1, DT), weights)
    pool = lax.all_to_all(pool, "frame", 0, 0, tiled=True)
    pool = call(spread_kernel, shape((64, 8, 128), F32), (V,), [])(pool)
    pooled = lax.all_to_all(pool, "dp", 0, 0, tiled=True)
    place = lax.axis_index("dp").astype(jnp.int32).reshape(1)
    video_loss, text_loss, grad_pooled, grad_text = call(
        loss_kernel,
        (shape((1,), F32), shape((1,), F32), shape((1, D), F32), shape((1, DT), F32)),
        (S, S, V, V, V, V, V, V, V, A),
        [pltpu.VMEM((D, E), BF16), pltpu.VMEM((64, D), F32), DMA],
        (S, S, V, V),
    )(
        place,
        logit_scale,
        pair_index.reshape(64, 1),
        pooled,
        text_pool,
        text_mapped,
        text_weight,
        gain_video.reshape(1, D),
        gain_text.reshape(1, DT),
        weights,
    )
    return (layer_out.reshape(1, 8, 32, D), video_loss, text_loss, grad_pooled, grad_text)


def solution(mesh):
    placed = (
        P("dp", "frame", None, None),
        P("dp", None, None),
        P("dp", None),
        P(),
        P(),
        P(),
        P(),
        P(),
        P(),
        P("dp", None),
        P("dp", None),
        P("dp", None),
        P("dp", None),
        P("dp", None),
        P("dp", None),
    )
    return jax.shard_map(
        on_device,
        mesh=mesh,
        in_specs=placed,
        out_specs=(P("dp", None, "frame", None), P("dp"), P("dp"), P("dp", None), P("dp", None)),
        check_vma=False,
    )
```

time: 788 us -> 189 us (0.24)
  waiting for transfers between devices: 586 us -> 95.3 us
  blocking collectives: 91.2 us -> 28.1 us
  matrix products: 29.2 us -> 0 us
  other arithmetic: 27.8 us -> 2.86 us
  Pallas kernels: 0 us -> 21.7 us
  between operations: 30.8 us -> 16.8 us
  starting transfers between devices: 7.36 us -> 18.4 us
    all_gather x6 -> x1, waiting for transfers between devices: 394 us -> 88.5 us  [on_device(): weights = lax.all_gather(mine, 'dp', axis=0, tiled=True)]
    unnamed x8 -> x1, waiting for transfers between devices: 192 us -> 0.02 us
    all_gather x2 -> x0, blocking collectives: 76.9 us -> none  [the longest x1 39.5 us: on_device(): lax.all_gather(text_mine, 'dp', axis=0, tiled=True)]
    all_to_all x0 -> x2, blocking collectives: none -> 28.1 us  [the longest x1 18.8 us: on_device(): lax.all_to_all(mixed.reshape(8, 32, WIDTH), 'frame', 0, 0, tiled=True)]
    dot_general x15 -> x0, matrix products: 25.1 us -> none  [the longest x4 11.1 us: project(): result = jnp.dot(flat, weight, preferred_element_type=jnp.float32)]
    pallas_call x0 -> x5, Pallas kernels: none -> 21.7 us  [the longest x1 6.58 us: on_device(): call(loss_kernel, (shape((1,), F32), shape((1,), F32), shape((1, D), F32)...]
    reduce_sum x18 -> x0, other arithmetic: 19.9 us -> none  [the longest x4 6.41 us: layer_norm(): spread = jnp.mean(center * center, axis=-1, keepdims=True)]
    psum x1 -> x0, blocking collectives: 14.4 us -> none  [on_device(): pooled = lax.psum(partial_pool, 'frame') / divisor]
  transfers between devices with their start and end apart: 8 -> 3, of which waited for: 7 -> 2; matrix products, arithmetic and copies ran while one was open for 6% -> 0% of each run, Pallas kernels for 0% -> 5%
where the time goes in v1:
time: 189 us; the launch traced here: 188 us
  waiting for transfers between devices  95.3 us (50%)
  blocking collectives  28.1 us (15%)
  Pallas kernels  21.7 us (11%)
  starting transfers between devices  18.4 us (10%)
  between operations  16.8 us (9%)
  local copies, waits for them, and re-layouts  4.97 us (3%)
  other arithmetic  2.86 us (2%)
    all_gather x1, waiting for transfers between devices, on_device(): weights = lax.all_gather(mine, 'dp', axis=0, tiled=True)  88.5 us
    all_to_all x1, blocking collectives, on_device(): lax.all_to_all(mixed.reshape(8, 32, WIDTH), 'frame', 0, 0, tiled=True)  18.8 us
    all_to_all x1, starting transfers between devices, on_device(): lax.all_to_all(tokens.reshape(8, 32, D), 'frame', 0, 0, tiled=True)  10.9 us
    all_to_all x1, blocking collectives, on_device(): pool = lax.all_to_all(pool, 'frame', 0, 0, tiled=True)  9.25 us
    all_to_all x1, starting transfers between devices, on_device(): pooled = lax.all_to_all(pool, 'dp', 0, 0, tiled=True)  7.51 us
    all_to_all x1, waiting for transfers between devices, on_device(): pooled = lax.all_to_all(pool, 'dp', 0, 0, tiled=True)  6.84 us
    pallas_call x1, Pallas kernels, on_device(): call(loss_kernel, (shape((1,), F32), shape((1,), F32), shape((1, D), F32)...  6.58 us
    pallas_call x1, Pallas kernels, on_device(): call(temporal_kernel, (shape((256, D), BF16), shape((8, 8, 128), F32)), (...  5.9 us
  transfers between devices with their start and end apart: 3, of which 2 were waited for; matrix products, arithmetic and copies ran while one was open for 0% of the time, Pallas kernels for 5%

profile of v1, /device:TPU:1, one launch (start us, length us, event | category | flops | bytes accessed | tf_op | source)
XLA Modules:
  0.0 188.1 jit_solution(9116148389838390149)
XLA Ops:
  7.2 0.0 copy-start
  7.2 0.0 copy-start.3
  7.2 0.0 all-gather.2.cloned.1.call-start
  7.2 1.3 bitcast_reduce_fusion
  9.8 0.8 constant_dynamic-update-slice_fusion.2
  10.7 0.1 pad.2.clone
  11.4 0.0 copy-done
  11.4 0.8 constant_dynamic-update-slice_fusion.1
  12.2 0.7 constant_dynamic-update-slice_fusion
  13.0 0.8 maximum_dynamic-update-slice_fusion.1
  13.8 0.7 maximum_dynamic-update-slice_fusion
  14.5 0.0 copy-start.5
  14.5 0.7 copy-done.5
  15.2 0.0 all-gather.2.cloned.1.call-update
  15.2 10.9 %all-to-all-start.1 = ((bf16[8,32,1024]{2,1,0:T(8,128)(2,1)}), bf16[8,32,1024]{2,1,0:T(8,128)(2,1)S(1)}, u32[]{:S(2)}, u32[]{:S(2)}) async-start(bf16[8,32,1024]{2,1,0:T(8,128)(2,1)} %bitcast.15), calls=%async_computation.1 | async-start | bytes 1048576 | tf_op jit(solution)/shard_map/all_to_all | solution.py:269
  26.1 88.5 %all-gather.2.cloned.1.call-done.weights_ref = bf16[1024,5632]{1,0:T(8,128)(2,1)} async-done(((bf16[16,5632]{1,0:T(8,128)(2,1)}), bf16[1024,5632]{1,0:T(8,128)(2,1)}) %all-gather.2.cloned.1.call-update) | async-done | bytes 11534352 | tf_op jit(solution)/shard_map/all_gather | solution.py:268
  114.5 0.0 copy-start.1
  114.5 1.0 copy-done.1
  115.6 0.0 copy-start.2
  115.6 0.7 copy-done.2
  116.3 0.0 copy-start.6
  116.3 0.0 copy-start.7
  116.3 4.2 %shard_map.182 = bf16[256,512]{1,0:T(8,128)(2,1)S(1)} custom-call(bf16[256,1024]{1,0:T(8,128)(2,1)S(1)} %bitcast.16, f32[1,1024]{1,0:T(1,128)S(1)} %bitcast.20, bf16[1024,5632]{1,0:T(8,128)(2,1)} %all-gather.2.cloned.1.call-done.weights_ref), custom_call_target="tpu_custom_call" | custom-call | tf_op jit(solution)/shard_map/pallas_call | solution.py:271
  120.4 0.0 all-to-all-done.1
  120.5 18.8 %all_to_all.20 = bf16[8,32,512]{2,1,0:T(8,128)(2,1)S(1)} all-to-all(bf16[8,32,512]{2,1,0:T(8,128)(2,1)S(1)} %bitcast.18), channel_id=1, replica_groups=mesh['dp'=64,'frame'=8] {'frame'}, dimensions={0} | all-to-all | bytes 524288 | tf_op jit(solution)/shard_map/all_to_all | solution.py:277
  139.3 0.0 copy-done.3
  139.3 0.0 copy-start.4
  139.3 5.9 %shard_map.183 = (bf16[256,1024]{1,0:T(8,128)(2,1)}, f32[8,8,128]{2,1,0:T(8,128)S(1)}) custom-call(bf16[256,512]{1,0:T(8,128)(2,1)S(1)} %bitcast.19, bf16[256,1024]{1,0:T(8,128)(2,1)S(1)} %bitcast.17, f32[1,1024]{1,0:T(1,128)S(1)} %bitcast.21, bf16[1024,5632]{1,0:T(8,128)(2,1)} %all-gather.2.cloned.1.call-done.weights_ref), custom_call_target="tpu_custom_call" | custom-call | tf_op jit(solution)/shard_map/pallas_call | solution.py:278
  145.2 9.2 %all_to_all.21.parts_ref = f32[8,8,128]{2,1,0:T(8,128)S(1)} all-to-all(f32[8,8,128]{2,1,0:T(8,128)S(1)} %get-tuple-element.17), channel_id=1, replica_groups=mesh['dp'=64,'frame'=8] {'frame'}, dimensions={0} | all-to-all | bytes 65536 | tf_op jit(solution)/shard_map/all_to_all | solution.py:296
  154.4 0.7 shard_map.184
  155.1 7.5 %all-to-all-start.3 = ((f32[64,8,128]{2,1,0:T(8,128)}), f32[64,8,128]{2,1,0:T(8,128)S(1)}, u32[]{:S(2)}, u32[]{:S(2)}) async-start(f32[64,8,128]{2,1,0:T(8,128)} %shard_map.184), calls=%async_computation.3 | async-start | bytes 524288 | tf_op jit(solution)/shard_map/all_to_all | solution.py:298
  163.3 0.0 copy-done.6
  163.3 0.0 copy-done.7
  163.3 0.1 copy.20.pairs_ref
  163.4 4.4 %shard_map.185 = (f32[64,768]{1,0:T(8,128)S(1)}, f32[64,768]{1,0:T(8,128)S(1)}, bf16[768,768]{1,0:T(8,128)(2,1)S(1)}) custom-call(f32[1,768]{1,0:T(1,128)S(1)} %reshape.54.gain_ref.gain_text_ref, bf16[1024,5632]{1,0:T(8,128)(2,1)} %all-gather.2.cloned.1.call-done.weights_ref), custom_call_target="tpu_custom_call" | custom-call | tf_op jit(solution)/shard_map/pallas_call | solution.py:290
  167.8 6.8 %all-to-all-done.3.pooled_ref = f32[64,8,128]{2,1,0:T(8,128)S(1)} async-done(((f32[64,8,128]{2,1,0:T(8,128)}), f32[64,8,128]{2,1,0:T(8,128)S(1)}, u32[]{:S(2)}, u32[]{:S(2)}) %all-to-all-start.3) | async-done | bytes 262176 | tf_op jit(solution)/shard_map/all_to_all | solution.py:298
  174.7 0.0 copy-done.4
  174.7 6.6 %shard_map.186 = (f32[1]{0:T(128)}, f32[1]{0:T(128)}, f32[1,1024]{1,0:T(1,128)}, f32[1,768]{1,0:T(1,128)}) custom-call(s32[1]{0:T(128)} %bitcast.10.place_ref, f32[1]{0:T(128)S(6)} %copy.25.scale_ref, s32[64,1]{1,0:T(8,128)S(1)} %copy.20.pairs_ref, f32[64,8,128]{2,1,0:T(8,128)S(1)} %all-to-all-done.3.pooled_ref, ...), custom_call_target="tpu_custom_call" | custom-call | tf_op jit(solution)/shard_map/pallas_call | solution.py:300
  (3 shorter events, 0.0 us)
Async XLA Ops:
  7.2 4.2 %copy-start = (bf16[1,77,768]{2,1,0:T(8,128)(2,1)S(1)}, bf16[1,77,768]{2,1,0:T(8,128)(2,1)}, u32[]{:S(2)}) copy-start(bf16[1,77,768]{2,1,0:T(8,128)(2,1)} %param.16) | copy-start | bytes 354820
  7.2 132.1 %copy-start.3 = (f32[1024]{0:T(1024)S(1)}, f32[1024]{0:T(1024)}, u32[]{:S(2)}) copy-start(f32[1024]{0:T(1024)} %param.21) | copy-start | bytes 12292
  7.2 107.3 %all-gather.2.cloned.1.call-start = ((), (), s32[]{:S(2)}) async-start(), calls=%async_computation.4 | async-start | bytes 11714560 | tf_op jit(solution)/shard_map/all_gather | solution.py:268
  14.5 0.7 copy-start.5
  15.2 105.2 %all-to-all-start.1 = ((bf16[8,32,1024]{2,1,0:T(8,128)(2,1)}), bf16[8,32,1024]{2,1,0:T(8,128)(2,1)S(1)}, u32[]{:S(2)}, u32[]{:S(2)}) async-start(bf16[8,32,1024]{2,1,0:T(8,128)(2,1)} %bitcast.15), calls=%async_computation.1 | async-start | bytes 1048576 | tf_op jit(solution)/shard_map/all_to_all | solution.py:269
  114.5 1.0 copy-start.1
  115.6 0.7 copy-start.2
  116.3 47.0 %copy-start.6 = (f32[768]{0:T(1024)S(1)}, f32[768]{0:T(1024)}, u32[]{:S(2)}) copy-start(f32[768]{0:T(1024)} %param.23) | copy-start | bytes 9220
  116.3 47.1 %copy-start.7 = (s32[64]{0:T(128)S(1)}, s32[64]{0:T(128)}, u32[]{:S(2)}) copy-start(s32[64]{0:T(128)} %param.18) | copy-start | bytes 772
  139.3 35.4 %copy-start.4 = (f32[1024]{0:T(1024)S(1)}, f32[1024]{0:T(1024)}, u32[]{:S(2)}) copy-start(f32[1024]{0:T(1024)} %param.22) | copy-start | bytes 12292
  155.1 19.5 %all-to-all-start.3 = ((f32[64,8,128]{2,1,0:T(8,128)}), f32[64,8,128]{2,1,0:T(8,128)S(1)}, u32[]{:S(2)}, u32[]{:S(2)}) async-start(f32[64,8,128]{2,1,0:T(8,128)} %shard_map.184), calls=%async_computation.3 | async-start | bytes 524288 | tf_op jit(solution)/shard_map/all_to_all | solution.py:298
Sparse Core Ops, SparseCore 0:
  15.3 99.1 all-gather.1

commit v2 on v1

--- a/solution.py
+++ b/solution.py
@@ -19,12 +19,22 @@
 BF16 = jnp.bfloat16
 VMEM_LIMIT = 48 * 1024 * 1024
 
-QKV_S = 0
-QKV_T = 1536
-W_VIDEO = 3072
-W_TEXT = 3840
-W_OUT = 4608
-PACKED = 5632
+QKV_T = 0
+W_TEXT = 1536
+W_OUT = 2304
+W_VIDEO = 3328
+PACKED = 4096
+
+X, Y = 4, 8
+ROWS_OF_X = [[(x * Y + y) * 2 + c for x in range(X)] for y in range(Y) for c in range(2)]
+ROWS_OF_Y = [[(x * Y + y) * 2 + c for y in range(Y)] for x in range(X) for c in range(2)]
+ROWS_OF_YC = [[(x * Y + y) * 2 + c for y in range(Y) for c in range(2)] for x in range(X)]
+CHIPS_OF_CORE = [[i * 2 + c for i in range(X * Y)] for c in range(2)]
+OTHER_CORE = [(i, i ^ 1) for i in range(2 * X * Y)]
+FRAMES = 8
+CORES_AND_FRAMES = [
+    [(2 * i + c) * FRAMES + f for c in range(2) for f in range(FRAMES)] for i in range(X * Y)
+]
 
 
 def dot(a, b):
@@ -73,32 +83,66 @@
         mixed_ref[:, at : at + 2 * HD] = jnp.where(low, mixed[0], mixed[1]).astype(BF16)
 
 
-def spatial_kernel(tokens_ref, gain_ref, weights_ref, mixed_ref, qkv, packed, sem):
-    copy = pltpu.make_async_copy(weights_ref.at[:, QKV_S : QKV_S + 3 * WIDTH], qkv, sem)
-    copy.start()
+def spatial_kernel(core_ref, tokens_ref, gain_ref, own_ref, other_ref, mixed_ref, qkv, packed, sems):
+    core = core_ref[0]
+    copy_own = pltpu.make_async_copy(own_ref, qkv.at[:, core], sems.at[0])
+    copy_other = pltpu.make_async_copy(other_ref, qkv.at[:, 1 - core], sems.at[1])
+    copy_own.start()
+    copy_other.start()
     normed = layer_norm(tokens_ref[...].astype(F32), gain_ref[...]).astype(BF16)
-    copy.wait()
-    packed[...] = dot(normed, qkv[...]).astype(BF16)
+    copy_own.wait()
+    copy_other.wait()
+    packed[...] = dot(normed, qkv[...].reshape(D, 3 * WIDTH)).astype(BF16)
     attend(packed, mixed_ref, None)
+    mixed_ref[:, WIDTH:] = tokens_ref[...]
+
+
+def gather_rows(weights_ref, first, target, sems):
+    width = target.shape[-1]
+    return [
+        pltpu.make_async_copy(
+            weights_ref.at[y, c, :, :, first : first + width], target.at[:, y, c], sems.at[2 * y + c]
+        )
+        for y in range(Y)
+        for c in range(2)
+    ]
+
+
+def pack_kernel(ids_ref, states_ref, qkv_ref, text_ref, out_s_ref, out_t_ref, video_ref, packed_ref):
+    ids = ids_ref[...]
+    positions = lax.broadcasted_iota(jnp.int32, ids.shape, 1)
+    end_place = jnp.min(jnp.where(ids == jnp.max(ids), positions, ids.shape[1]))
+    states = states_ref[...].astype(F32)
+    rows = lax.broadcasted_iota(jnp.int32, states.shape, 0)
+    text_row = jnp.sum(jnp.where(rows == end_place, states, 0.0), axis=0, keepdims=True)
+    text = jnp.concatenate([text_ref[...].astype(F32), jnp.zeros((4, E), F32)], axis=0)
+    place = lax.broadcasted_iota(jnp.int32, text.shape, 0)
+    text = jnp.where(place < 12, text, jnp.where(place == 12, text_row, 0.0))
+    packed_ref[:, QKV_T : QKV_T + 3 * WIDTH] = qkv_ref[...]
+    packed_ref[:, W_TEXT : W_TEXT + E] = text.astype(BF16)
+    outs = jnp.concatenate([out_s_ref[...].astype(F32), out_t_ref[...].astype(F32)], axis=0)
+    packed_ref[:, W_OUT : W_OUT + D] = outs.astype(BF16)
+    packed_ref[:, W_VIDEO : W_VIDEO + E] = video_ref[...]
 
 
 def temporal_kernel(
-    mixed_ref, tokens_ref, gain_ref, weights_ref, out_ref, pool_ref, qkv, outs, packed, mixed, sems
+    arrived_ref, gain_ref, weights_ref, out_ref, pool_ref, qkv, outs, packed, mixed, sems
 ):
-    copy_out = pltpu.make_async_copy(weights_ref.at[:, W_OUT : W_OUT + D], outs, sems.at[0])
-    copy_qkv = pltpu.make_async_copy(
-        weights_ref.at[:, QKV_T : QKV_T + 3 * WIDTH], qkv, sems.at[1]
-    )
-    copy_out.start()
-    copy_qkv.start()
-    copy_out.wait()
+    copies_out = gather_rows(weights_ref, W_OUT, outs, sems.at[0])
+    copies_qkv = gather_rows(weights_ref, QKV_T, qkv, sems.at[1])
+    for copy in copies_out + copies_qkv:
+        copy.start()
+    for copy in copies_out:
+        copy.wait()
     both = outs[...].astype(F32).reshape(64, 2, 8, D)
     out_spatial = both[:, 0].reshape(WIDTH, D).astype(BF16)
     out_temporal = both[:, 1].reshape(WIDTH, D).astype(BF16)
-    spatial = (tokens_ref[...].astype(F32) + dot(mixed_ref[...], out_spatial)).astype(BF16)
+    spatial = arrived_ref[:, WIDTH:].astype(F32) + dot(arrived_ref[:, :WIDTH], out_spatial)
+    spatial = spatial.astype(BF16)
     normed = layer_norm(spatial.astype(F32), gain_ref[...]).astype(BF16)
-    copy_qkv.wait()
-    packed[...] = dot(normed, qkv[...]).astype(BF16)
+    for copy in copies_qkv:
+        copy.wait()
+    packed[...] = dot(normed, qkv[...].reshape(D, 3 * WIDTH)).astype(BF16)
     rows = packed.shape[0]
     patches = 32
     place = lax.broadcasted_iota(jnp.int32, (rows, rows), 0) % patches
@@ -108,27 +152,35 @@
     out_ref[...] = output
     total = jnp.sum(output.astype(F32), axis=0, keepdims=True)
     for chunk in range(D // 128):
-        pool_ref[:, chunk, :] = jnp.broadcast_to(total[:, chunk * 128 : (chunk + 1) * 128], (8, 128))
+        pool_ref[:, chunk, :] = jnp.broadcast_to(
+            total[:, chunk * 128 : (chunk + 1) * 128], (2 * FRAMES, 128)
+        )
 
 
 def spread_kernel(parts_ref, every_ref):
-    mine = jnp.sum(parts_ref[...], axis=0) * (1.0 / (8 * 256))
-    every_ref[...] = jnp.broadcast_to(mine[None], every_ref.shape)
-
-
-def text_kernel(gain_ref, weights_ref, pool_ref, mapped_ref, weight_ref, packed, sem):
-    copy = pltpu.make_async_copy(weights_ref.at[:, W_TEXT : W_TEXT + E], packed, sem)
-    copy.start()
-    copy.wait()
+    for c in range(2):
+        total = jnp.sum(parts_ref[c * FRAMES : (c + 1) * FRAMES], axis=0) * (1.0 / (8 * 256))
+        every_ref[:, c] = jnp.broadcast_to(total[None], (X * Y,) + total.shape)
+
+
+def text_kernel(
+    gain_ref, weights_ref, pool_ref, mapped_ref, weight_ref, gathered, sems
+):
+    copies = gather_rows(weights_ref, W_TEXT, gathered, sems)
+    for copy in copies:
+        copy.start()
+    for copy in copies:
+        copy.wait()
+    packed = gathered[...].reshape(D, E)
     column = lax.broadcasted_iota(jnp.int32, (DT, D), 1)
     place = column % 16
     row = jnp.where(place < 12, (column // 16) * 12 + place, -1)
     pick = (row == lax.broadcasted_iota(jnp.int32, (DT, D), 0)).astype(BF16)
-    weight = dot(pick, packed[...]).astype(BF16)
+    weight = dot(pick, packed).astype(BF16)
     weight_ref[...] = weight
     column = lax.broadcasted_iota(jnp.int32, (64, D), 1)
     pick = (column == 16 * lax.broadcasted_iota(jnp.int32, (64, D), 0) + 12).astype(BF16)
-    pool = dot(pick, packed[...])
+    pool = dot(pick, packed)
     pool_ref[...] = pool
     mapped_ref[...] = exact(dot, layer_norm(pool, gain_ref[...]), weight)
 
@@ -167,20 +219,23 @@
     text_loss_ref,
     grad_pooled_ref,
     grad_text_ref,
-    weight,
+    gathered,
     pooled_all,
-    sem,
+    sems,
 ):
-    copy = pltpu.make_async_copy(weights_ref.at[:, W_VIDEO : W_VIDEO + E], weight, sem)
-    copy.start()
     me = place_ref[0]
+    copies = gather_rows(weights_ref, W_VIDEO, gathered, sems)
+    for copy in copies:
+        copy.start()
     scale = scale_ref[0]
     for chunk in range(D // 128):
         pooled_all[:, chunk * 128 : (chunk + 1) * 128] = pooled_ref[:, chunk, :]
     gain = gain_video_ref[...]
     normed = layer_norm(pooled_all[...], gain)
-    copy.wait()
-    mapped = exact(dot, normed, weight[...])
+    for copy in copies:
+        copy.wait()
+    weight = gathered[...].reshape(D, E)
+    mapped = exact(dot, normed, weight)
     video = unit_rows(mapped)
     text_mapped = text_mapped_ref[...]
     text = unit_rows(text_mapped)
@@ -215,7 +270,7 @@
     mine_text_mapped = jnp.sum(jnp.where(mine_row, text_mapped, 0.0), axis=0, keepdims=True)
     mine_pooled = jnp.sum(jnp.where(mine_row, pooled_all[...], 0.0), axis=0, keepdims=True)
     mine_text_pool = jnp.sum(jnp.where(mine_row, text_pool_ref[...], 0.0), axis=0, keepdims=True)
-    back = exact(dot_t, unit_back(mine_mapped, grad_video), weight[...])
+    back = exact(dot_t, unit_back(mine_mapped, grad_video), weight)
     grad_pooled_ref[...] = norm_back(mine_pooled, gain, back)
     back = exact(dot_t, unit_back(mine_text_mapped, grad_caption), text_weight_ref[...])
     grad_text_ref[...] = norm_back(mine_text_pool, gain_text_ref[...], back)
@@ -238,6 +293,11 @@
 
 def shape(dims, dtype):
     return jax.ShapeDtypeStruct(dims, dtype)
+
+
+def send_all(block, groups):
+    copies = jnp.broadcast_to(block[None], (len(groups[0]),) + block.shape)
+    return lax.all_to_all(copies, "dp", 0, 0, tiled=True, axis_index_groups=groups)
 
 
 def on_device(
@@ -259,55 +319,68 @@
 ):
     V, S, A = pltpu.VMEM, pltpu.SMEM, pl.ANY
     DMA = pltpu.SemaphoreType.DMA
+    halves = (X, Y, 2, 16)
     tokens = video_tokens.reshape(256, D)
-    end_place = jnp.argmax(caption_ids[0])
-    text_row = lax.dynamic_slice_in_dim(text_states[0], end_place, 1, 0)
-    text_part = jnp.concatenate([w_text, text_row, jnp.zeros((3, E), BF16)], axis=0)
-    outs = jnp.concatenate([w_out_spatial, w_out_temporal], axis=0)
-    mine = jnp.concatenate([w_qkv_spatial, w_qkv_temporal, w_video, text_part, outs], axis=1)
-    weights = lax.all_gather(mine, "dp", axis=0, tiled=True)
-    by_patch = lax.all_to_all(tokens.reshape(8, 32, D), "frame", 0, 0, tiled=True)
+    place = lax.axis_index("dp").astype(jnp.int32).reshape(1)
+    core = place % 2
+    packed = call(pack_kernel, shape((16, PACKED), BF16), (V,) * 7, [])(
+        caption_ids,
+        text_states.reshape(text_states.shape[1:]),
+        w_qkv_temporal,
+        w_text,
+        w_out_spatial,
+        w_out_temporal,
+        w_video,
+    )
+    own = send_all(w_qkv_spatial, ROWS_OF_Y)
+    packed = lax.all_gather(packed, "dp", axis=0, tiled=True, axis_index_groups=ROWS_OF_X)
+    own, packed = lax.optimization_barrier((own, packed))
+    weights = lax.all_gather(packed, "dp", axis=0, tiled=True, axis_index_groups=ROWS_OF_YC)
+    weights = weights.reshape(Y, 2, X, 16, PACKED)
+    own = send_all(own.reshape(Y * 16, 3 * WIDTH), ROWS_OF_X).reshape(X * Y, 16, 3 * WIDTH)
+    other = lax.ppermute(own, "dp", OTHER_CORE)
 
     mixed = call(
         spatial_kernel,
-        shape((256, WIDTH), BF16),
-        (V, V, A),
-        [pltpu.VMEM((D, 3 * WIDTH), BF16), pltpu.VMEM((256, 3 * WIDTH), BF16), DMA],
-    )(tokens, gain_spatial.reshape(1, D), weights)
-    mixed = lax.all_to_all(mixed.reshape(8, 32, WIDTH), "frame", 0, 0, tiled=True)
+        shape((256, WIDTH + D), BF16),
+        (S, V, V, A, A),
+        [pltpu.VMEM((X * Y, 2, 16, 3 * WIDTH), BF16), pltpu.VMEM((256, 3 * WIDTH), BF16), DMA((2,))],
+    )(core, tokens, gain_spatial.reshape(1, D), own, other)
+    mixed = lax.all_to_all(mixed.reshape(8, 32, WIDTH + D), "frame", 0, 0, tiled=True)
     layer_out, pool = call(
         temporal_kernel,
-        (shape((256, D), BF16), shape((8, 8, 128), F32)),
-        (V, V, V, A),
+        (shape((256, D), BF16), shape((2 * FRAMES, 8, 128), F32)),
+        (V, V, A),
         [
-            pltpu.VMEM((D, 3 * WIDTH), BF16),
-            pltpu.VMEM((D, D), BF16),
+            pltpu.VMEM(halves + (3 * WIDTH,), BF16),
+            pltpu.VMEM(halves + (D,), BF16),
             pltpu.VMEM((256, 3 * WIDTH), BF16),
             pltpu.VMEM((256, WIDTH), BF16),
-            DMA((2,)),
+            DMA((2, 2 * Y)),
         ],
-    )(mixed.reshape(256, WIDTH), by_patch.reshape(256, D), gain_temporal.reshape(1, D), weights)
+    )(mixed.reshape(256, WIDTH + D), gain_temporal.reshape(1, D), weights)
     text_pool, text_mapped, text_weight = call(
         text_kernel,
         (shape((64, DT), F32), shape((64, E), F32), shape((DT, E), BF16)),
         (V, A),
-        [pltpu.VMEM((D, E), BF16), DMA],
+        [pltpu.VMEM(halves + (E,), BF16), DMA((2 * Y,))],
     )(gain_text.reshape(1, DT), weights)
-    pool = lax.all_to_all(pool, "frame", 0, 0, tiled=True)
-    pool = call(spread_kernel, shape((64, 8, 128), F32), (V,), [])(pool)
-    pooled = lax.all_to_all(pool, "dp", 0, 0, tiled=True)
-    place = lax.axis_index("dp").astype(jnp.int32).reshape(1)
+    pool = lax.all_to_all(
+        pool, ("dp", "frame"), 0, 0, tiled=True, axis_index_groups=CORES_AND_FRAMES
+    )
+    pool = call(spread_kernel, shape((X * Y, 2, 8, 128), F32), (V,), [])(pool)
+    pooled = lax.all_to_all(pool, "dp", 0, 0, tiled=True, axis_index_groups=CHIPS_OF_CORE)
     video_loss, text_loss, grad_pooled, grad_text = call(
         loss_kernel,
         (shape((1,), F32), shape((1,), F32), shape((1, D), F32), shape((1, DT), F32)),
         (S, S, V, V, V, V, V, V, V, A),
-        [pltpu.VMEM((D, E), BF16), pltpu.VMEM((64, D), F32), DMA],
+        [pltpu.VMEM(halves + (E,), BF16), pltpu.VMEM((64, D), F32), DMA((2 * Y,))],
         (S, S, V, V),
     )(
         place,
         logit_scale,
         pair_index.reshape(64, 1),
-        pooled,
+        pooled.reshape(64, 8, 128),
         text_pool,
         text_mapped,
         text_weight,

time: 189 us -> 155 us (0.82)
  the two profiles are of different devices: /device:TPU:1 before, /device:TPU:8 now
where the time goes in v2:
time: 155 us; the launch traced here: 154 us
  blocking collectives  79.2 us (51%)
  Pallas kernels  21.5 us (14%)
  starting transfers between devices  20.1 us (13%)
  between operations  14.8 us (10%)
  waiting for transfers between devices  10.1 us (7%)
  local copies, waits for them, and re-layouts  8.12 us (5%)
    all_to_all x1, blocking collectives, on_device(): lax.all_to_all(mixed.reshape(8, 32, WIDTH + D), 'frame', 0, 0, tiled=True)  33.1 us
    all_to_all x1, blocking collectives, send_all(): lax.all_to_all(copies, 'dp', 0, 0, tiled=True, axis_index_groups=groups)  20 us
    all_gather x1, blocking collectives, on_device(): lax.all_gather(packed, 'dp', axis=0, tiled=True, axis_index_groups=ROWS_O...  14.1 us
    all_to_all x1, blocking collectives, on_device(): lax.all_to_all(pool, ('dp', 'frame'), 0, 0, tiled=True, axis_index_groups...  12 us
    all_to_all x1, starting transfers between devices, send_all(): lax.all_to_all(copies, 'dp', 0, 0, tiled=True, axis_index_groups=groups)  9.18 us
    all_to_all x1, starting transfers between devices, on_device(): lax.all_to_all(pool, 'dp', 0, 0, tiled=True, axis_index_groups=CHIPS_OF_C...  9.01 us
    all_to_all x1, waiting for transfers between devices, on_device(): lax.all_to_all(pool, 'dp', 0, 0, tiled=True, axis_index_groups=CHIPS_OF_C...  6.71 us
    pallas_call x1, Pallas kernels, on_device(): call(loss_kernel, (shape((1,), F32), shape((1,), F32), shape((1, D), F32)...  6.62 us
  transfers between devices with their start and end apart: 4, of which 2 were waited for; matrix products, arithmetic and copies ran while one was open for 0% of the time, Pallas kernels for 5%

profile of v2, /device:TPU:8, one launch (start us, length us, event | category | flops | bytes accessed | tf_op | source)
XLA Modules:
  0.0 153.8 jit_solution(17376455062209066344)
XLA Ops:
  7.2 1.6 %broadcast_in_dim.6 = bf16[8,16,1536]{2,1,0:T(8,128)(2,1)} broadcast(bf16[16,1536]{1,0:T(8,128)(2,1)} %param.24), dimensions={1,2} | broadcast | bytes 442368 | tf_op jit(solution)/shard_map/broadcast_in_dim | solution.py:299
  8.7 9.2 %all-to-all-start = ((bf16[8,16,1536]{2,1,0:T(8,128)(2,1)}), bf16[8,16,1536]{2,1,0:T(8,128)(2,1)S(1)}, u32[]{:S(2)}, u32[]{:S(2)}) async-start(bf16[8,16,1536]{2,1,0:T(8,128)(2,1)} %broadcast_in_dim.6), calls=%async_computation | async-start | bytes 786432 | tf_op jit(solution)/shard_map/all_to_all | solution.py:300
  17.9 0.0 all-gather.2.cloned.1.call-start
  17.9 0.0 copy-start.1
  17.9 0.9 copy-done.1
  18.8 0.0 copy-start.2
  18.8 0.8 copy-done.2
  19.6 0.0 copy-start.3
  19.6 0.7 copy-done.3
  20.4 0.0 copy-start.4
  20.4 0.7 copy-done.4
  21.1 0.0 copy-start.5
  21.1 0.7 copy-done.5
  21.8 0.0 copy-start.6
  21.8 0.7 copy-done.6
  22.5 0.0 copy-start.10
  22.5 0.7 copy-done.10
  23.2 0.4 shard_map.182
  23.6 14.1 %all_gather.6 = bf16[64,4096]{1,0:T(8,128)(2,1)} all-gather(bf16[16,4096]{1,0:T(8,128)(2,1)S(1)} %shard_map.182), channel_id=1, replica_groups={{0,128,256,384},{8,136,264,392},{16,144,272,400},{24,152,280,408},{32,1..., dimensions={0}, use_global_device_ids=true | all-gather | bytes 655360 | tf_op jit(solution)/shard_map/all_gather | solution.py:336
  37.7 0.0 all-to-all-done
  37.7 0.0 all-gather.2.cloned.1.call-update
  37.7 0.1 broadcast_in_dim.15
  37.9 0.0 copy-start.9
  37.9 20.0 %all_to_all.25 = bf16[4,128,1536]{2,1,0:T(8,128)(2,1)S(1)} all-to-all(bf16[4,128,1536]{2,1,0:T(8,128)(2,1)S(1)} %broadcast_in_dim.15), channel_id=1, replica_groups={{0,128,256,384},{8,136,264,392},{16,144,272,400},{24,152,280,408},{32,1..., dimensions={0} | all-to-all | bytes 3145728 | tf_op jit(solution)/shard_map/all_to_all | solution.py:300
  57.9 1.9 %collective-permute-start = (bf16[32,16,1536]{2,1,0:T(8,128)(2,1)S(1)}, bf16[32,16,1536]{2,1,0:T(8,128)(2,1)S(1)}, u32[]{:S(2)}, u32[]{:S(2)}) collective-permute-start(bf16[32,16,1536]{2,1,0:T(8,128)(2,1)S(1)} %bitcast.14), channel_id=1, source_target_pairs={{0,8},{8,0},{16,24},{24,16},{32,40},{40,32},{48,56},{56,48},{64,72... | collective-permute-start | bytes 4718600 | tf_op jit(solution)/shard_map/ppermute | solution.py:341
  59.8 3.4 %collective-permute-done.other_ref = bf16[32,16,1536]{2,1,0:T(8,128)(2,1)S(1)} collective-permute-done((bf16[32,16,1536]{2,1,0:T(8,128)(2,1)S(1)}, bf16[32,16,1536]{2,1,0:T(8,128)(2,1)S(1)}, u32[]{:S(2)}, u32[]{:S(2)}) %collective-permute-start) | collective-permute-done | bytes 1572896 | tf_op jit(solution)/shard_map/ppermute | solution.py:341
  63.2 0.0 copy-done.9
  63.2 0.0 copy-start
  63.2 1.0 copy-done
  64.3 2.9 %shard_map.183 = bf16[256,1536]{1,0:T(8,128)(2,1)S(1)} custom-call(s32[1]{0:T(128)S(6)} %select_n.7.core_ref, bf16[256,1024]{1,0:T(8,128)(2,1)S(1)} %bitcast.19, f32[1,1024]{1,0:T(1,128)S(1)} %bitcast.23, bf16[32,16,1536]{2,1,0:T(8,128)(2,1)S(1)} %bitcast.15, bf16[32,16,1536]{2,1,0:T(8,128)(2,1)S(1)} %collective-permute-done.other_ref), custom_call_target="tpu_custom_call" | custom-call | tf_op jit(solution)/shard_map/pallas_call | solution.py:343
  67.2 0.0 copy-start.7
  67.2 33.1 %all_to_all.26 = bf16[8,32,1536]{2,1,0:T(8,128)(2,1)S(1)} all-to-all(bf16[8,32,1536]{2,1,0:T(8,128)(2,1)S(1)} %bitcast.17), channel_id=1, replica_groups=mesh['dp'=64,'frame'=8] {'frame'}, dimensions={0} | all-to-all | bytes 1572864 | tf_op jit(solution)/shard_map/all_to_all | solution.py:349
  100.3 0.0 all-gather.2.cloned.1.call-done
  100.3 0.0 copy-done.7
  100.3 0.0 copy-start.12
  100.3 0.0 copy-start.11
  100.4 6.2 %shard_map.184 = (bf16[256,1024]{1,0:T(8,128)(2,1)}, f32[16,8,128]{2,1,0:T(8,128)S(1)}) custom-call(bf16[256,1536]{1,0:T(8,128)(2,1)S(1)} %bitcast.16, f32[1,1024]{1,0:T(1,128)S(1)} %bitcast.21, bf16[8,2,4,16,4096]{4,3,2,1,0:T(8,128)(2,1)} %bitcast.24), custom_call_target="tpu_custom_call" | custom-call | tf_op jit(solution)/shard_map/pallas_call | solution.py:350
  106.6 12.0 %all_to_all.27.parts_ref = f32[16,8,128]{2,1,0:T(8,128)S(1)} all-to-all(f32[16,8,128]{2,1,0:T(8,128)S(1)} %get-tuple-element.19), channel_id=1, replica_groups={{0,1,2,3,4,5,6,7,8,9,10,11,12,13,14,15},{16,17,18,19,20,21,22,23,24,25,..., dimensions={0} | all-to-all | bytes 131072 | tf_op jit(solution)/shard_map/all_to_all | solution.py:368
  118.5 0.7 shard_map.185
  119.3 9.0 %all-to-all-start.4 = ((f32[32,2,8,128]{3,2,1,0:T(8,128)}), f32[32,2,8,128]{3,2,1,0:T(8,128)S(1)}, u32[]{:S(2)}, u32[]{:S(2)}) async-start(f32[32,2,8,128]{3,2,1,0:T(8,128)} %shard_map.185), calls=%async_computation.4 | async-start | bytes 524288 | tf_op jit(solution)/shard_map/all_to_all | solution.py:372
  128.9 0.0 copy-done.12
  129.0 0.1 copy.20.pairs_ref
  129.1 0.0 copy-done.11
  129.1 0.0 copy-start.8
  129.1 4.6 %shard_map.186 = (f32[64,768]{1,0:T(8,128)S(1)}, f32[64,768]{1,0:T(8,128)S(1)}, bf16[768,768]{1,0:T(8,128)(2,1)S(1)}) custom-call(f32[1,768]{1,0:T(1,128)S(1)} %reshape.69.gain_ref.gain_text_ref, bf16[8,2,4,16,4096]{4,3,2,1,0:T(8,128)(2,1)} %bitcast.25), custom_call_target="tpu_custom_call" | custom-call | tf_op jit(solution)/shard_map/pallas_call | solution.py:362
  133.6 6.7 %all-to-all-done.4 = f32[32,2,8,128]{3,2,1,0:T(8,128)S(1)} async-done(((f32[32,2,8,128]{3,2,1,0:T(8,128)}), f32[32,2,8,128]{3,2,1,0:T(8,128)S(1)}, u32[]{:S(2)}, u32[]{:S(2)}) %all-to-all-start.4) | async-done | bytes 262176 | tf_op jit(solution)/shard_map/all_to_all | solution.py:372
  140.4 0.0 copy-done.8
  140.4 6.6 %shard_map.187 = (f32[1]{0:T(128)}, f32[1]{0:T(128)}, f32[1,1024]{1,0:T(1,128)}, f32[1,768]{1,0:T(1,128)}) custom-call(s32[1]{0:T(128)} %bitcast.place_ref, f32[1]{0:T(128)S(6)} %copy.21.scale_ref, s32[64,1]{1,0:T(8,128)S(1)} %copy.20.pairs_ref, f32[64,8,128]{2,1,0:T(8,128)S(1)} %bitcast.18, f32[64,768]{1,0:T(8,128)S(1)} %get-tuple-element.20.text_pool_ref, ...), custom_call_target="tpu_custom_call" | custom-call | tf_op jit(solution)/shard_map/pallas_call | solution.py:373
  (1 shorter events, 0.0 us)
Async XLA Ops:
  8.7 29.0 %all-to-all-start = ((bf16[8,16,1536]{2,1,0:T(8,128)(2,1)}), bf16[8,16,1536]{2,1,0:T(8,128)(2,1)S(1)}, u32[]{:S(2)}, u32[]{:S(2)}) async-start(bf16[8,16,1536]{2,1,0:T(8,128)(2,1)} %broadcast_in_dim.6), calls=%async_computation | async-start | bytes 786432 | tf_op jit(solution)/shard_map/all_to_all | solution.py:300
  17.9 82.4 %all-gather.2.cloned.1.call-start = ((), (), s32[]{:S(2)}) async-start(), calls=%async_computation.5 | async-start | bytes 8912896 | tf_op jit(solution)/shard_map/all_gather | solution.py:338
  17.9 0.9 copy-start.1
  18.8 0.8 copy-start.2
  19.6 0.7 copy-start.3
  20.4 0.7 copy-start.4
  21.1 0.7 copy-start.5
  21.8 0.7 copy-start.6
  22.5 0.7 copy-start.10
  37.9 25.3 %copy-start.9 = (f32[1024]{0:T(1024)S(1)}, f32[1024]{0:T(1024)}, u32[]{:S(2)}) copy-start(f32[1024]{0:T(1024)} %param.20) | copy-start | bytes 12292
  57.9 5.3 %collective-permute-start = (bf16[32,16,1536]{2,1,0:T(8,128)(2,1)S(1)}, bf16[32,16,1536]{2,1,0:T(8,128)(2,1)S(1)}, u32[]{:S(2)}, u32[]{:S(2)}) collective-permute-start(bf16[32,16,1536]{2,1,0:T(8,128)(2,1)S(1)} %bitcast.14), channel_id=1, source_target_pairs={{0,8},{8,0},{16,24},{24,16},{32,40},{40,32},{48,56},{56,48},{64,72... | collective-permute-start | bytes 4718600 | tf_op jit(solution)/shard_map/ppermute | solution.py:341
  63.2 1.0 copy-start
  67.2 33.2 %copy-start.7 = (f32[1024]{0:T(1024)S(1)}, f32[1024]{0:T(1024)}, u32[]{:S(2)}) copy-start(f32[1024]{0:T(1024)} %param.21) | copy-start | bytes 12292
  100.3 28.6 %copy-start.12 = (s32[64]{0:T(128)S(1)}, s32[64]{0:T(128)}, u32[]{:S(2)}) copy-start(s32[64]{0:T(128)} %param.18) | copy-start | bytes 772
  100.3 28.7 %copy-start.11 = (f32[768]{0:T(1024)S(1)}, f32[768]{0:T(1024)}, u32[]{:S(2)}) copy-start(f32[768]{0:T(1024)} %param.23) | copy-start | bytes 9220
  119.3 21.1 %all-to-all-start.4 = ((f32[32,2,8,128]{3,2,1,0:T(8,128)}), f32[32,2,8,128]{3,2,1,0:T(8,128)S(1)}, u32[]{:S(2)}, u32[]{:S(2)}) async-start(f32[32,2,8,128]{3,2,1,0:T(8,128)} %shard_map.185), calls=%async_computation.4 | async-start | bytes 524288 | tf_op jit(solution)/shard_map/all_to_all | solution.py:372
  129.1 11.3 %copy-start.8 = (f32[1024]{0:T(1024)S(1)}, f32[1024]{0:T(1024)}, u32[]{:S(2)}) copy-start(f32[1024]{0:T(1024)} %param.22) | copy-start | bytes 12292
Sparse Core Ops, SparseCore 0:
  37.9 59.1 all-gather.1

commit v3 on v2

--- a/solution.py
+++ b/solution.py
@@ -17,7 +17,10 @@
 UNIT_EPS = 1e-06
 F32 = jnp.float32
 BF16 = jnp.bfloat16
-VMEM_LIMIT = 48 * 1024 * 1024
+MIB = 1024 * 1024
+VMEM_LIMIT = 48 * MIB
+VMEM_WHOLE = 63 * MIB
+VMEM_MOST = 52 * MIB
 
 QKV_T = 0
 W_TEXT = 1536
@@ -29,12 +32,8 @@
 ROWS_OF_X = [[(x * Y + y) * 2 + c for x in range(X)] for y in range(Y) for c in range(2)]
 ROWS_OF_Y = [[(x * Y + y) * 2 + c for y in range(Y)] for x in range(X) for c in range(2)]
 ROWS_OF_YC = [[(x * Y + y) * 2 + c for y in range(Y) for c in range(2)] for x in range(X)]
-CHIPS_OF_CORE = [[i * 2 + c for i in range(X * Y)] for c in range(2)]
 OTHER_CORE = [(i, i ^ 1) for i in range(2 * X * Y)]
 FRAMES = 8
-CORES_AND_FRAMES = [
-    [(2 * i + c) * FRAMES + f for c in range(2) for f in range(FRAMES)] for i in range(X * Y)
-]
 
 
 def dot(a, b):
@@ -54,8 +53,16 @@
 
 
 def exact(dot_fn, a, weight):
-    first, second, third = pieces(a)
-    return dot_fn(third, weight) + dot_fn(second, weight) + dot_fn(first, weight)
+    rows = a.shape[0]
+    parts = dot_fn(jnp.concatenate(pieces(a), axis=0), weight)
+    return parts[2 * rows :] + parts[rows : 2 * rows] + parts[:rows]
+
+
+def exact_row(dot_fn, a, weight):
+    rows = lax.broadcasted_iota(jnp.int32, (16, a.shape[1]), 0)
+    first, second, third = (piece.astype(F32) for piece in pieces(a))
+    block = jnp.where(rows == 0, third, jnp.where(rows == 1, second, jnp.where(rows == 2, first, 0.0)))
+    return jnp.sum(dot_fn(block.astype(BF16), weight), axis=0, keepdims=True)
 
 
 def layer_norm(values, gain):
@@ -64,37 +71,63 @@
     return center * lax.rsqrt(spread + NORM_EPS) * gain
 
 
-def attend(packed_ref, mixed_ref, mask):
-    rows = packed_ref.shape[0]
-    low = lax.broadcasted_iota(jnp.int32, (rows, 2 * HD), 1) < HD
-    for pair in range(HEADS // 2):
-        at = pair * 2 * HD
-        query = packed_ref[:, at : at + 2 * HD]
-        key = packed_ref[:, WIDTH + at : WIDTH + at + 2 * HD]
-        value = packed_ref[:, 2 * WIDTH + at : 2 * WIDTH + at + 2 * HD]
-        mixed = []
-        for lanes in (low, ~low):
-            scores = dot_t(jnp.where(lanes, query, jnp.zeros_like(query)), key) * (HD**-0.5)
-            if mask is not None:
-                scores = jnp.where(mask, scores, -1e30)
-            weight = jnp.exp(scores - jnp.max(scores, axis=-1, keepdims=True))
-            probs = weight * (1.0 / jnp.sum(weight, axis=-1, keepdims=True))
-            mixed.append(dot(probs.astype(BF16), value))
-        mixed_ref[:, at : at + 2 * HD] = jnp.where(low, mixed[0], mixed[1]).astype(BF16)
-
-
-def spatial_kernel(core_ref, tokens_ref, gain_ref, own_ref, other_ref, mixed_ref, qkv, packed, sems):
+def attend_pair(query, key, value, mask):
+    low = lax.broadcasted_iota(jnp.int32, query.shape, 1) < HD
+    mixed = []
+    for lanes in (low, ~low):
+        scores = dot_t(jnp.where(lanes, query, jnp.zeros_like(query)), key) * (HD**-0.5)
+        if mask is not None:
+            scores = jnp.where(mask, scores, -1e30)
+        weight = jnp.exp(scores - jnp.max(scores, axis=-1, keepdims=True))
+        probs = weight * (1.0 / jnp.sum(weight, axis=-1, keepdims=True))
+        mixed.append(dot(probs.astype(BF16), value))
+    return jnp.where(low, mixed[0], mixed[1]).astype(BF16)
+
+
+def attend(packed_ref, mixed_ref):
+    for at in range(0, WIDTH, 2 * HD):
+        query, key, value = (
+            packed_ref[:, part * WIDTH + at : part * WIDTH + at + 2 * HD] for part in range(3)
+        )
+        mixed_ref[:, at : at + 2 * HD] = attend_pair(query, key, value, None)
+
+
+def attend_frames(packed_ref, mixed_ref):
+    frames, patches, _ = packed_ref.shape
+    block = 16
+    rows = frames * block
+    place = lax.broadcasted_iota(jnp.int32, (rows, rows), 0) % block
+    mask = place == lax.broadcasted_iota(jnp.int32, (rows, rows), 1) % block
+    for first in range(0, patches, block):
+        for at in range(0, WIDTH, 2 * HD):
+            query, key, value = (
+                packed_ref[
+                    :, first : first + block, part * WIDTH + at : part * WIDTH + at + 2 * HD
+                ].reshape(rows, 2 * HD)
+                for part in range(3)
+            )
+            mixed = attend_pair(query, key, value, mask)
+            mixed_ref[:, first : first + block, at : at + 2 * HD] = mixed.reshape(
+                frames, block, 2 * HD
+            )
+
+
+def spatial_kernel(
+    core_ref, tokens_ref, gain_ref, own_ref, other_ref, mixed_ref, tokens, qkv, packed, sems
+):
     core = core_ref[0]
+    copy_tokens = pltpu.make_async_copy(tokens_ref, tokens, sems.at[2])
     copy_own = pltpu.make_async_copy(own_ref, qkv.at[:, core], sems.at[0])
     copy_other = pltpu.make_async_copy(other_ref, qkv.at[:, 1 - core], sems.at[1])
+    copy_tokens.start()
     copy_own.start()
     copy_other.start()
-    normed = layer_norm(tokens_ref[...].astype(F32), gain_ref[...]).astype(BF16)
+    copy_tokens.wait()
+    normed = layer_norm(tokens[...].astype(F32), gain_ref[...]).astype(BF16)
     copy_own.wait()
     copy_other.wait()
     packed[...] = dot(normed, qkv[...].reshape(D, 3 * WIDTH)).astype(BF16)
-    attend(packed, mixed_ref, None)
-    mixed_ref[:, WIDTH:] = tokens_ref[...]
+    attend(packed, mixed_ref)
 
 
 def gather_rows(weights_ref, first, target, sems):
@@ -108,59 +141,95 @@
     ]
 
 
-def pack_kernel(ids_ref, states_ref, qkv_ref, text_ref, out_s_ref, out_t_ref, video_ref, packed_ref):
-    ids = ids_ref[...]
+def pack_kernel(
+    ids_ref, states_ref, qkv_ref, text_ref, out_s_ref, out_t_ref, video_ref, packed_ref,
+    ids_here, states_here, text_here, out_s_here, out_t_here, sems,
+):
+    pairs = (
+        (ids_ref, ids_here),
+        (states_ref, states_here),
+        (text_ref, text_here),
+        (out_s_ref, out_s_here),
+        (out_t_ref, out_t_here),
+        (qkv_ref, packed_ref.at[:, QKV_T : QKV_T + 3 * WIDTH]),
+        (video_ref, packed_ref.at[:, W_VIDEO : W_VIDEO + E]),
+    )
+    copies = [pltpu.make_async_copy(*pair, sems.at[i]) for i, pair in enumerate(pairs)]
+    for copy in copies:
+        copy.start()
+    for copy in copies:
+        copy.wait()
+    ids = ids_here[...]
     positions = lax.broadcasted_iota(jnp.int32, ids.shape, 1)
     end_place = jnp.min(jnp.where(ids == jnp.max(ids), positions, ids.shape[1]))
-    states = states_ref[...].astype(F32)
+    states = states_here[...].astype(F32)
     rows = lax.broadcasted_iota(jnp.int32, states.shape, 0)
     text_row = jnp.sum(jnp.where(rows == end_place, states, 0.0), axis=0, keepdims=True)
-    text = jnp.concatenate([text_ref[...].astype(F32), jnp.zeros((4, E), F32)], axis=0)
+    text = jnp.concatenate([text_here[...].astype(F32), jnp.zeros((4, E), F32)], axis=0)
     place = lax.broadcasted_iota(jnp.int32, text.shape, 0)
     text = jnp.where(place < 12, text, jnp.where(place == 12, text_row, 0.0))
-    packed_ref[:, QKV_T : QKV_T + 3 * WIDTH] = qkv_ref[...]
     packed_ref[:, W_TEXT : W_TEXT + E] = text.astype(BF16)
-    outs = jnp.concatenate([out_s_ref[...].astype(F32), out_t_ref[...].astype(F32)], axis=0)
+    outs = jnp.concatenate([out_s_here[...].astype(F32), out_t_here[...].astype(F32)], axis=0)
     packed_ref[:, W_OUT : W_OUT + D] = outs.astype(BF16)
-    packed_ref[:, W_VIDEO : W_VIDEO + E] = video_ref[...]
-
-
-def temporal_kernel(
-    arrived_ref, gain_ref, weights_ref, out_ref, pool_ref, qkv, outs, packed, mixed, sems
-):
+
+
+def deal_kernel(frame_ref, tokens_ref, *rest):
+    dealt, sems = rest[:-1], rest[-1]
+    copies = [
+        pltpu.make_async_copy(
+            tokens_ref.at[(frame_ref[0] + step) % FRAMES], dealt[step - 1], sems.at[step - 1]
+        )
+        for step in range(1, FRAMES)
+    ]
+    for copy in copies:
+        copy.start()
+    for copy in copies:
+        copy.wait()
+
+
+def temporal_kernel(frame_ref, mixed_ref, gain_ref, weights_ref, tokens_ref, *rest):
+    dealt, rest = rest[: FRAMES - 1], rest[FRAMES - 1 :]
+    out_ref, pool_ref, tokens, qkv, outs, packed, mixed, sems = rest
+    frame = frame_ref[0]
+    copies_tokens = [pltpu.make_async_copy(tokens_ref.at[frame], tokens.at[frame], sems.at[2, 0])]
+    for step in range(1, FRAMES):
+        source = (frame + FRAMES - step) % FRAMES
+        copies_tokens.append(
+            pltpu.make_async_copy(dealt[step - 1], tokens.at[source], sems.at[2, step])
+        )
     copies_out = gather_rows(weights_ref, W_OUT, outs, sems.at[0])
     copies_qkv = gather_rows(weights_ref, QKV_T, qkv, sems.at[1])
-    for copy in copies_out + copies_qkv:
+    for copy in copies_out + copies_tokens + copies_qkv:
         copy.start()
     for copy in copies_out:
         copy.wait()
     both = outs[...].astype(F32).reshape(64, 2, 8, D)
     out_spatial = both[:, 0].reshape(WIDTH, D).astype(BF16)
     out_temporal = both[:, 1].reshape(WIDTH, D).astype(BF16)
-    spatial = arrived_ref[:, WIDTH:].astype(F32) + dot(arrived_ref[:, :WIDTH], out_spatial)
+    for copy in copies_tokens:
+        copy.wait()
+    rows = tokens.shape[0] * tokens.shape[1]
+    spatial = tokens[...].reshape(rows, D).astype(F32) + dot(mixed_ref[...], out_spatial)
     spatial = spatial.astype(BF16)
     normed = layer_norm(spatial.astype(F32), gain_ref[...]).astype(BF16)
     for copy in copies_qkv:
         copy.wait()
-    packed[...] = dot(normed, qkv[...].reshape(D, 3 * WIDTH)).astype(BF16)
-    rows = packed.shape[0]
-    patches = 32
-    place = lax.broadcasted_iota(jnp.int32, (rows, rows), 0) % patches
-    other = lax.broadcasted_iota(jnp.int32, (rows, rows), 1) % patches
-    attend(packed, mixed, place == other)
-    output = (spatial.astype(F32) + dot(mixed[...], out_temporal)).astype(BF16)
+    projected = dot(normed, qkv[...].reshape(D, 3 * WIDTH)).astype(BF16)
+    packed[...] = projected.reshape(packed.shape)
+    attend_frames(packed, mixed)
+    output = spatial.astype(F32) + dot(mixed[...].reshape(rows, WIDTH), out_temporal)
+    output = output.astype(BF16)
     out_ref[...] = output
     total = jnp.sum(output.astype(F32), axis=0, keepdims=True)
     for chunk in range(D // 128):
         pool_ref[:, chunk, :] = jnp.broadcast_to(
-            total[:, chunk * 128 : (chunk + 1) * 128], (2 * FRAMES, 128)
+            total[:, chunk * 128 : (chunk + 1) * 128], (FRAMES, 128)
         )
 
 
 def spread_kernel(parts_ref, every_ref):
-    for c in range(2):
-        total = jnp.sum(parts_ref[c * FRAMES : (c + 1) * FRAMES], axis=0) * (1.0 / (8 * 256))
-        every_ref[:, c] = jnp.broadcast_to(total[None], (X * Y,) + total.shape)
+    mine = jnp.sum(parts_ref[...], axis=0) * (1.0 / (8 * 256))
+    every_ref[...] = jnp.broadcast_to(mine[None], every_ref.shape)
 
 
 def text_kernel(
@@ -220,12 +289,14 @@
     grad_pooled_ref,
     grad_text_ref,
     gathered,
+    text_weight,
     pooled_all,
     sems,
 ):
     me = place_ref[0]
-    copies = gather_rows(weights_ref, W_VIDEO, gathered, sems)
-    for copy in copies:
+    copies = gather_rows(weights_ref, 0, gathered, sems)
+    copy_text = pltpu.make_async_copy(text_weight_ref, text_weight, sems.at[2 * Y])
+    for copy in copies + [copy_text]:
         copy.start()
     scale = scale_ref[0]
     for chunk in range(D // 128):
@@ -270,13 +341,14 @@
     mine_text_mapped = jnp.sum(jnp.where(mine_row, text_mapped, 0.0), axis=0, keepdims=True)
     mine_pooled = jnp.sum(jnp.where(mine_row, pooled_all[...], 0.0), axis=0, keepdims=True)
     mine_text_pool = jnp.sum(jnp.where(mine_row, text_pool_ref[...], 0.0), axis=0, keepdims=True)
-    back = exact(dot_t, unit_back(mine_mapped, grad_video), weight)
+    back = exact_row(dot_t, unit_back(mine_mapped, grad_video), weight)
     grad_pooled_ref[...] = norm_back(mine_pooled, gain, back)
-    back = exact(dot_t, unit_back(mine_text_mapped, grad_caption), text_weight_ref[...])
+    copy_text.wait()
+    back = exact_row(dot_t, unit_back(mine_text_mapped, grad_caption), text_weight[...])
     grad_text_ref[...] = norm_back(mine_text_pool, gain_text_ref[...], back)
 
 
-def call(kernel, out_shape, in_spaces, scratch, out_spaces=None, cost=(0, 0)):
+def call(kernel, out_shape, in_spaces, scratch, out_spaces=None, vmem=VMEM_LIMIT):
     many = isinstance(out_shape, (tuple, list))
     out_spaces = out_spaces or ([pltpu.VMEM] * (len(out_shape) if many else 1))
     out_specs = [pl.BlockSpec(memory_space=space) for space in out_spaces]
@@ -286,8 +358,7 @@
         in_specs=[pl.BlockSpec(memory_space=space) for space in in_spaces],
         out_specs=out_specs if many else out_specs[0],
         scratch_shapes=scratch,
-        compiler_params=pltpu.CompilerParams(vmem_limit_bytes=VMEM_LIMIT),
-        cost_estimate=pl.CostEstimate(flops=cost[0], bytes_accessed=cost[1], transcendentals=0),
+        compiler_params=pltpu.CompilerParams(vmem_limit_bytes=vmem),
     )
 
 
@@ -321,9 +392,23 @@
     DMA = pltpu.SemaphoreType.DMA
     halves = (X, Y, 2, 16)
     tokens = video_tokens.reshape(256, D)
+    dealing = video_tokens.reshape(FRAMES, 32, D)
     place = lax.axis_index("dp").astype(jnp.int32).reshape(1)
-    core = place % 2
-    packed = call(pack_kernel, shape((16, PACKED), BF16), (V,) * 7, [])(
+    frame = lax.axis_index("frame").astype(jnp.int32).reshape(1)
+    packed = call(
+        pack_kernel,
+        shape((16, PACKED), BF16),
+        (A,) * 7,
+        [
+            pltpu.VMEM(caption_ids.shape, jnp.int32),
+            pltpu.VMEM(text_states.shape[1:], BF16),
+            pltpu.VMEM(w_text.shape, BF16),
+            pltpu.VMEM(w_out_spatial.shape, BF16),
+            pltpu.VMEM(w_out_temporal.shape, BF16),
+            DMA((7,)),
+        ],
+        vmem=VMEM_WHOLE,
+    )(
         caption_ids,
         text_states.reshape(text_states.shape[1:]),
         w_qkv_temporal,
@@ -335,58 +420,80 @@
     own = send_all(w_qkv_spatial, ROWS_OF_Y)
     packed = lax.all_gather(packed, "dp", axis=0, tiled=True, axis_index_groups=ROWS_OF_X)
     own, packed = lax.optimization_barrier((own, packed))
-    weights = lax.all_gather(packed, "dp", axis=0, tiled=True, axis_index_groups=ROWS_OF_YC)
-    weights = weights.reshape(Y, 2, X, 16, PACKED)
+    early = lax.all_gather(
+        packed[:, :W_VIDEO], "dp", axis=0, tiled=True, axis_index_groups=ROWS_OF_YC
+    ).reshape(Y, 2, X, 16, W_VIDEO)
+    late = lax.all_gather(
+        packed[:, W_VIDEO:], "dp", axis=0, tiled=True, axis_index_groups=ROWS_OF_YC
+    ).reshape(Y, 2, X, 16, E)
     own = send_all(own.reshape(Y * 16, 3 * WIDTH), ROWS_OF_X).reshape(X * Y, 16, 3 * WIDTH)
+    dealt = call(
+        deal_kernel, (shape((32, D), BF16),) * (FRAMES - 1), (S, A), [DMA((FRAMES,))],
+        (A,) * (FRAMES - 1),
+    )(frame, dealing)
+    dealt = [
+        lax.ppermute(block, "frame", [(i, (i + 1 + step) % FRAMES) for i in range(FRAMES)])
+        for step, block in enumerate(dealt)
+    ]
     other = lax.ppermute(own, "dp", OTHER_CORE)
 
     mixed = call(
         spatial_kernel,
-        shape((256, WIDTH + D), BF16),
-        (S, V, V, A, A),
-        [pltpu.VMEM((X * Y, 2, 16, 3 * WIDTH), BF16), pltpu.VMEM((256, 3 * WIDTH), BF16), DMA((2,))],
-    )(core, tokens, gain_spatial.reshape(1, D), own, other)
-    mixed = lax.all_to_all(mixed.reshape(8, 32, WIDTH + D), "frame", 0, 0, tiled=True)
+        shape((256, WIDTH), BF16),
+        (S, A, V, A, A),
+        [
+            pltpu.VMEM((256, D), BF16),
+            pltpu.VMEM((X * Y, 2, 16, 3 * WIDTH), BF16),
+            pltpu.VMEM((256, 3 * WIDTH), BF16),
+            DMA((3,)),
+        ],
+    )(place % 2, tokens, gain_spatial.reshape(1, D), own, other)
+    mixed = lax.all_to_all(mixed.reshape(8, 32, WIDTH), "frame", 0, 0, tiled=True)
     layer_out, pool = call(
         temporal_kernel,
-        (shape((256, D), BF16), shape((2 * FRAMES, 8, 128), F32)),
-        (V, V, A),
+        (shape((256, D), BF16), shape((FRAMES, 8, 128), F32)),
+        (S, V, V, A, A) + (A,) * (FRAMES - 1),
         [
+            pltpu.VMEM((FRAMES, 32, D), BF16),
             pltpu.VMEM(halves + (3 * WIDTH,), BF16),
             pltpu.VMEM(halves + (D,), BF16),
-            pltpu.VMEM((256, 3 * WIDTH), BF16),
-            pltpu.VMEM((256, WIDTH), BF16),
-            DMA((2, 2 * Y)),
+            pltpu.VMEM((FRAMES, 32, 3 * WIDTH), BF16),
+            pltpu.VMEM((FRAMES, 32, WIDTH), BF16),
+            DMA((3, 2 * Y)),
         ],
-    )(mixed.reshape(256, WIDTH + D), gain_temporal.reshape(1, D), weights)
+    )(frame, mixed.reshape(256, WIDTH), gain_temporal.reshape(1, D), early, dealing, *dealt)
     text_pool, text_mapped, text_weight = call(
         text_kernel,
         (shape((64, DT), F32), shape((64, E), F32), shape((DT, E), BF16)),
         (V, A),
         [pltpu.VMEM(halves + (E,), BF16), DMA((2 * Y,))],
-    )(gain_text.reshape(1, DT), weights)
-    pool = lax.all_to_all(
-        pool, ("dp", "frame"), 0, 0, tiled=True, axis_index_groups=CORES_AND_FRAMES
-    )
-    pool = call(spread_kernel, shape((X * Y, 2, 8, 128), F32), (V,), [])(pool)
-    pooled = lax.all_to_all(pool, "dp", 0, 0, tiled=True, axis_index_groups=CHIPS_OF_CORE)
+    )(gain_text.reshape(1, DT), early)
+    pool = lax.all_to_all(pool, "frame", 0, 0, tiled=True)
+    pool = call(spread_kernel, shape((64, 8, 128), F32), (V,), [])(pool)
+    pooled = lax.all_to_all(pool, "dp", 0, 0, tiled=True)
     video_loss, text_loss, grad_pooled, grad_text = call(
         loss_kernel,
         (shape((1,), F32), shape((1,), F32), shape((1, D), F32), shape((1, DT), F32)),
-        (S, S, V, V, V, V, V, V, V, A),
-        [pltpu.VMEM(halves + (E,), BF16), pltpu.VMEM((64, D), F32), DMA((2 * Y,))],
+        (S, S, V, V, V, V, A, V, V, A),
+        [
+            pltpu.VMEM(halves + (E,), BF16),
+            pltpu.VMEM((DT, E), BF16),
+            pltpu.VMEM((64, D), F32),
+            DMA((2 * Y + 1,)),
+        ],
         (S, S, V, V),
+        vmem=VMEM_MOST,
     )(
         place,
         logit_scale,
         pair_index.reshape(64, 1),
-        pooled.reshape(64, 8, 128),
+        pooled,
         text_pool,
         text_mapped,
         text_weight,
         gain_video.reshape(1, D),
         gain_text.reshape(1, DT),
-        weights,
+        late,
     )
     return (layer_out.reshape(1, 8, 32, D), video_loss, text_loss, grad_pooled, grad_text)
 

time: 155 us -> 168 us (1.084)
  the two profiles are of different devices: /device:TPU:8 before, /device:TPU:1 now
where the time goes in v3:
time: 168 us; the launch traced here: 167 us
  starting transfers between devices  68.9 us (41%)
  waiting for transfers between devices  28.7 us (17%)
  Pallas kernels  27.3 us (16%)
  blocking collectives  22.8 us (14%)
  between operations  14.9 us (9%)
  local copies, waits for them, and re-layouts  4.44 us (3%)
    ppermute x7, starting transfers between devices, on_device(): lax.ppermute(block, 'frame', [(i, (i + 1 + step) % FRAMES) for i in range...  28.2 us
    all_to_all x2, waiting for transfers between devices, send_all(): lax.all_to_all(copies, 'dp', 0, 0, tiled=True, axis_index_groups=groups)  15.9 us
    all_to_all x2, starting transfers between devices, send_all(): lax.all_to_all(copies, 'dp', 0, 0, tiled=True, axis_index_groups=groups)  12 us
    all_gather x1, blocking collectives, on_device(): lax.all_gather(packed, 'dp', axis=0, tiled=True, axis_index_groups=ROWS_O...  11.9 us
    all_to_all x1, starting transfers between devices, on_device(): pooled = lax.all_to_all(pool, 'dp', 0, 0, tiled=True)  11.3 us
    all_to_all x1, blocking collectives, on_device(): pool = lax.all_to_all(pool, 'frame', 0, 0, tiled=True)  10.9 us
    all_to_all x1, starting transfers between devices, on_device(): lax.all_to_all(mixed.reshape(8, 32, WIDTH), 'frame', 0, 0, tiled=True)  10.4 us
    pallas_call x1, Pallas kernels, on_device(): call(temporal_kernel, (shape((256, D), BF16), shape((FRAMES, 8, 128), F32...  10.2 us
  transfers between devices with their start and end apart: 14, of which 5 were waited for; matrix products, arithmetic and copies ran while one was open for 1% of the time, Pallas kernels for 13%

profile of v3, /device:TPU:1, one launch (start us, length us, event | category | flops | bytes accessed | tf_op | source)
XLA Modules:
  0.0 167.1 jit_solution(16543747331860074949)
XLA Ops:
  7.2 1.6 broadcast_in_dim.6
  8.7 7.7 %all-to-all-start = ((bf16[8,16,1536]{2,1,0:T(8,128)(2,1)}), bf16[8,16,1536]{2,1,0:T(8,128)(2,1)S(1)}, u32[]{:S(2)}, u32[]{:S(2)}) async-start(bf16[8,16,1536]{2,1,0:T(8,128)(2,1)} %broadcast_in_dim.6), calls=%async_computation | async-start | bytes 786432 | tf_op jit(solution)/shard_map/all_to_all | solution.py:371
  16.4 0.0 all-gather.3.cloned.1.call-start
  16.4 2.1 %shard_map.182 = bf16[16,4096]{1,0:T(8,128)(2,1)} custom-call(s32[1,77]{1,0:T(1,128)} %ids_ref.1, bf16[77,768]{1,0:T(8,128)(2,1)} %bitcast.29, bf16[16,1536]{1,0:T(8,128)(2,1)} %qkv_ref.1, bf16[12,768]{1,0:T(8,128)(2,1)} %text_ref.1, bf16[8,1024]{1,0:T(8,128)(2,1)} %out_s_ref.1, bf16[8,1024]{1,0:T(8,128)(2,1)} %out_t_ref.1, bf16[16,768]{1,0:T(8,128)(2,1)} %video_ref.1), custom_call_target="tpu_custom_call" | custom-call | tf_op jit(solution)/shard_map/pallas_call | solution.py:398
  18.5 11.9 %all_gather.9 = bf16[64,4096]{1,0:T(8,128)(2,1)S(1)} all-gather(bf16[16,4096]{1,0:T(8,128)(2,1)} %shard_map.182), channel_id=1, replica_groups={{0,128,256,384},{8,136,264,392},{16,144,272,400},{24,152,280,408},{32,1..., dimensions={0}, use_global_device_ids=true | all-gather | bytes 655360 | tf_op jit(solution)/shard_map/all_gather | solution.py:421
  30.4 0.0 all-to-all-done
  30.4 0.8 slice.6
  31.2 0.0 all-gather.3.cloned.1.call-update
  31.2 1.3 broadcast_in_dim.15
  32.5 0.0 copy-start
  32.5 0.0 copy-start.1
  32.5 4.3 %all-to-all-start.1 = ((bf16[4,128,1536]{2,1,0:T(8,128)(2,1)}), bf16[4,128,1536]{2,1,0:T(8,128)(2,1)S(1)}, u32[]{:S(2)}, u32[]{:S(2)}) async-start(bf16[4,128,1536]{2,1,0:T(8,128)(2,1)} %broadcast_in_dim.15), calls=%async_computation.1 | async-start | bytes 3145728 | tf_op jit(solution)/shard_map/all_to_all | solution.py:371
  36.9 0.0 all-gather.5.cloned.1.call-start
  36.9 0.6 slice.7
  37.5 0.1 all-gather.5.cloned.1.call-update
  37.6 15.9 %all-to-all-done.1 = bf16[4,128,1536]{2,1,0:T(8,128)(2,1)S(1)} async-done(((bf16[4,128,1536]{2,1,0:T(8,128)(2,1)}), bf16[4,128,1536]{2,1,0:T(8,128)(2,1)S(1)}, u32[]{:S(2)}, u32[]{:S(2)}) %all-to-all-start.1) | async-done | bytes 1572896 | tf_op jit(solution)/shard_map/all_to_all | solution.py:371
  53.5 6.9 %collective-permute-start = (bf16[32,16,1536]{2,1,0:T(8,128)(2,1)S(1)}, bf16[32,16,1536]{2,1,0:T(8,128)(2,1)}, u32[]{:S(2)}, u32[]{:S(2)}) collective-permute-start(bf16[32,16,1536]{2,1,0:T(8,128)(2,1)S(1)} %bitcast.16), channel_id=1, source_target_pairs={{0,8},{8,0},{16,24},{24,16},{32,40},{40,32},{48,56},{56,48},{64,72... | collective-permute-start | bytes 4718600 | tf_op jit(solution)/shard_map/ppermute | solution.py:438
  60.4 3.1 %collective-permute-done.other_ref = bf16[32,16,1536]{2,1,0:T(8,128)(2,1)} collective-permute-done((bf16[32,16,1536]{2,1,0:T(8,128)(2,1)S(1)}, bf16[32,16,1536]{2,1,0:T(8,128)(2,1)}, u32[]{:S(2)}, u32[]{:S(2)}) %collective-permute-start) | collective-permute-done | bytes 1572896 | tf_op jit(solution)/shard_map/ppermute | solution.py:438
  63.6 0.0 copy-done
  63.6 0.0 copy-done.1
  63.6 0.0 copy-start.2
  63.6 4.5 %shard_map.183 = bf16[256,512]{1,0:T(8,128)(2,1)} custom-call(s32[1]{0:T(128)S(6)} %select_n.7.core_ref, bf16[256,1024]{1,0:T(8,128)(2,1)S(1)} %bitcast.18, f32[1,1024]{1,0:T(1,128)S(1)} %bitcast.22, bf16[32,16,1536]{2,1,0:T(8,128)(2,1)S(1)} %bitcast.17, bf16[32,16,1536]{2,1,0:T(8,128)(2,1)} %collective-permute-done.other_ref), custom_call_target="tpu_custom_call" | custom-call | tf_op jit(solution)/shard_map/pallas_call | solution.py:440
  68.1 10.4 %all-to-all-start.2 = ((bf16[8,32,512]{2,1,0:T(8,128)(2,1)}), bf16[8,32,512]{2,1,0:T(8,128)(2,1)S(1)}, u32[]{:S(2)}, u32[]{:S(2)}) async-start(bf16[8,32,512]{2,1,0:T(8,128)(2,1)} %bitcast.7), calls=%async_computation.2 | async-start | bytes 524288 | tf_op jit(solution)/shard_map/all_to_all | solution.py:451
  78.5 0.7 shard_map.184
  79.2 3.4 %collective-permute-start.1 = (bf16[32,1024]{1,0:T(8,128)(2,1)S(1)}, bf16[32,1024]{1,0:T(8,128)(2,1)S(1)}, u32[]{:S(2)}, u32[]{:S(2)}) collective-permute-start(bf16[32,1024]{1,0:T(8,128)(2,1)S(1)} %get-tuple-element.25), channel_id=1, source_target_pairs={{0,1},{1,2},{2,3},{3,4},{4,5},{5,6},{6,7},{7,0},{8,9},{9,10},{10,1... | collective-permute-start | bytes 196616 | tf_op jit(solution)/shard_map/ppermute | solution.py:435
  82.6 4.0 %collective-permute-start.2 = (bf16[32,1024]{1,0:T(8,128)(2,1)S(1)}, bf16[32,1024]{1,0:T(8,128)(2,1)S(1)}, u32[]{:S(2)}, u32[]{:S(2)}) collective-permute-start(bf16[32,1024]{1,0:T(8,128)(2,1)S(1)} %get-tuple-element.26), channel_id=1, source_target_pairs={{0,2},{1,3},{2,4},{3,5},{4,6},{5,7},{6,0},{7,1},{8,10},{9,11},{10,... | collective-permute-start | bytes 196616 | tf_op jit(solution)/shard_map/ppermute | solution.py:435
  86.6 4.3 %collective-permute-start.3 = (bf16[32,1024]{1,0:T(8,128)(2,1)S(1)}, bf16[32,1024]{1,0:T(8,128)(2,1)S(1)}, u32[]{:S(2)}, u32[]{:S(2)}) collective-permute-start(bf16[32,1024]{1,0:T(8,128)(2,1)S(1)} %get-tuple-element.27), channel_id=1, source_target_pairs={{0,3},{1,4},{2,5},{3,6},{4,7},{5,0},{6,1},{7,2},{8,11},{9,12},{10,... | collective-permute-start | bytes 196616 | tf_op jit(solution)/shard_map/ppermute | solution.py:435
  90.9 4.0 %collective-permute-start.4 = (bf16[32,1024]{1,0:T(8,128)(2,1)S(1)}, bf16[32,1024]{1,0:T(8,128)(2,1)S(1)}, u32[]{:S(2)}, u32[]{:S(2)}) collective-permute-start(bf16[32,1024]{1,0:T(8,128)(2,1)S(1)} %get-tuple-element.28), channel_id=1, source_target_pairs={{0,4},{1,5},{2,6},{3,7},{4,0},{5,1},{6,2},{7,3},{8,12},{9,13},{10,... | collective-permute-start | bytes 196616 | tf_op jit(solution)/shard_map/ppermute | solution.py:435
  94.9 4.3 %collective-permute-start.5 = (bf16[32,1024]{1,0:T(8,128)(2,1)S(1)}, bf16[32,1024]{1,0:T(8,128)(2,1)S(1)}, u32[]{:S(2)}, u32[]{:S(2)}) collective-permute-start(bf16[32,1024]{1,0:T(8,128)(2,1)S(1)} %get-tuple-element.29), channel_id=1, source_target_pairs={{0,5},{1,6},{2,7},{3,0},{4,1},{5,2},{6,3},{7,4},{8,13},{9,14},{10,... | collective-permute-start | bytes 196616 | tf_op jit(solution)/shard_map/ppermute | solution.py:435
  99.2 0.0 collective-permute-done.1.rest_0_
  99.2 5.2 %collective-permute-start.6 = (bf16[32,1024]{1,0:T(8,128)(2,1)S(1)}, bf16[32,1024]{1,0:T(8,128)(2,1)S(1)}, u32[]{:S(2)}, u32[]{:S(2)}) collective-permute-start(bf16[32,1024]{1,0:T(8,128)(2,1)S(1)} %get-tuple-element.30), channel_id=1, source_target_pairs={{0,6},{1,7},{2,0},{3,1},{4,2},{5,3},{6,4},{7,5},{8,14},{9,15},{10,... | collective-permute-start | bytes 196616 | tf_op jit(solution)/shard_map/ppermute | solution.py:435
  104.4 0.0 collective-permute-done.2.rest_1_
  104.4 3.1 %collective-permute-start.7 = (bf16[32,1024]{1,0:T(8,128)(2,1)S(1)}, bf16[32,1024]{1,0:T(8,128)(2,1)S(1)}, u32[]{:S(2)}, u32[]{:S(2)}) collective-permute-start(bf16[32,1024]{1,0:T(8,128)(2,1)S(1)} %get-tuple-element.31), channel_id=1, source_target_pairs={{0,7},{1,0},{2,1},{3,2},{4,3},{5,4},{6,5},{7,6},{8,15},{9,8},{10,9... | collective-permute-start | bytes 196616 | tf_op jit(solution)/shard_map/ppermute | solution.py:435
  107.5 0.0 collective-permute-done.3.rest_2_
  107.5 0.0 collective-permute-done.4.rest_3_
  107.5 0.0 collective-permute-done.5.rest_4_
  107.5 1.5 collective-permute-done.6.rest_5_
  109.1 1.1 collective-permute-done.7.rest_6_
  110.2 0.0 all-to-all-done.2
  110.2 0.0 all-gather.3.cloned.1.call-done
  110.2 0.0 copy-done.2
  110.2 0.0 copy-start.4
  110.2 0.0 copy-start.5
  110.2 10.2 %shard_map.185 = (bf16[256,1024]{1,0:T(8,128)(2,1)}, f32[8,8,128]{2,1,0:T(8,128)S(1)}) custom-call(s32[1]{0:T(128)} %bitcast.frame_ref, bf16[256,512]{1,0:T(8,128)(2,1)S(1)} %bitcast.21, f32[1,1024]{1,0:T(1,128)S(1)} %bitcast.23, bf16[8,2,4,16,3328]{4,3,2,1,0:T(8,128)(2,1)} %bitcast.25, bf16[8,32,1024]{2,1,0:T(8,128)(2,1)S(1)} %bitcast.20, ...), custom_call_target="tpu_custom_call" | custom-call | tf_op jit(solution)/shard_map/pallas_call | solution.py:452
  120.4 10.9 %all_to_all.25.parts_ref = f32[8,8,128]{2,1,0:T(8,128)S(1)} all-to-all(f32[8,8,128]{2,1,0:T(8,128)S(1)} %get-tuple-element.33), channel_id=1, replica_groups=mesh['dp'=64,'frame'=8] {'frame'}, dimensions={0} | all-to-all | bytes 65536 | tf_op jit(solution)/shard_map/all_to_all | solution.py:471
  131.3 0.7 shard_map.186
  132.1 11.3 %all-to-all-start.4 = ((f32[64,8,128]{2,1,0:T(8,128)}), f32[64,8,128]{2,1,0:T(8,128)S(1)}, u32[]{:S(2)}, u32[]{:S(2)}) async-start(f32[64,8,128]{2,1,0:T(8,128)} %shard_map.186), calls=%async_computation.4 | async-start | bytes 524288 | tf_op jit(solution)/shard_map/all_to_all | solution.py:473
  143.4 0.0 copy-done.4
  143.4 0.0 copy-done.5
  143.4 0.1 copy.20.pairs_ref
  144.2 0.0 copy-start.3
  144.2 4.2 %shard_map.187 = (f32[64,768]{1,0:T(8,128)S(1)}, f32[64,768]{1,0:T(8,128)S(1)}, bf16[768,768]{1,0:T(8,128)(2,1)S(1)}) custom-call(f32[1,768]{1,0:T(1,128)S(1)} %reshape.76.gain_ref.gain_text_ref, bf16[8,2,4,16,3328]{4,3,2,1,0:T(8,128)(2,1)} %bitcast.26), custom_call_target="tpu_custom_call" | custom-call | tf_op jit(solution)/shard_map/pallas_call | solution.py:465
  148.4 0.0 all-gather.5.cloned.1.call-done
  148.5 6.9 %all-to-all-done.4.pooled_ref = f32[64,8,128]{2,1,0:T(8,128)S(1)} async-done(((f32[64,8,128]{2,1,0:T(8,128)}), f32[64,8,128]{2,1,0:T(8,128)S(1)}, u32[]{:S(2)}, u32[]{:S(2)}) %all-to-all-start.4) | async-done | bytes 262176 | tf_op jit(solution)/shard_map/all_to_all | solution.py:473
  155.4 0.0 copy-done.3
  155.4 4.8 %shard_map.188 = (f32[1]{0:T(128)}, f32[1]{0:T(128)}, f32[1,1024]{1,0:T(1,128)}, f32[1,768]{1,0:T(1,128)}) custom-call(s32[1]{0:T(128)} %bitcast.1.place_ref, f32[1]{0:T(128)S(6)} %copy.21.scale_ref, s32[64,1]{1,0:T(8,128)S(1)} %copy.20.pairs_ref, f32[64,8,128]{2,1,0:T(8,128)S(1)} %all-to-all-done.4.pooled_ref, ...), custom_call_target="tpu_custom_call" | custom-call | tf_op jit(solution)/shard_map/pallas_call | solution.py:474
  (1 shorter events, 0.0 us)
Async XLA Ops:
  8.7 21.7 %all-to-all-start = ((bf16[8,16,1536]{2,1,0:T(8,128)(2,1)}), bf16[8,16,1536]{2,1,0:T(8,128)(2,1)S(1)}, u32[]{:S(2)}, u32[]{:S(2)}) async-start(bf16[8,16,1536]{2,1,0:T(8,128)(2,1)} %broadcast_in_dim.6), calls=%async_computation | async-start | bytes 786432 | tf_op jit(solution)/shard_map/all_to_all | solution.py:371
  16.4 93.8 %all-gather.3.cloned.1.call-start = ((), (), s32[]{:S(2)}) async-start(), calls=%async_computation.5 | async-start | bytes 7241728 | tf_op jit(solution)/shard_map/all_gather | solution.py:423
  32.5 31.1 %copy-start = (bf16[1,1,256,1024]{3,2,1,0:T(8,128)(2,1)S(1)}, bf16[1,1,256,1024]{3,2,1,0:T(8,128)(2,1)}, u32[]{:S(2)}) copy-start(bf16[1,1,256,1024]{3,2,1,0:T(8,128)(2,1)} %param.15) | copy-start | bytes 1572868
  32.5 31.1 %copy-start.1 = (f32[1024]{0:T(1024)S(1)}, f32[1024]{0:T(1024)}, u32[]{:S(2)}) copy-start(f32[1024]{0:T(1024)} %param.20) | copy-start | bytes 12292
  32.5 21.0 %all-to-all-start.1 = ((bf16[4,128,1536]{2,1,0:T(8,128)(2,1)}), bf16[4,128,1536]{2,1,0:T(8,128)(2,1)S(1)}, u32[]{:S(2)}, u32[]{:S(2)}) async-start(bf16[4,128,1536]{2,1,0:T(8,128)(2,1)} %broadcast_in_dim.15), calls=%async_computation.1 | async-start | bytes 3145728 | tf_op jit(solution)/shard_map/all_to_all | solution.py:371
  36.9 111.6 %all-gather.5.cloned.1.call-start = ((), (), s32[]{:S(2)}) async-start(), calls=%async_computation.6 | async-start | bytes 1671168 | tf_op jit(solution)/shard_map/all_gather | solution.py:426
  53.5 10.1 %collective-permute-start = (bf16[32,16,1536]{2,1,0:T(8,128)(2,1)S(1)}, bf16[32,16,1536]{2,1,0:T(8,128)(2,1)}, u32[]{:S(2)}, u32[]{:S(2)}) collective-permute-start(bf16[32,16,1536]{2,1,0:T(8,128)(2,1)S(1)} %bitcast.16), channel_id=1, source_target_pairs={{0,8},{8,0},{16,24},{24,16},{32,40},{40,32},{48,56},{56,48},{64,72... | collective-permute-start | bytes 4718600 | tf_op jit(solution)/shard_map/ppermute | solution.py:438
  63.6 46.6 %copy-start.2 = (f32[1024]{0:T(1024)S(1)}, f32[1024]{0:T(1024)}, u32[]{:S(2)}) copy-start(f32[1024]{0:T(1024)} %param.21) | copy-start | bytes 12292
  68.1 42.0 %all-to-all-start.2 = ((bf16[8,32,512]{2,1,0:T(8,128)(2,1)}), bf16[8,32,512]{2,1,0:T(8,128)(2,1)S(1)}, u32[]{:S(2)}, u32[]{:S(2)}) async-start(bf16[8,32,512]{2,1,0:T(8,128)(2,1)} %bitcast.7), calls=%async_computation.2 | async-start | bytes 524288 | tf_op jit(solution)/shard_map/all_to_all | solution.py:451
  79.2 20.0 %collective-permute-start.1 = (bf16[32,1024]{1,0:T(8,128)(2,1)S(1)}, bf16[32,1024]{1,0:T(8,128)(2,1)S(1)}, u32[]{:S(2)}, u32[]{:S(2)}) collective-permute-start(bf16[32,1024]{1,0:T(8,128)(2,1)S(1)} %get-tuple-element.25), channel_id=1, source_target_pairs={{0,1},{1,2},{2,3},{3,4},{4,5},{5,6},{6,7},{7,0},{8,9},{9,10},{10,1... | collective-permute-start | bytes 196616 | tf_op jit(solution)/shard_map/ppermute | solution.py:435
  82.6 21.8 %collective-permute-start.2 = (bf16[32,1024]{1,0:T(8,128)(2,1)S(1)}, bf16[32,1024]{1,0:T(8,128)(2,1)S(1)}, u32[]{:S(2)}, u32[]{:S(2)}) collective-permute-start(bf16[32,1024]{1,0:T(8,128)(2,1)S(1)} %get-tuple-element.26), channel_id=1, source_target_pairs={{0,2},{1,3},{2,4},{3,5},{4,6},{5,7},{6,0},{7,1},{8,10},{9,11},{10,... | collective-permute-start | bytes 196616 | tf_op jit(solution)/shard_map/ppermute | solution.py:435
  86.6 20.9 %collective-permute-start.3 = (bf16[32,1024]{1,0:T(8,128)(2,1)S(1)}, bf16[32,1024]{1,0:T(8,128)(2,1)S(1)}, u32[]{:S(2)}, u32[]{:S(2)}) collective-permute-start(bf16[32,1024]{1,0:T(8,128)(2,1)S(1)} %get-tuple-element.27), channel_id=1, source_target_pairs={{0,3},{1,4},{2,5},{3,6},{4,7},{5,0},{6,1},{7,2},{8,11},{9,12},{10,... | collective-permute-start | bytes 196616 | tf_op jit(solution)/shard_map/ppermute | solution.py:435
  90.9 16.6 %collective-permute-start.4 = (bf16[32,1024]{1,0:T(8,128)(2,1)S(1)}, bf16[32,1024]{1,0:T(8,128)(2,1)S(1)}, u32[]{:S(2)}, u32[]{:S(2)}) collective-permute-start(bf16[32,1024]{1,0:T(8,128)(2,1)S(1)} %get-tuple-element.28), channel_id=1, source_target_pairs={{0,4},{1,5},{2,6},{3,7},{4,0},{5,1},{6,2},{7,3},{8,12},{9,13},{10,... | collective-permute-start | bytes 196616 | tf_op jit(solution)/shard_map/ppermute | solution.py:435
  94.9 12.7 %collective-permute-start.5 = (bf16[32,1024]{1,0:T(8,128)(2,1)S(1)}, bf16[32,1024]{1,0:T(8,128)(2,1)S(1)}, u32[]{:S(2)}, u32[]{:S(2)}) collective-permute-start(bf16[32,1024]{1,0:T(8,128)(2,1)S(1)} %get-tuple-element.29), channel_id=1, source_target_pairs={{0,5},{1,6},{2,7},{3,0},{4,1},{5,2},{6,3},{7,4},{8,13},{9,14},{10,... | collective-permute-start | bytes 196616 | tf_op jit(solution)/shard_map/ppermute | solution.py:435
  99.2 9.9 %collective-permute-start.6 = (bf16[32,1024]{1,0:T(8,128)(2,1)S(1)}, bf16[32,1024]{1,0:T(8,128)(2,1)S(1)}, u32[]{:S(2)}, u32[]{:S(2)}) collective-permute-start(bf16[32,1024]{1,0:T(8,128)(2,1)S(1)} %get-tuple-element.30), channel_id=1, source_target_pairs={{0,6},{1,7},{2,0},{3,1},{4,2},{5,3},{6,4},{7,5},{8,14},{9,15},{10,... | collective-permute-start | bytes 196616 | tf_op jit(solution)/shard_map/ppermute | solution.py:435
  104.4 5.7 %collective-permute-start.7 = (bf16[32,1024]{1,0:T(8,128)(2,1)S(1)}, bf16[32,1024]{1,0:T(8,128)(2,1)S(1)}, u32[]{:S(2)}, u32[]{:S(2)}) collective-permute-start(bf16[32,1024]{1,0:T(8,128)(2,1)S(1)} %get-tuple-element.31), channel_id=1, source_target_pairs={{0,7},{1,0},{2,1},{3,2},{4,3},{5,4},{6,5},{7,6},{8,15},{9,8},{10,9... | collective-permute-start | bytes 196616 | tf_op jit(solution)/shard_map/ppermute | solution.py:435
  110.2 33.2 %copy-start.4 = (f32[768]{0:T(1024)S(1)}, f32[768]{0:T(1024)}, u32[]{:S(2)}) copy-start(f32[768]{0:T(1024)} %param.23) | copy-start | bytes 9220
  110.2 33.3 %copy-start.5 = (s32[64]{0:T(128)S(1)}, s32[64]{0:T(128)}, u32[]{:S(2)}) copy-start(s32[64]{0:T(128)} %param.18) | copy-start | bytes 772
  132.1 23.3 %all-to-all-start.4 = ((f32[64,8,128]{2,1,0:T(8,128)}), f32[64,8,128]{2,1,0:T(8,128)S(1)}, u32[]{:S(2)}, u32[]{:S(2)}) async-start(f32[64,8,128]{2,1,0:T(8,128)} %shard_map.186), calls=%async_computation.4 | async-start | bytes 524288 | tf_op jit(solution)/shard_map/all_to_all | solution.py:473
  144.2 11.2 %copy-start.3 = (f32[1024]{0:T(1024)S(1)}, f32[1024]{0:T(1024)}, u32[]{:S(2)}) copy-start(f32[1024]{0:T(1024)} %param.22) | copy-start | bytes 12292
Sparse Core Ops, SparseCore 0:
  31.3 57.6 all-gather.2
  91.1 40.4 all-gather.4

commit v4 on v3

--- a/solution.py
+++ b/solution.py
@@ -84,32 +84,12 @@
     return jnp.where(low, mixed[0], mixed[1]).astype(BF16)
 
 
-def attend(packed_ref, mixed_ref):
+def attend(packed_ref, mixed_ref, mask):
     for at in range(0, WIDTH, 2 * HD):
         query, key, value = (
             packed_ref[:, part * WIDTH + at : part * WIDTH + at + 2 * HD] for part in range(3)
         )
-        mixed_ref[:, at : at + 2 * HD] = attend_pair(query, key, value, None)
-
-
-def attend_frames(packed_ref, mixed_ref):
-    frames, patches, _ = packed_ref.shape
-    block = 16
-    rows = frames * block
-    place = lax.broadcasted_iota(jnp.int32, (rows, rows), 0) % block
-    mask = place == lax.broadcasted_iota(jnp.int32, (rows, rows), 1) % block
-    for first in range(0, patches, block):
-        for at in range(0, WIDTH, 2 * HD):
-            query, key, value = (
-                packed_ref[
-                    :, first : first + block, part * WIDTH + at : part * WIDTH + at + 2 * HD
-                ].reshape(rows, 2 * HD)
-                for part in range(3)
-            )
-            mixed = attend_pair(query, key, value, mask)
-            mixed_ref[:, first : first + block, at : at + 2 * HD] = mixed.reshape(
-                frames, block, 2 * HD
-            )
+        mixed_ref[:, at : at + 2 * HD] = attend_pair(query, key, value, mask)
 
 
 def spatial_kernel(
@@ -127,7 +107,7 @@
     copy_own.wait()
     copy_other.wait()
     packed[...] = dot(normed, qkv[...].reshape(D, 3 * WIDTH)).astype(BF16)
-    attend(packed, mixed_ref)
+    attend(packed, mixed_ref, None)
 
 
 def gather_rows(weights_ref, first, target, sems):
@@ -214,10 +194,11 @@
     normed = layer_norm(spatial.astype(F32), gain_ref[...]).astype(BF16)
     for copy in copies_qkv:
         copy.wait()
-    projected = dot(normed, qkv[...].reshape(D, 3 * WIDTH)).astype(BF16)
-    packed[...] = projected.reshape(packed.shape)
-    attend_frames(packed, mixed)
-    output = spatial.astype(F32) + dot(mixed[...].reshape(rows, WIDTH), out_temporal)
+    packed[...] = dot(normed, qkv[...].reshape(D, 3 * WIDTH)).astype(BF16)
+    patches = tokens.shape[1]
+    place = lax.broadcasted_iota(jnp.int32, (rows, rows), 0) % patches
+    attend(packed, mixed, place == lax.broadcasted_iota(jnp.int32, (rows, rows), 1) % patches)
+    output = spatial.astype(F32) + dot(mixed[...], out_temporal)
     output = output.astype(BF16)
     out_ref[...] = output
     total = jnp.sum(output.astype(F32), axis=0, keepdims=True)
@@ -435,6 +416,7 @@
         lax.ppermute(block, "frame", [(i, (i + 1 + step) % FRAMES) for i in range(FRAMES)])
         for step, block in enumerate(dealt)
     ]
+    own, dealt[:4] = lax.optimization_barrier((own, dealt[:4]))
     other = lax.ppermute(own, "dp", OTHER_CORE)
 
     mixed = call(
@@ -457,8 +439,8 @@
             pltpu.VMEM((FRAMES, 32, D), BF16),
             pltpu.VMEM(halves + (3 * WIDTH,), BF16),
             pltpu.VMEM(halves + (D,), BF16),
-            pltpu.VMEM((FRAMES, 32, 3 * WIDTH), BF16),
-            pltpu.VMEM((FRAMES, 32, WIDTH), BF16),
+            pltpu.VMEM((256, 3 * WIDTH), BF16),
+            pltpu.VMEM((256, WIDTH), BF16),
             DMA((3, 2 * Y)),
         ],
     )(frame, mixed.reshape(256, WIDTH), gain_temporal.reshape(1, D), early, dealing, *dealt)

time: 168 us -> 155 us (0.923)
  waiting for transfers between devices: 28.7 us -> 22 us
  starting transfers between devices: 68.9 us -> 65.1 us
  Pallas kernels: 27.3 us -> 23.7 us
    all_to_all x2, waiting for transfers between devices: 15.9 us -> 0.01 us  [send_all(): lax.all_to_all(copies, 'dp', 0, 0, tiled=True, axis_index_groups=groups)]
    ppermute x7, waiting for transfers between devices: 2.62 us -> 11.8 us  [on_device(): lax.ppermute(block, 'frame', [(i, (i + 1 + step) % FRAMES) for i in range...]
    all_to_all x1, starting transfers between devices: 10.4 us -> 3.42 us  [on_device(): lax.all_to_all(mixed.reshape(8, 32, WIDTH), 'frame', 0, 0, tiled=True)]
    pallas_call x1, Pallas kernels: 10.2 us -> 6.58 us  [on_device(): call(temporal_kernel, (shape((256, D), BF16), shape((FRAMES, 8, 128), F32...]
    ppermute x7, starting transfers between devices: 28.2 us -> 31.2 us  [on_device(): lax.ppermute(block, 'frame', [(i, (i + 1 + step) % FRAMES) for i in range...]
    all_to_all x1, starting transfers between devices: 11.3 us -> 13.1 us  [on_device(): pooled = lax.all_to_all(pool, 'dp', 0, 0, tiled=True)]
  transfers between devices with their start and end apart: 14 -> 14, of which waited for: 5 -> 5; matrix products, arithmetic and copies ran while one was open for 1% -> 1% of each run, Pallas kernels for 13% -> 12%
where the time goes in v4:
time: 155 us; the launch traced here: 154 us
  starting transfers between devices  65.1 us (42%)
  blocking collectives  24.1 us (16%)
  Pallas kernels  23.7 us (15%)
  waiting for transfers between devices  22 us (14%)
  between operations  14.9 us (10%)
  local copies, waits for them, and re-layouts  4.44 us (3%)
    ppermute x7, starting transfers between devices, on_device(): lax.ppermute(block, 'frame', [(i, (i + 1 + step) % FRAMES) for i in range...  31.2 us
    all_to_all x1, starting transfers between devices, on_device(): pooled = lax.all_to_all(pool, 'dp', 0, 0, tiled=True)  13.1 us
    all_to_all x1, blocking collectives, on_device(): pool = lax.all_to_all(pool, 'frame', 0, 0, tiled=True)  12.2 us
    all_to_all x2, starting transfers between devices, send_all(): lax.all_to_all(copies, 'dp', 0, 0, tiled=True, axis_index_groups=groups)  12 us
    all_gather x1, blocking collectives, on_device(): lax.all_gather(packed, 'dp', axis=0, tiled=True, axis_index_groups=ROWS_O...  11.9 us
    ppermute x7, waiting for transfers between devices, on_device(): lax.ppermute(block, 'frame', [(i, (i + 1 + step) % FRAMES) for i in range...  11.8 us
    all_to_all x1, waiting for transfers between devices, on_device(): pooled = lax.all_to_all(pool, 'dp', 0, 0, tiled=True)  6.94 us
    pallas_call x1, Pallas kernels, on_device(): call(temporal_kernel, (shape((256, D), BF16), shape((FRAMES, 8, 128), F32...  6.58 us
  transfers between devices with their start and end apart: 14, of which 5 were waited for; matrix products, arithmetic and copies ran while one was open for 1% of the time, Pallas kernels for 12%

profile of v4, /device:TPU:1, one launch (start us, length us, event | category | flops | bytes accessed | tf_op | source)
XLA Modules:
  0.0 154.3 jit_solution(16208125267271554598)
XLA Ops:
  7.2 1.6 %broadcast_in_dim.6 = bf16[8,16,1536]{2,1,0:T(8,128)(2,1)} broadcast(bf16[16,1536]{1,0:T(8,128)(2,1)} %param.24), dimensions={1,2} | broadcast | bytes 442368 | tf_op jit(solution)/shard_map/broadcast_in_dim | solution.py:351
  8.7 7.7 %all-to-all-start = ((bf16[8,16,1536]{2,1,0:T(8,128)(2,1)}), bf16[8,16,1536]{2,1,0:T(8,128)(2,1)S(1)}, u32[]{:S(2)}, u32[]{:S(2)}) async-start(bf16[8,16,1536]{2,1,0:T(8,128)(2,1)} %broadcast_in_dim.6), calls=%async_computation | async-start | bytes 786432 | tf_op jit(solution)/shard_map/all_to_all | solution.py:352
  16.4 0.0 all-gather.3.cloned.1.call-start
  16.4 2.1 %shard_map.182 = bf16[16,4096]{1,0:T(8,128)(2,1)} custom-call(s32[1,77]{1,0:T(1,128)} %ids_ref.1, bf16[77,768]{1,0:T(8,128)(2,1)} %bitcast.29, bf16[16,1536]{1,0:T(8,128)(2,1)} %qkv_ref.1, bf16[12,768]{1,0:T(8,128)(2,1)} %text_ref.1, bf16[8,1024]{1,0:T(8,128)(2,1)} %out_s_ref.1, bf16[8,1024]{1,0:T(8,128)(2,1)} %out_t_ref.1, bf16[16,768]{1,0:T(8,128)(2,1)} %video_ref.1), custom_call_target="tpu_custom_call" | custom-call | tf_op jit(solution)/shard_map/pallas_call | solution.py:379
  18.5 11.9 %all_gather.9 = bf16[64,4096]{1,0:T(8,128)(2,1)S(1)} all-gather(bf16[16,4096]{1,0:T(8,128)(2,1)} %shard_map.182), channel_id=1, replica_groups={{0,128,256,384},{8,136,264,392},{16,144,272,400},{24,152,280,408},{32,1..., dimensions={0}, use_global_device_ids=true | all-gather | bytes 655360 | tf_op jit(solution)/shard_map/all_gather | solution.py:402
  30.4 0.0 all-to-all-done
  30.4 0.8 slice.6
  31.2 0.0 all-gather.3.cloned.1.call-update
  31.2 1.3 broadcast_in_dim.15
  32.5 0.0 copy-start
  32.5 0.0 copy-start.1
  32.5 4.3 %all-to-all-start.1 = ((bf16[4,128,1536]{2,1,0:T(8,128)(2,1)}), bf16[4,128,1536]{2,1,0:T(8,128)(2,1)S(1)}, u32[]{:S(2)}, u32[]{:S(2)}) async-start(bf16[4,128,1536]{2,1,0:T(8,128)(2,1)} %broadcast_in_dim.15), calls=%async_computation.1 | async-start | bytes 3145728 | tf_op jit(solution)/shard_map/all_to_all | solution.py:352
  36.9 0.0 all-gather.5.cloned.1.call-start
  36.9 0.6 slice.7
  37.5 0.1 all-gather.5.cloned.1.call-update
  37.6 0.0 copy-done
  37.6 0.7 shard_map.183
  38.3 4.0 %collective-permute-start = (bf16[32,1024]{1,0:T(8,128)(2,1)S(1)}, bf16[32,1024]{1,0:T(8,128)(2,1)S(1)}, u32[]{:S(2)}, u32[]{:S(2)}) collective-permute-start(bf16[32,1024]{1,0:T(8,128)(2,1)S(1)} %get-tuple-element.29), channel_id=1, source_target_pairs={{0,1},{1,2},{2,3},{3,4},{4,5},{5,6},{6,7},{7,0},{8,9},{9,10},{10,1... | collective-permute-start | bytes 196616 | tf_op jit(solution)/shard_map/ppermute | solution.py:416
  42.3 5.8 %collective-permute-start.1 = (bf16[32,1024]{1,0:T(8,128)(2,1)S(1)}, bf16[32,1024]{1,0:T(8,128)(2,1)S(1)}, u32[]{:S(2)}, u32[]{:S(2)}) collective-permute-start(bf16[32,1024]{1,0:T(8,128)(2,1)S(1)} %get-tuple-element.30), channel_id=1, source_target_pairs={{0,2},{1,3},{2,4},{3,5},{4,6},{5,7},{6,0},{7,1},{8,10},{9,11},{10,... | collective-permute-start | bytes 196616 | tf_op jit(solution)/shard_map/ppermute | solution.py:416
  48.1 7.0 %collective-permute-start.2 = (bf16[32,1024]{1,0:T(8,128)(2,1)S(1)}, bf16[32,1024]{1,0:T(8,128)(2,1)S(1)}, u32[]{:S(2)}, u32[]{:S(2)}) collective-permute-start(bf16[32,1024]{1,0:T(8,128)(2,1)S(1)} %get-tuple-element.31), channel_id=1, source_target_pairs={{0,3},{1,4},{2,5},{3,6},{4,7},{5,0},{6,1},{7,2},{8,11},{9,12},{10,... | collective-permute-start | bytes 196616 | tf_op jit(solution)/shard_map/ppermute | solution.py:416
  55.2 2.8 %collective-permute-start.3 = (bf16[32,1024]{1,0:T(8,128)(2,1)S(1)}, bf16[32,1024]{1,0:T(8,128)(2,1)S(1)}, u32[]{:S(2)}, u32[]{:S(2)}) collective-permute-start(bf16[32,1024]{1,0:T(8,128)(2,1)S(1)} %get-tuple-element.32), channel_id=1, source_target_pairs={{0,4},{1,5},{2,6},{3,7},{4,0},{5,1},{6,2},{7,3},{8,12},{9,13},{10,... | collective-permute-start | bytes 196616 | tf_op jit(solution)/shard_map/ppermute | solution.py:416
  58.0 0.0 collective-permute-done.rest_0_
  58.0 0.0 collective-permute-done.1.rest_1_
  58.0 0.0 collective-permute-done.2.rest_2_
  58.0 7.1 %collective-permute-done.3.rest_3_ = bf16[32,1024]{1,0:T(8,128)(2,1)S(1)} collective-permute-done((bf16[32,1024]{1,0:T(8,128)(2,1)S(1)}, bf16[32,1024]{1,0:T(8,128)(2,1)S(1)}, u32[]{:S(2)}, u32[]{:S(2)}) %collective-permute-start.3) | collective-permute-done | bytes 65568 | tf_op jit(solution)/shard_map/ppermute | solution.py:416
  65.2 0.0 all-to-all-done.1
  65.2 5.3 %collective-permute-start.4 = (bf16[32,16,1536]{2,1,0:T(8,128)(2,1)S(1)}, bf16[32,16,1536]{2,1,0:T(8,128)(2,1)}, u32[]{:S(2)}, u32[]{:S(2)}) collective-permute-start(bf16[32,16,1536]{2,1,0:T(8,128)(2,1)S(1)} %bitcast.16), channel_id=1, source_target_pairs={{0,8},{8,0},{16,24},{24,16},{32,40},{40,32},{48,56},{56,48},{64,72... | collective-permute-start | bytes 4718600 | tf_op jit(solution)/shard_map/ppermute | solution.py:420
  70.5 3.1 %collective-permute-done.4.other_ref = bf16[32,16,1536]{2,1,0:T(8,128)(2,1)} collective-permute-done((bf16[32,16,1536]{2,1,0:T(8,128)(2,1)S(1)}, bf16[32,16,1536]{2,1,0:T(8,128)(2,1)}, u32[]{:S(2)}, u32[]{:S(2)}) %collective-permute-start.4) | collective-permute-done | bytes 1572896 | tf_op jit(solution)/shard_map/ppermute | solution.py:420
  73.6 0.0 copy-done.1
  73.6 0.0 copy-start.2
  73.6 4.6 %shard_map.184 = bf16[256,512]{1,0:T(8,128)(2,1)} custom-call(s32[1]{0:T(128)S(6)} %select_n.7.core_ref, bf16[256,1024]{1,0:T(8,128)(2,1)S(1)} %bitcast.19, f32[1,1024]{1,0:T(1,128)S(1)} %bitcast.22, bf16[32,16,1536]{2,1,0:T(8,128)(2,1)S(1)} %bitcast.17, bf16[32,16,1536]{2,1,0:T(8,128)(2,1)} %collective-permute-done.4.other_ref), custom_call_target="tpu_custom_call" | custom-call | tf_op jit(solution)/shard_map/pallas_call | solution.py:422
  78.2 3.4 %all-to-all-start.2 = ((bf16[8,32,512]{2,1,0:T(8,128)(2,1)}), bf16[8,32,512]{2,1,0:T(8,128)(2,1)S(1)}, u32[]{:S(2)}, u32[]{:S(2)}) async-start(bf16[8,32,512]{2,1,0:T(8,128)(2,1)} %bitcast.8), calls=%async_computation.2 | async-start | bytes 524288 | tf_op jit(solution)/shard_map/all_to_all | solution.py:433
  81.7 6.3 %collective-permute-start.5 = (bf16[32,1024]{1,0:T(8,128)(2,1)S(1)}, bf16[32,1024]{1,0:T(8,128)(2,1)S(1)}, u32[]{:S(2)}, u32[]{:S(2)}) collective-permute-start(bf16[32,1024]{1,0:T(8,128)(2,1)S(1)} %get-tuple-element.39), channel_id=1, source_target_pairs={{0,5},{1,6},{2,7},{3,0},{4,1},{5,2},{6,3},{7,4},{8,13},{9,14},{10,... | collective-permute-start | bytes 196616 | tf_op jit(solution)/shard_map/ppermute | solution.py:416
  88.0 3.1 %collective-permute-start.6 = (bf16[32,1024]{1,0:T(8,128)(2,1)S(1)}, bf16[32,1024]{1,0:T(8,128)(2,1)S(1)}, u32[]{:S(2)}, u32[]{:S(2)}) collective-permute-start(bf16[32,1024]{1,0:T(8,128)(2,1)S(1)} %get-tuple-element.40), channel_id=1, source_target_pairs={{0,6},{1,7},{2,0},{3,1},{4,2},{5,3},{6,4},{7,5},{8,14},{9,15},{10,... | collective-permute-start | bytes 196616 | tf_op jit(solution)/shard_map/ppermute | solution.py:416
  91.0 2.2 %collective-permute-start.7 = (bf16[32,1024]{1,0:T(8,128)(2,1)S(1)}, bf16[32,1024]{1,0:T(8,128)(2,1)S(1)}, u32[]{:S(2)}, u32[]{:S(2)}) collective-permute-start(bf16[32,1024]{1,0:T(8,128)(2,1)S(1)} %get-tuple-element.41), channel_id=1, source_target_pairs={{0,7},{1,0},{2,1},{3,2},{4,3},{5,4},{6,5},{7,6},{8,15},{9,8},{10,9... | collective-permute-start | bytes 196616 | tf_op jit(solution)/shard_map/ppermute | solution.py:416
  93.2 0.0 collective-permute-done.5.rest_4_
  93.2 3.6 %collective-permute-done.6.rest_5_ = bf16[32,1024]{1,0:T(8,128)(2,1)S(1)} collective-permute-done((bf16[32,1024]{1,0:T(8,128)(2,1)S(1)}, bf16[32,1024]{1,0:T(8,128)(2,1)S(1)}, u32[]{:S(2)}, u32[]{:S(2)}) %collective-permute-start.6) | collective-permute-done | bytes 65568 | tf_op jit(solution)/shard_map/ppermute | solution.py:416
  96.9 1.1 collective-permute-done.7.rest_6_
  97.9 0.0 all-to-all-done.2
  97.9 0.0 all-gather.3.cloned.1.call-done
  97.9 0.0 copy-done.2
  97.9 0.0 copy-start.4
  98.0 0.0 copy-start.5
  98.0 6.6 %shard_map.185 = (bf16[256,1024]{1,0:T(8,128)(2,1)}, f32[8,8,128]{2,1,0:T(8,128)S(1)}) custom-call(s32[1]{0:T(128)} %bitcast.frame_ref, bf16[256,512]{1,0:T(8,128)(2,1)S(1)} %bitcast.21, f32[1,1024]{1,0:T(1,128)S(1)} %bitcast.23, bf16[8,2,4,16,3328]{4,3,2,1,0:T(8,128)(2,1)} %bitcast.25, bf16[8,32,1024]{2,1,0:T(8,128)(2,1)S(1)} %bitcast.20, ...), custom_call_target="tpu_custom_call" | custom-call | tf_op jit(solution)/shard_map/pallas_call | solution.py:434
  104.6 12.2 %all_to_all.25.parts_ref = f32[8,8,128]{2,1,0:T(8,128)S(1)} all-to-all(f32[8,8,128]{2,1,0:T(8,128)S(1)} %get-tuple-element.43), channel_id=1, replica_groups=mesh['dp'=64,'frame'=8] {'frame'}, dimensions={0} | all-to-all | bytes 65536 | tf_op jit(solution)/shard_map/all_to_all | solution.py:453
  116.8 0.7 shard_map.186
  117.5 13.1 %all-to-all-start.4 = ((f32[64,8,128]{2,1,0:T(8,128)}), f32[64,8,128]{2,1,0:T(8,128)S(1)}, u32[]{:S(2)}, u32[]{:S(2)}) async-start(f32[64,8,128]{2,1,0:T(8,128)} %shard_map.186), calls=%async_computation.4 | async-start | bytes 524288 | tf_op jit(solution)/shard_map/all_to_all | solution.py:455
  130.7 0.0 copy-done.4
  130.7 0.0 copy-done.5
  130.7 0.1 copy.20.pairs_ref
  131.4 0.0 copy-start.3
  131.4 4.2 %shard_map.187 = (f32[64,768]{1,0:T(8,128)S(1)}, f32[64,768]{1,0:T(8,128)S(1)}, bf16[768,768]{1,0:T(8,128)(2,1)S(1)}) custom-call(f32[1,768]{1,0:T(1,128)S(1)} %reshape.76.gain_ref.gain_text_ref, bf16[8,2,4,16,3328]{4,3,2,1,0:T(8,128)(2,1)} %bitcast.26), custom_call_target="tpu_custom_call" | custom-call | tf_op jit(solution)/shard_map/pallas_call | solution.py:447
  135.7 0.0 all-gather.5.cloned.1.call-done
  135.7 6.9 %all-to-all-done.4.pooled_ref = f32[64,8,128]{2,1,0:T(8,128)S(1)} async-done(((f32[64,8,128]{2,1,0:T(8,128)}), f32[64,8,128]{2,1,0:T(8,128)S(1)}, u32[]{:S(2)}, u32[]{:S(2)}) %all-to-all-start.4) | async-done | bytes 262176 | tf_op jit(solution)/shard_map/all_to_all | solution.py:455
  142.6 0.0 copy-done.3
  142.6 4.8 %shard_map.188 = (f32[1]{0:T(128)}, f32[1]{0:T(128)}, f32[1,1024]{1,0:T(1,128)}, f32[1,768]{1,0:T(1,128)}) custom-call(s32[1]{0:T(128)} %bitcast.1.place_ref, f32[1]{0:T(128)S(6)} %copy.21.scale_ref, s32[64,1]{1,0:T(8,128)S(1)} %copy.20.pairs_ref, f32[64,8,128]{2,1,0:T(8,128)S(1)} %all-to-all-done.4.pooled_ref, ...), custom_call_target="tpu_custom_call" | custom-call | tf_op jit(solution)/shard_map/pallas_call | solution.py:456
  (1 shorter events, 0.0 us)
Async XLA Ops:
  8.7 21.7 %all-to-all-start = ((bf16[8,16,1536]{2,1,0:T(8,128)(2,1)}), bf16[8,16,1536]{2,1,0:T(8,128)(2,1)S(1)}, u32[]{:S(2)}, u32[]{:S(2)}) async-start(bf16[8,16,1536]{2,1,0:T(8,128)(2,1)} %broadcast_in_dim.6), calls=%async_computation | async-start | bytes 786432 | tf_op jit(solution)/shard_map/all_to_all | solution.py:352
  16.4 81.6 %all-gather.3.cloned.1.call-start = ((), (), s32[]{:S(2)}) async-start(), calls=%async_computation.5 | async-start | bytes 7241728 | tf_op jit(solution)/shard_map/all_gather | solution.py:404
  32.5 5.1 %copy-start = (bf16[1,1,256,1024]{3,2,1,0:T(8,128)(2,1)S(1)}, bf16[1,1,256,1024]{3,2,1,0:T(8,128)(2,1)}, u32[]{:S(2)}) copy-start(bf16[1,1,256,1024]{3,2,1,0:T(8,128)(2,1)} %param.15) | copy-start | bytes 1572868
  32.5 41.1 %copy-start.1 = (f32[1024]{0:T(1024)S(1)}, f32[1024]{0:T(1024)}, u32[]{:S(2)}) copy-start(f32[1024]{0:T(1024)} %param.20) | copy-start | bytes 12292
  32.5 32.7 %all-to-all-start.1 = ((bf16[4,128,1536]{2,1,0:T(8,128)(2,1)}), bf16[4,128,1536]{2,1,0:T(8,128)(2,1)S(1)}, u32[]{:S(2)}, u32[]{:S(2)}) async-start(bf16[4,128,1536]{2,1,0:T(8,128)(2,1)} %broadcast_in_dim.15), calls=%async_computation.1 | async-start | bytes 3145728 | tf_op jit(solution)/shard_map/all_to_all | solution.py:352
  36.9 98.8 %all-gather.5.cloned.1.call-start = ((), (), s32[]{:S(2)}) async-start(), calls=%async_computation.6 | async-start | bytes 1671168 | tf_op jit(solution)/shard_map/all_gather | solution.py:407
  38.3 19.7 %collective-permute-start = (bf16[32,1024]{1,0:T(8,128)(2,1)S(1)}, bf16[32,1024]{1,0:T(8,128)(2,1)S(1)}, u32[]{:S(2)}, u32[]{:S(2)}) collective-permute-start(bf16[32,1024]{1,0:T(8,128)(2,1)S(1)} %get-tuple-element.29), channel_id=1, source_target_pairs={{0,1},{1,2},{2,3},{3,4},{4,5},{5,6},{6,7},{7,0},{8,9},{9,10},{10,1... | collective-permute-start | bytes 196616 | tf_op jit(solution)/shard_map/ppermute | solution.py:416
  42.3 15.7 %collective-permute-start.1 = (bf16[32,1024]{1,0:T(8,128)(2,1)S(1)}, bf16[32,1024]{1,0:T(8,128)(2,1)S(1)}, u32[]{:S(2)}, u32[]{:S(2)}) collective-permute-start(bf16[32,1024]{1,0:T(8,128)(2,1)S(1)} %get-tuple-element.30), channel_id=1, source_target_pairs={{0,2},{1,3},{2,4},{3,5},{4,6},{5,7},{6,0},{7,1},{8,10},{9,11},{10,... | collective-permute-start | bytes 196616 | tf_op jit(solution)/shard_map/ppermute | solution.py:416
  48.1 9.9 %collective-permute-start.2 = (bf16[32,1024]{1,0:T(8,128)(2,1)S(1)}, bf16[32,1024]{1,0:T(8,128)(2,1)S(1)}, u32[]{:S(2)}, u32[]{:S(2)}) collective-permute-start(bf16[32,1024]{1,0:T(8,128)(2,1)S(1)} %get-tuple-element.31), channel_id=1, source_target_pairs={{0,3},{1,4},{2,5},{3,6},{4,7},{5,0},{6,1},{7,2},{8,11},{9,12},{10,... | collective-permute-start | bytes 196616 | tf_op jit(solution)/shard_map/ppermute | solution.py:416
  55.2 10.0 %collective-permute-start.3 = (bf16[32,1024]{1,0:T(8,128)(2,1)S(1)}, bf16[32,1024]{1,0:T(8,128)(2,1)S(1)}, u32[]{:S(2)}, u32[]{:S(2)}) collective-permute-start(bf16[32,1024]{1,0:T(8,128)(2,1)S(1)} %get-tuple-element.32), channel_id=1, source_target_pairs={{0,4},{1,5},{2,6},{3,7},{4,0},{5,1},{6,2},{7,3},{8,12},{9,13},{10,... | collective-permute-start | bytes 196616 | tf_op jit(solution)/shard_map/ppermute | solution.py:416
  65.2 8.4 %collective-permute-start.4 = (bf16[32,16,1536]{2,1,0:T(8,128)(2,1)S(1)}, bf16[32,16,1536]{2,1,0:T(8,128)(2,1)}, u32[]{:S(2)}, u32[]{:S(2)}) collective-permute-start(bf16[32,16,1536]{2,1,0:T(8,128)(2,1)S(1)} %bitcast.16), channel_id=1, source_target_pairs={{0,8},{8,0},{16,24},{24,16},{32,40},{40,32},{48,56},{56,48},{64,72... | collective-permute-start | bytes 4718600 | tf_op jit(solution)/shard_map/ppermute | solution.py:420
  73.6 24.3 %copy-start.2 = (f32[1024]{0:T(1024)S(1)}, f32[1024]{0:T(1024)}, u32[]{:S(2)}) copy-start(f32[1024]{0:T(1024)} %param.21) | copy-start | bytes 12292
  78.2 19.7 %all-to-all-start.2 = ((bf16[8,32,512]{2,1,0:T(8,128)(2,1)}), bf16[8,32,512]{2,1,0:T(8,128)(2,1)S(1)}, u32[]{:S(2)}, u32[]{:S(2)}) async-start(bf16[8,32,512]{2,1,0:T(8,128)(2,1)} %bitcast.8), calls=%async_computation.2 | async-start | bytes 524288 | tf_op jit(solution)/shard_map/all_to_all | solution.py:433
  81.7 11.6 %collective-permute-start.5 = (bf16[32,1024]{1,0:T(8,128)(2,1)S(1)}, bf16[32,1024]{1,0:T(8,128)(2,1)S(1)}, u32[]{:S(2)}, u32[]{:S(2)}) collective-permute-start(bf16[32,1024]{1,0:T(8,128)(2,1)S(1)} %get-tuple-element.39), channel_id=1, source_target_pairs={{0,5},{1,6},{2,7},{3,0},{4,1},{5,2},{6,3},{7,4},{8,13},{9,14},{10,... | collective-permute-start | bytes 196616 | tf_op jit(solution)/shard_map/ppermute | solution.py:416
  88.0 8.9 %collective-permute-start.6 = (bf16[32,1024]{1,0:T(8,128)(2,1)S(1)}, bf16[32,1024]{1,0:T(8,128)(2,1)S(1)}, u32[]{:S(2)}, u32[]{:S(2)}) collective-permute-start(bf16[32,1024]{1,0:T(8,128)(2,1)S(1)} %get-tuple-element.40), channel_id=1, source_target_pairs={{0,6},{1,7},{2,0},{3,1},{4,2},{5,3},{6,4},{7,5},{8,14},{9,15},{10,... | collective-permute-start | bytes 196616 | tf_op jit(solution)/shard_map/ppermute | solution.py:416
  91.0 6.9 %collective-permute-start.7 = (bf16[32,1024]{1,0:T(8,128)(2,1)S(1)}, bf16[32,1024]{1,0:T(8,128)(2,1)S(1)}, u32[]{:S(2)}, u32[]{:S(2)}) collective-permute-start(bf16[32,1024]{1,0:T(8,128)(2,1)S(1)} %get-tuple-element.41), channel_id=1, source_target_pairs={{0,7},{1,0},{2,1},{3,2},{4,3},{5,4},{6,5},{7,6},{8,15},{9,8},{10,9... | collective-permute-start | bytes 196616 | tf_op jit(solution)/shard_map/ppermute | solution.py:416
  97.9 32.7 %copy-start.4 = (f32[768]{0:T(1024)S(1)}, f32[768]{0:T(1024)}, u32[]{:S(2)}) copy-start(f32[768]{0:T(1024)} %param.23) | copy-start | bytes 9220
  98.0 32.7 %copy-start.5 = (s32[64]{0:T(128)S(1)}, s32[64]{0:T(128)}, u32[]{:S(2)}) copy-start(s32[64]{0:T(128)} %param.18) | copy-start | bytes 772
  117.5 25.1 %all-to-all-start.4 = ((f32[64,8,128]{2,1,0:T(8,128)}), f32[64,8,128]{2,1,0:T(8,128)S(1)}, u32[]{:S(2)}, u32[]{:S(2)}) async-start(f32[64,8,128]{2,1,0:T(8,128)} %shard_map.186), calls=%async_computation.4 | async-start | bytes 524288 | tf_op jit(solution)/shard_map/all_to_all | solution.py:455
  131.4 11.2 %copy-start.3 = (f32[1024]{0:T(1024)S(1)}, f32[1024]{0:T(1024)}, u32[]{:S(2)}) copy-start(f32[1024]{0:T(1024)} %param.22) | copy-start | bytes 12292
Sparse Core Ops, SparseCore 0:
  31.3 57.6 all-gather.2
  91.1 40.3 all-gather.4

commit v5 on v4

--- a/solution.py
+++ b/solution.py
@@ -25,8 +25,7 @@
 QKV_T = 0
 W_TEXT = 1536
 W_OUT = 2304
-W_VIDEO = 3328
-PACKED = 4096
+PACKED = 3328
 
 X, Y = 4, 8
 ROWS_OF_X = [[(x * Y + y) * 2 + c for x in range(X)] for y in range(Y) for c in range(2)]
@@ -122,23 +121,24 @@
 
 
 def pack_kernel(
-    ids_ref, states_ref, qkv_ref, text_ref, out_s_ref, out_t_ref, video_ref, packed_ref,
-    ids_here, states_here, text_here, out_s_here, out_t_here, sems,
+    ids_ref, states_ref, qkv_ref, text_ref, out_s_ref, out_t_ref, spatial_ref, packed_ref, copies_ref,
+    ids_here, states_here, text_here, out_s_here, out_t_here, spatial_here, sems,
 ):
     pairs = (
+        (spatial_ref, spatial_here),
         (ids_ref, ids_here),
         (states_ref, states_here),
         (text_ref, text_here),
         (out_s_ref, out_s_here),
         (out_t_ref, out_t_here),
         (qkv_ref, packed_ref.at[:, QKV_T : QKV_T + 3 * WIDTH]),
-        (video_ref, packed_ref.at[:, W_VIDEO : W_VIDEO + E]),
     )
     copies = [pltpu.make_async_copy(*pair, sems.at[i]) for i, pair in enumerate(pairs)]
     for copy in copies:
         copy.start()
     for copy in copies:
         copy.wait()
+    copies_ref[...] = jnp.broadcast_to(spatial_here[...][None], copies_ref.shape)
     ids = ids_here[...]
     positions = lax.broadcasted_iota(jnp.int32, ids.shape, 1)
     end_place = jnp.min(jnp.where(ids == jnp.max(ids), positions, ids.shape[1]))
@@ -153,49 +153,25 @@
     packed_ref[:, W_OUT : W_OUT + D] = outs.astype(BF16)
 
 
-def deal_kernel(frame_ref, tokens_ref, *rest):
-    dealt, sems = rest[:-1], rest[-1]
-    copies = [
-        pltpu.make_async_copy(
-            tokens_ref.at[(frame_ref[0] + step) % FRAMES], dealt[step - 1], sems.at[step - 1]
-        )
-        for step in range(1, FRAMES)
-    ]
-    for copy in copies:
-        copy.start()
-    for copy in copies:
-        copy.wait()
-
-
-def temporal_kernel(frame_ref, mixed_ref, gain_ref, weights_ref, tokens_ref, *rest):
-    dealt, rest = rest[: FRAMES - 1], rest[FRAMES - 1 :]
-    out_ref, pool_ref, tokens, qkv, outs, packed, mixed, sems = rest
-    frame = frame_ref[0]
-    copies_tokens = [pltpu.make_async_copy(tokens_ref.at[frame], tokens.at[frame], sems.at[2, 0])]
-    for step in range(1, FRAMES):
-        source = (frame + FRAMES - step) % FRAMES
-        copies_tokens.append(
-            pltpu.make_async_copy(dealt[step - 1], tokens.at[source], sems.at[2, step])
-        )
+def temporal_kernel(
+    mixed_ref, tokens_ref, gain_ref, weights_ref, out_ref, pool_ref, qkv, outs, packed, mixed, sems
+):
     copies_out = gather_rows(weights_ref, W_OUT, outs, sems.at[0])
     copies_qkv = gather_rows(weights_ref, QKV_T, qkv, sems.at[1])
-    for copy in copies_out + copies_tokens + copies_qkv:
+    for copy in copies_out + copies_qkv:
         copy.start()
     for copy in copies_out:
         copy.wait()
     both = outs[...].astype(F32).reshape(64, 2, 8, D)
     out_spatial = both[:, 0].reshape(WIDTH, D).astype(BF16)
     out_temporal = both[:, 1].reshape(WIDTH, D).astype(BF16)
-    for copy in copies_tokens:
-        copy.wait()
-    rows = tokens.shape[0] * tokens.shape[1]
-    spatial = tokens[...].reshape(rows, D).astype(F32) + dot(mixed_ref[...], out_spatial)
-    spatial = spatial.astype(BF16)
+    rows = tokens_ref.shape[0]
+    spatial = (tokens_ref[...].astype(F32) + dot(mixed_ref[...], out_spatial)).astype(BF16)
     normed = layer_norm(spatial.astype(F32), gain_ref[...]).astype(BF16)
     for copy in copies_qkv:
         copy.wait()
     packed[...] = dot(normed, qkv[...].reshape(D, 3 * WIDTH)).astype(BF16)
-    patches = tokens.shape[1]
+    patches = rows // FRAMES
     place = lax.broadcasted_iota(jnp.int32, (rows, rows), 0) % patches
     attend(packed, mixed, place == lax.broadcasted_iota(jnp.int32, (rows, rows), 1) % patches)
     output = spatial.astype(F32) + dot(mixed[...], out_temporal)
@@ -347,8 +323,7 @@
     return jax.ShapeDtypeStruct(dims, dtype)
 
 
-def send_all(block, groups):
-    copies = jnp.broadcast_to(block[None], (len(groups[0]),) + block.shape)
+def send_all(copies, groups):
     return lax.all_to_all(copies, "dp", 0, 0, tiled=True, axis_index_groups=groups)
 
 
@@ -373,12 +348,10 @@
     DMA = pltpu.SemaphoreType.DMA
     halves = (X, Y, 2, 16)
     tokens = video_tokens.reshape(256, D)
-    dealing = video_tokens.reshape(FRAMES, 32, D)
     place = lax.axis_index("dp").astype(jnp.int32).reshape(1)
-    frame = lax.axis_index("frame").astype(jnp.int32).reshape(1)
-    packed = call(
+    packed, own = call(
         pack_kernel,
-        shape((16, PACKED), BF16),
+        (shape((16, PACKED), BF16), shape((Y, 16, 3 * WIDTH), BF16)),
         (A,) * 7,
         [
             pltpu.VMEM(caption_ids.shape, jnp.int32),
@@ -386,6 +359,7 @@
             pltpu.VMEM(w_text.shape, BF16),
             pltpu.VMEM(w_out_spatial.shape, BF16),
             pltpu.VMEM(w_out_temporal.shape, BF16),
+            pltpu.VMEM(w_qkv_spatial.shape, BF16),
             DMA((7,)),
         ],
         vmem=VMEM_WHOLE,
@@ -396,27 +370,21 @@
         w_text,
         w_out_spatial,
         w_out_temporal,
-        w_video,
-    )
-    own = send_all(w_qkv_spatial, ROWS_OF_Y)
-    packed = lax.all_gather(packed, "dp", axis=0, tiled=True, axis_index_groups=ROWS_OF_X)
-    own, packed = lax.optimization_barrier((own, packed))
-    early = lax.all_gather(
-        packed[:, :W_VIDEO], "dp", axis=0, tiled=True, axis_index_groups=ROWS_OF_YC
-    ).reshape(Y, 2, X, 16, W_VIDEO)
-    late = lax.all_gather(
-        packed[:, W_VIDEO:], "dp", axis=0, tiled=True, axis_index_groups=ROWS_OF_YC
-    ).reshape(Y, 2, X, 16, E)
-    own = send_all(own.reshape(Y * 16, 3 * WIDTH), ROWS_OF_X).reshape(X * Y, 16, 3 * WIDTH)
-    dealt = call(
-        deal_kernel, (shape((32, D), BF16),) * (FRAMES - 1), (S, A), [DMA((FRAMES,))],
-        (A,) * (FRAMES - 1),
-    )(frame, dealing)
-    dealt = [
-        lax.ppermute(block, "frame", [(i, (i + 1 + step) % FRAMES) for i in range(FRAMES)])
-        for step, block in enumerate(dealt)
-    ]
-    own, dealt[:4] = lax.optimization_barrier((own, dealt[:4]))
+        w_qkv_spatial,
+    )
+    barrier = lax.optimization_barrier
+    gather = functools.partial(lax.all_gather, axis_name="dp", axis=0, tiled=True)
+    own = send_all(own, ROWS_OF_Y)
+    packed = gather(packed, axis_index_groups=ROWS_OF_X)
+    own, packed, w_video = barrier((own, packed, w_video))
+    early = gather(packed, axis_index_groups=ROWS_OF_YC).reshape(Y, 2, X, 16, PACKED)
+    own = jnp.broadcast_to(own.reshape(1, Y * 16, 3 * WIDTH), (X, Y * 16, 3 * WIDTH))
+    own = send_all(own, ROWS_OF_X)
+    late = gather(w_video, axis_index_groups=ROWS_OF_X)
+    own, late, dealing = barrier((own, late, tokens.reshape(FRAMES, 32, D)))
+    late = gather(late, axis_index_groups=ROWS_OF_YC).reshape(Y, 2, X, 16, E)
+    by_patch = lax.all_to_all(dealing, "frame", 0, 0, tiled=True)
+    own = own.reshape(X * Y, 16, 3 * WIDTH)
     other = lax.ppermute(own, "dp", OTHER_CORE)
 
     mixed = call(
@@ -430,20 +398,20 @@
             DMA((3,)),
         ],
     )(place % 2, tokens, gain_spatial.reshape(1, D), own, other)
-    mixed = lax.all_to_all(mixed.reshape(8, 32, WIDTH), "frame", 0, 0, tiled=True)
+    mixed, by_patch = barrier((mixed, by_patch))
+    mixed = lax.all_to_all(mixed.reshape(FRAMES, 32, WIDTH), "frame", 0, 0, tiled=True)
     layer_out, pool = call(
         temporal_kernel,
         (shape((256, D), BF16), shape((FRAMES, 8, 128), F32)),
-        (S, V, V, A, A) + (A,) * (FRAMES - 1),
+        (V, V, V, A),
         [
-            pltpu.VMEM((FRAMES, 32, D), BF16),
             pltpu.VMEM(halves + (3 * WIDTH,), BF16),
             pltpu.VMEM(halves + (D,), BF16),
             pltpu.VMEM((256, 3 * WIDTH), BF16),
             pltpu.VMEM((256, WIDTH), BF16),
-            DMA((3, 2 * Y)),
+            DMA((2, 2 * Y)),
         ],
-    )(frame, mixed.reshape(256, WIDTH), gain_temporal.reshape(1, D), early, dealing, *dealt)
+    )(mixed.reshape(256, WIDTH), by_patch.reshape(256, D), gain_temporal.reshape(1, D), early)
     text_pool, text_mapped, text_weight = call(
         text_kernel,
         (shape((64, DT), F32), shape((64, E), F32), shape((DT, E), BF16)),

time: 155 us -> 158 us (1.019)
  blocking collectives: 24.1 us -> 59.9 us
  starting transfers between devices: 65.1 us -> 38.1 us
  local copies, waits for them, and re-layouts: 4.44 us -> 1.46 us
  Pallas kernels: 23.7 us -> 22 us
    ppermute x7 -> x0, starting transfers between devices: 31.2 us -> none  [on_device(): lax.ppermute(block, 'frame', [(i, (i + 1 + step) % FRAMES) for i in range...]
    all_gather x1 -> x2, blocking collectives: 11.9 us -> 35.9 us  [the longest x1 23.5 us: on_device(): late = gather(w_video, axis_index_groups=ROWS_OF_X)]
    all_to_all x0 -> x1, blocking collectives: none -> 14.6 us  [on_device(): lax.all_to_all(mixed.reshape(FRAMES, 32, WIDTH), 'frame', 0, 0, tiled=True)]
    all_to_all x1, waiting for transfers between devices: 0.01 us -> 14.1 us  [on_device(): by_patch = lax.all_to_all(dealing, 'frame', 0, 0, tiled=True)]
    ppermute x7 -> x0, waiting for transfers between devices: 11.8 us -> none  [on_device(): lax.ppermute(block, 'frame', [(i, (i + 1 + step) % FRAMES) for i in range...]
    all_to_all x1, starting transfers between devices: 3.42 us -> 10 us  [on_device(): by_patch = lax.all_to_all(dealing, 'frame', 0, 0, tiled=True)]
    all_to_all x1, starting transfers between devices: 13.1 us -> 8.35 us  [on_device(): pooled = lax.all_to_all(pool, 'dp', 0, 0, tiled=True)]
    ppermute x1, waiting for transfers between devices: 3.13 us -> 0.01 us  [on_device(): other = lax.ppermute(own, 'dp', OTHER_CORE)]
  transfers between devices with their start and end apart: 14 -> 7, of which waited for: 5 -> 2; matrix products, arithmetic and copies ran while one was open for 1% -> 1% of each run, Pallas kernels for 12% -> 10%
where the time goes in v5:
time: 158 us; the launch traced here: 157 us
  blocking collectives  59.9 us (38%)
  starting transfers between devices  38.1 us (24%)
  Pallas kernels  22 us (14%)
  waiting for transfers between devices  21.1 us (13%)
  between operations  14.8 us (9%)
    all_gather x1, blocking collectives, on_device(): late = gather(w_video, axis_index_groups=ROWS_OF_X)  23.5 us
    all_to_all x1, blocking collectives, on_device(): lax.all_to_all(mixed.reshape(FRAMES, 32, WIDTH), 'frame', 0, 0, tiled=True)  14.6 us
    all_to_all x1, waiting for transfers between devices, on_device(): by_patch = lax.all_to_all(dealing, 'frame', 0, 0, tiled=True)  14.1 us
    all_to_all x2, starting transfers between devices, send_all(): lax.all_to_all(copies, 'dp', 0, 0, tiled=True, axis_index_groups=groups)  13.5 us
    all_gather x1, blocking collectives, on_device(): packed = gather(packed, axis_index_groups=ROWS_OF_X)  12.4 us
    all_to_all x1, starting transfers between devices, on_device(): by_patch = lax.all_to_all(dealing, 'frame', 0, 0, tiled=True)  10 us
    all_to_all x1, blocking collectives, on_device(): pool = lax.all_to_all(pool, 'frame', 0, 0, tiled=True)  9.31 us
    all_to_all x1, starting transfers between devices, on_device(): pooled = lax.all_to_all(pool, 'dp', 0, 0, tiled=True)  8.35 us
  transfers between devices with their start and end apart: 7, of which 2 were waited for; matrix products, arithmetic and copies ran while one was open for 1% of the time, Pallas kernels for 10%

profile of v5, /device:TPU:1, one launch (start us, length us, event | category | flops | bytes accessed | tf_op | source)
XLA Modules:
  0.0 157.3 jit_solution(10227238314647652664)
XLA Ops:
  7.2 2.1 %shard_map.182 = (bf16[16,3328]{1,0:T(8,128)(2,1)}, bf16[8,16,1536]{2,1,0:T(8,128)(2,1)}) custom-call(s32[1,77]{1,0:T(1,128)} %ids_ref.1, bf16[77,768]{1,0:T(8,128)(2,1)} %bitcast.28, bf16[16,1536]{1,0:T(8,128)(2,1)} %qkv_ref.1, bf16[12,768]{1,0:T(8,128)(2,1)} %text_ref.1, bf16[8,1024]{1,0:T(8,128)(2,1)} %out_s_ref.1, bf16[8,1024]{1,0:T(8,128)(2,1)} %out_t_ref.1, ...), custom_call_target="tpu_custom_call" | custom-call | tf_op jit(solution)/shard_map/pallas_call | solution.py:352
  9.3 7.7 %all-to-all-start = ((bf16[8,16,1536]{2,1,0:T(8,128)(2,1)}), bf16[8,16,1536]{2,1,0:T(8,128)(2,1)S(1)}, u32[]{:S(2)}, u32[]{:S(2)}) async-start(bf16[8,16,1536]{2,1,0:T(8,128)(2,1)} %get-tuple-element.24), calls=%async_computation | async-start | bytes 786432 | tf_op jit(solution)/shard_map/all_to_all | solution.py:327
  16.9 0.0 all-gather.3.cloned.1.call-start
  17.0 12.4 %all_gather.12 = bf16[64,3328]{1,0:T(8,128)(2,1)} all-gather(bf16[16,3328]{1,0:T(8,128)(2,1)} %get-tuple-element.25), channel_id=1, replica_groups={{0,128,256,384},{8,136,264,392},{16,144,272,400},{24,152,280,408},{32,1..., dimensions={0}, use_global_device_ids=true | all-gather | bytes 532480 | tf_op jit(solution)/shard_map/all_gather | solution.py:378
  29.4 0.0 all-to-all-done
  29.4 0.0 all-gather.3.cloned.1.call-update
  29.4 1.3 broadcast_in_dim.8
  30.8 0.0 copy-start.3
  30.8 0.0 copy-start.1
  30.8 5.9 %all-to-all-start.1 = ((bf16[4,128,1536]{2,1,0:T(8,128)(2,1)}), bf16[4,128,1536]{2,1,0:T(8,128)(2,1)S(1)}, u32[]{:S(2)}, u32[]{:S(2)}) async-start(bf16[4,128,1536]{2,1,0:T(8,128)(2,1)} %broadcast_in_dim.8), calls=%async_computation.1 | async-start | bytes 3145728 | tf_op jit(solution)/shard_map/all_to_all | solution.py:327
  36.6 0.0 all-gather.5.cloned.1.call-start
  36.6 0.0 copy-done.3
  36.6 23.5 %all_gather.13 = bf16[64,768]{1,0:T(8,128)(2,1)} all-gather(bf16[16,768]{1,0:T(8,128)(2,1)S(1)} %copy-done.3), channel_id=1, replica_groups={{0,128,256,384},{8,136,264,392},{16,144,272,400},{24,152,280,408},{32,1..., dimensions={0}, use_global_device_ids=true | all-gather | bytes 122880 | tf_op jit(solution)/shard_map/all_gather | solution.py:383
  60.1 0.0 all-to-all-done.1
  60.1 0.0 all-gather.5.cloned.1.call-update
  60.1 6.1 %collective-permute-start = (bf16[32,16,1536]{2,1,0:T(8,128)(2,1)S(1)}, bf16[32,16,1536]{2,1,0:T(8,128)(2,1)}, u32[]{:S(2)}, u32[]{:S(2)}) collective-permute-start(bf16[32,16,1536]{2,1,0:T(8,128)(2,1)S(1)} %bitcast.16), channel_id=1, source_target_pairs={{0,8},{8,0},{16,24},{24,16},{32,40},{40,32},{48,56},{56,48},{64,72... | collective-permute-start | bytes 4718600 | tf_op jit(solution)/shard_map/ppermute | solution.py:388
  66.2 10.0 %all-to-all-start.2 = ((bf16[8,32,1024]{2,1,0:T(8,128)(2,1)}), bf16[8,32,1024]{2,1,0:T(8,128)(2,1)S(1)}, u32[]{:S(2)}, u32[]{:S(2)}) async-start(bf16[8,32,1024]{2,1,0:T(8,128)(2,1)} %bitcast.5), calls=%async_computation.2 | async-start | bytes 1048576 | tf_op jit(solution)/shard_map/all_to_all | solution.py:386
  76.3 0.0 collective-permute-done.other_ref
  76.3 0.0 copy-done.1
  76.3 0.0 copy-start
  76.3 3.9 %shard_map.183 = bf16[256,512]{1,0:T(8,128)(2,1)S(1)} custom-call(s32[1]{0:T(128)S(6)} %select_n.7.core_ref, bf16[256,1024]{1,0:T(8,128)(2,1)} %bitcast.1.tokens_ref, f32[1,1024]{1,0:T(1,128)S(1)} %bitcast.22, bf16[32,16,1536]{2,1,0:T(8,128)(2,1)S(1)} %bitcast.17, bf16[32,16,1536]{2,1,0:T(8,128)(2,1)} %collective-permute-done.other_ref), custom_call_target="tpu_custom_call" | custom-call | tf_op jit(solution)/shard_map/pallas_call | solution.py:390
  80.2 14.1 %all-to-all-done.2 = bf16[8,32,1024]{2,1,0:T(8,128)(2,1)S(1)} async-done(((bf16[8,32,1024]{2,1,0:T(8,128)(2,1)}), bf16[8,32,1024]{2,1,0:T(8,128)(2,1)S(1)}, u32[]{:S(2)}, u32[]{:S(2)}) %all-to-all-start.2) | async-done | bytes 524320 | tf_op jit(solution)/shard_map/all_to_all | solution.py:386
  94.3 14.6 %all_to_all.30 = bf16[8,32,512]{2,1,0:T(8,128)(2,1)S(1)} all-to-all(bf16[8,32,512]{2,1,0:T(8,128)(2,1)S(1)} %bitcast.20), channel_id=1, replica_groups=mesh['dp'=64,'frame'=8] {'frame'}, dimensions={0} | all-to-all | bytes 524288 | tf_op jit(solution)/shard_map/all_to_all | solution.py:402
  109.0 0.0 all-gather.3.cloned.1.call-done
  109.0 0.0 copy-done
  109.0 0.0 copy-start.5
  109.0 0.0 copy-start.4
  109.0 6.2 %shard_map.184 = (bf16[256,1024]{1,0:T(8,128)(2,1)}, f32[8,8,128]{2,1,0:T(8,128)S(1)}) custom-call(bf16[256,512]{1,0:T(8,128)(2,1)S(1)} %bitcast.19, bf16[256,1024]{1,0:T(8,128)(2,1)S(1)} %bitcast.18, f32[1,1024]{1,0:T(1,128)S(1)} %bitcast.21, bf16[8,2,4,16,3328]{4,3,2,1,0:T(8,128)(2,1)} %bitcast.24), custom_call_target="tpu_custom_call" | custom-call | tf_op jit(solution)/shard_map/pallas_call | solution.py:403
  115.2 9.3 %all_to_all.31.parts_ref = f32[8,8,128]{2,1,0:T(8,128)S(1)} all-to-all(f32[8,8,128]{2,1,0:T(8,128)S(1)} %get-tuple-element.34), channel_id=1, replica_groups=mesh['dp'=64,'frame'=8] {'frame'}, dimensions={0} | all-to-all | bytes 65536 | tf_op jit(solution)/shard_map/all_to_all | solution.py:421
  124.5 0.7 shard_map.185
  125.3 8.3 %all-to-all-start.5 = ((f32[64,8,128]{2,1,0:T(8,128)}), f32[64,8,128]{2,1,0:T(8,128)S(1)}, u32[]{:S(2)}, u32[]{:S(2)}) async-start(f32[64,8,128]{2,1,0:T(8,128)} %shard_map.185), calls=%async_computation.5 | async-start | bytes 524288 | tf_op jit(solution)/shard_map/all_to_all | solution.py:423
  134.3 0.0 copy-done.5
  134.3 0.1 copy.20.pairs_ref
  134.4 0.0 copy-done.4
  134.4 0.0 copy-start.2
  134.4 4.2 %shard_map.186 = (f32[64,768]{1,0:T(8,128)S(1)}, f32[64,768]{1,0:T(8,128)S(1)}, bf16[768,768]{1,0:T(8,128)(2,1)S(1)}) custom-call(f32[1,768]{1,0:T(1,128)S(1)} %reshape.72.gain_ref.gain_text_ref, bf16[8,2,4,16,3328]{4,3,2,1,0:T(8,128)(2,1)} %bitcast.25), custom_call_target="tpu_custom_call" | custom-call | tf_op jit(solution)/shard_map/pallas_call | solution.py:415
  138.6 0.0 all-gather.5.cloned.1.call-done
  138.7 7.0 %all-to-all-done.5.pooled_ref = f32[64,8,128]{2,1,0:T(8,128)S(1)} async-done(((f32[64,8,128]{2,1,0:T(8,128)}), f32[64,8,128]{2,1,0:T(8,128)S(1)}, u32[]{:S(2)}, u32[]{:S(2)}) %all-to-all-start.5) | async-done | bytes 262176 | tf_op jit(solution)/shard_map/all_to_all | solution.py:423
  145.6 0.0 copy-done.2
  145.6 4.8 %shard_map.187 = (f32[1]{0:T(128)}, f32[1]{0:T(128)}, f32[1,1024]{1,0:T(1,128)}, f32[1,768]{1,0:T(1,128)}) custom-call(s32[1]{0:T(128)} %bitcast.place_ref, f32[1]{0:T(128)S(6)} %copy.21.scale_ref, s32[64,1]{1,0:T(8,128)S(1)} %copy.20.pairs_ref, f32[64,8,128]{2,1,0:T(8,128)S(1)} %all-to-all-done.5.pooled_ref, f32[64,768]{1,0:T(8,128)S(1)} %get-tuple-element.35.text_pool_ref, ...), custom_call_target="tpu_custom_call" | custom-call | tf_op jit(solution)/shard_map/pallas_call | solution.py:424
  (1 shorter events, 0.0 us)
Async XLA Ops:
  9.3 20.1 %all-to-all-start = ((bf16[8,16,1536]{2,1,0:T(8,128)(2,1)}), bf16[8,16,1536]{2,1,0:T(8,128)(2,1)S(1)}, u32[]{:S(2)}, u32[]{:S(2)}) async-start(bf16[8,16,1536]{2,1,0:T(8,128)(2,1)} %get-tuple-element.24), calls=%async_computation | async-start | bytes 786432 | tf_op jit(solution)/shard_map/all_to_all | solution.py:327
  16.9 92.1 %all-gather.3.cloned.1.call-start = ((), (), s32[]{:S(2)}) async-start(), calls=%async_computation.6 | async-start | bytes 7241728 | tf_op jit(solution)/shard_map/all_gather | solution.py:380
  30.8 5.9 %copy-start.3 = (bf16[16,768]{1,0:T(8,128)(2,1)S(1)}, bf16[16,768]{1,0:T(8,128)(2,1)}, u32[]{:S(2)}) copy-start(bf16[16,768]{1,0:T(8,128)(2,1)} %param.28) | copy-start | bytes 73732
  30.8 45.5 %copy-start.1 = (f32[1024]{0:T(1024)S(1)}, f32[1024]{0:T(1024)}, u32[]{:S(2)}) copy-start(f32[1024]{0:T(1024)} %param.20) | copy-start | bytes 12292
  30.8 29.3 %all-to-all-start.1 = ((bf16[4,128,1536]{2,1,0:T(8,128)(2,1)}), bf16[4,128,1536]{2,1,0:T(8,128)(2,1)S(1)}, u32[]{:S(2)}, u32[]{:S(2)}) async-start(bf16[4,128,1536]{2,1,0:T(8,128)(2,1)} %broadcast_in_dim.8), calls=%async_computation.1 | async-start | bytes 3145728 | tf_op jit(solution)/shard_map/all_to_all | solution.py:327
  36.6 102.0 %all-gather.5.cloned.1.call-start = ((), (), s32[]{:S(2)}) async-start(), calls=%async_computation.7 | async-start | bytes 1671168 | tf_op jit(solution)/shard_map/all_gather | solution.py:385
  60.1 16.2 %collective-permute-start = (bf16[32,16,1536]{2,1,0:T(8,128)(2,1)S(1)}, bf16[32,16,1536]{2,1,0:T(8,128)(2,1)}, u32[]{:S(2)}, u32[]{:S(2)}) collective-permute-start(bf16[32,16,1536]{2,1,0:T(8,128)(2,1)S(1)} %bitcast.16), channel_id=1, source_target_pairs={{0,8},{8,0},{16,24},{24,16},{32,40},{40,32},{48,56},{56,48},{64,72... | collective-permute-start | bytes 4718600 | tf_op jit(solution)/shard_map/ppermute | solution.py:388
  66.2 28.1 %all-to-all-start.2 = ((bf16[8,32,1024]{2,1,0:T(8,128)(2,1)}), bf16[8,32,1024]{2,1,0:T(8,128)(2,1)S(1)}, u32[]{:S(2)}, u32[]{:S(2)}) async-start(bf16[8,32,1024]{2,1,0:T(8,128)(2,1)} %bitcast.5), calls=%async_computation.2 | async-start | bytes 1048576 | tf_op jit(solution)/shard_map/all_to_all | solution.py:386
  76.3 32.7 %copy-start = (f32[1024]{0:T(1024)S(1)}, f32[1024]{0:T(1024)}, u32[]{:S(2)}) copy-start(f32[1024]{0:T(1024)} %param.21) | copy-start | bytes 12292
  109.0 25.3 %copy-start.5 = (s32[64]{0:T(128)S(1)}, s32[64]{0:T(128)}, u32[]{:S(2)}) copy-start(s32[64]{0:T(128)} %param.18) | copy-start | bytes 772
  109.0 25.4 %copy-start.4 = (f32[768]{0:T(1024)S(1)}, f32[768]{0:T(1024)}, u32[]{:S(2)}) copy-start(f32[768]{0:T(1024)} %param.23) | copy-start | bytes 9220
  125.3 20.4 %all-to-all-start.5 = ((f32[64,8,128]{2,1,0:T(8,128)}), f32[64,8,128]{2,1,0:T(8,128)S(1)}, u32[]{:S(2)}, u32[]{:S(2)}) async-start(f32[64,8,128]{2,1,0:T(8,128)} %shard_map.185), calls=%async_computation.5 | async-start | bytes 524288 | tf_op jit(solution)/shard_map/all_to_all | solution.py:423
  134.4 11.2 %copy-start.2 = (f32[1024]{0:T(1024)S(1)}, f32[1024]{0:T(1024)}, u32[]{:S(2)}) copy-start(f32[1024]{0:T(1024)} %param.22) | copy-start | bytes 12292
Sparse Core Ops, SparseCore 0:
  29.5 57.0 all-gather.2
  88.8 40.4 all-gather.4

commit v6 on v5

--- a/solution.py
+++ b/solution.py
@@ -22,10 +22,12 @@
 VMEM_WHOLE = 63 * MIB
 VMEM_MOST = 52 * MIB
 
-QKV_T = 0
-W_TEXT = 1536
-W_OUT = 2304
-PACKED = 3328
+QKV = 0
+OUT = 1536
+PACKED_S = 2048
+W_TEXT = 2048
+W_VIDEO = 2816
+PACKED_T = 3584
 
 X, Y = 4, 8
 ROWS_OF_X = [[(x * Y + y) * 2 + c for x in range(X)] for y in range(Y) for c in range(2)]
@@ -91,22 +93,40 @@
         mixed_ref[:, at : at + 2 * HD] = attend_pair(query, key, value, mask)
 
 
+def out_halves(gathered):
+    halves = gathered.astype(F32).reshape(64, 2, 8, D // 2)
+    return [halves[:, side].reshape(WIDTH, D // 2).astype(BF16) for side in range(2)]
+
+
 def spatial_kernel(
-    core_ref, tokens_ref, gain_ref, own_ref, other_ref, mixed_ref, tokens, qkv, packed, sems
+    core_ref, tokens_ref, gain_ref, own_ref, other_ref, spatial_ref, qkv, outs, packed, mixed, sems
 ):
     core = core_ref[0]
-    copy_tokens = pltpu.make_async_copy(tokens_ref, tokens, sems.at[2])
-    copy_own = pltpu.make_async_copy(own_ref, qkv.at[:, core], sems.at[0])
-    copy_other = pltpu.make_async_copy(other_ref, qkv.at[:, 1 - core], sems.at[1])
-    copy_tokens.start()
-    copy_own.start()
-    copy_other.start()
-    copy_tokens.wait()
-    normed = layer_norm(tokens[...].astype(F32), gain_ref[...]).astype(BF16)
-    copy_own.wait()
-    copy_other.wait()
+    copies = []
+    for half, (ref, place) in enumerate(((own_ref, core), (other_ref, 1 - core))):
+        for part, (first, target) in enumerate(((QKV, qkv), (OUT, outs))):
+            copies.append(
+                pltpu.make_async_copy(
+                    ref.at[:, :, first : first + target.shape[-1]],
+                    target.at[:, place],
+                    sems.at[2 * half + part],
+                )
+            )
+    for copy in copies:
+        copy.start()
+    tokens = tokens_ref[...].astype(F32)
+    normed = layer_norm(tokens, gain_ref[...]).astype(BF16)
+    copies[0].wait()
+    copies[2].wait()
     packed[...] = dot(normed, qkv[...].reshape(D, 3 * WIDTH)).astype(BF16)
-    attend(packed, mixed_ref, None)
+    attend(packed, mixed, None)
+    copies[1].wait()
+    copies[3].wait()
+    for side, weight in enumerate(out_halves(outs[...])):
+        columns = slice(side * (D // 2), (side + 1) * (D // 2))
+        spatial_ref[:, columns] = (
+            tokens_ref[:, columns].astype(F32) + dot(mixed[...], weight)
+        ).astype(BF16)
 
 
 def gather_rows(weights_ref, first, target, sems):
@@ -121,24 +141,31 @@
 
 
 def pack_kernel(
-    ids_ref, states_ref, qkv_ref, text_ref, out_s_ref, out_t_ref, spatial_ref, packed_ref, copies_ref,
-    ids_here, states_here, text_here, out_s_here, out_t_here, spatial_here, sems,
+    ids_ref, states_ref, qkv_ref, text_ref, out_s_ref, out_t_ref, video_ref, spatial_ref,
+    packed_ref, copies_ref,
+    ids_here, states_here, text_here, out_s_here, out_t_here, sems,
 ):
     pairs = (
-        (spatial_ref, spatial_here),
+        (spatial_ref, copies_ref.at[0, :, QKV : QKV + 3 * WIDTH]),
         (ids_ref, ids_here),
         (states_ref, states_here),
         (text_ref, text_here),
         (out_s_ref, out_s_here),
         (out_t_ref, out_t_here),
-        (qkv_ref, packed_ref.at[:, QKV_T : QKV_T + 3 * WIDTH]),
+        (qkv_ref, packed_ref.at[:, QKV : QKV + 3 * WIDTH]),
+        (video_ref, packed_ref.at[:, W_VIDEO : W_VIDEO + E]),
     )
     copies = [pltpu.make_async_copy(*pair, sems.at[i]) for i, pair in enumerate(pairs)]
     for copy in copies:
         copy.start()
     for copy in copies:
         copy.wait()
-    copies_ref[...] = jnp.broadcast_to(spatial_here[...][None], copies_ref.shape)
+    for source, target in ((out_s_here, copies_ref.at[0]), (out_t_here, packed_ref)):
+        rows = source[...].astype(F32)
+        rows = jnp.concatenate([rows[:, : D // 2], rows[:, D // 2 :]], axis=0)
+        target[:, OUT : OUT + D // 2] = rows.astype(BF16)
+    for copy in range(1, Y):
+        copies_ref[copy] = copies_ref[0]
     ids = ids_here[...]
     positions = lax.broadcasted_iota(jnp.int32, ids.shape, 1)
     end_place = jnp.min(jnp.where(ids == jnp.max(ids), positions, ids.shape[1]))
@@ -149,39 +176,36 @@
     place = lax.broadcasted_iota(jnp.int32, text.shape, 0)
     text = jnp.where(place < 12, text, jnp.where(place == 12, text_row, 0.0))
     packed_ref[:, W_TEXT : W_TEXT + E] = text.astype(BF16)
-    outs = jnp.concatenate([out_s_here[...].astype(F32), out_t_here[...].astype(F32)], axis=0)
-    packed_ref[:, W_OUT : W_OUT + D] = outs.astype(BF16)
 
 
 def temporal_kernel(
-    mixed_ref, tokens_ref, gain_ref, weights_ref, out_ref, pool_ref, qkv, outs, packed, mixed, sems
-):
-    copies_out = gather_rows(weights_ref, W_OUT, outs, sems.at[0])
-    copies_qkv = gather_rows(weights_ref, QKV_T, qkv, sems.at[1])
-    for copy in copies_out + copies_qkv:
+    spatial_ref, gain_ref, weights_ref, out_ref, pool_ref, qkv, outs, packed, mixed, sems
+):
+    copies_qkv = gather_rows(weights_ref, QKV, qkv, sems.at[0])
+    copies_out = gather_rows(weights_ref, OUT, outs, sems.at[1])
+    for copy in copies_qkv + copies_out:
         copy.start()
-    for copy in copies_out:
-        copy.wait()
-    both = outs[...].astype(F32).reshape(64, 2, 8, D)
-    out_spatial = both[:, 0].reshape(WIDTH, D).astype(BF16)
-    out_temporal = both[:, 1].reshape(WIDTH, D).astype(BF16)
-    rows = tokens_ref.shape[0]
-    spatial = (tokens_ref[...].astype(F32) + dot(mixed_ref[...], out_spatial)).astype(BF16)
-    normed = layer_norm(spatial.astype(F32), gain_ref[...]).astype(BF16)
+    rows = spatial_ref.shape[0]
+    spatial = spatial_ref[...].astype(F32)
+    normed = layer_norm(spatial, gain_ref[...]).astype(BF16)
     for copy in copies_qkv:
         copy.wait()
     packed[...] = dot(normed, qkv[...].reshape(D, 3 * WIDTH)).astype(BF16)
     patches = rows // FRAMES
     place = lax.broadcasted_iota(jnp.int32, (rows, rows), 0) % patches
     attend(packed, mixed, place == lax.broadcasted_iota(jnp.int32, (rows, rows), 1) % patches)
-    output = spatial.astype(F32) + dot(mixed[...], out_temporal)
-    output = output.astype(BF16)
-    out_ref[...] = output
-    total = jnp.sum(output.astype(F32), axis=0, keepdims=True)
-    for chunk in range(D // 128):
-        pool_ref[:, chunk, :] = jnp.broadcast_to(
-            total[:, chunk * 128 : (chunk + 1) * 128], (FRAMES, 128)
-        )
+    for copy in copies_out:
+        copy.wait()
+    half = D // 2
+    for side, weight in enumerate(out_halves(outs[...])):
+        columns = slice(side * half, (side + 1) * half)
+        output = (spatial_ref[:, columns].astype(F32) + dot(mixed[...], weight)).astype(BF16)
+        out_ref[:, columns] = output
+        total = jnp.sum(output.astype(F32), axis=0, keepdims=True)
+        for chunk in range(half // 128):
+            pool_ref[:, side * (half // 128) + chunk, :] = jnp.broadcast_to(
+                total[:, chunk * 128 : (chunk + 1) * 128], (FRAMES, 128)
+            )
 
 
 def spread_kernel(parts_ref, every_ref):
@@ -251,7 +275,7 @@
     sems,
 ):
     me = place_ref[0]
-    copies = gather_rows(weights_ref, 0, gathered, sems)
+    copies = gather_rows(weights_ref, W_VIDEO, gathered, sems)
     copy_text = pltpu.make_async_copy(text_weight_ref, text_weight, sems.at[2 * Y])
     for copy in copies + [copy_text]:
         copy.start()
@@ -351,16 +375,15 @@
     place = lax.axis_index("dp").astype(jnp.int32).reshape(1)
     packed, own = call(
         pack_kernel,
-        (shape((16, PACKED), BF16), shape((Y, 16, 3 * WIDTH), BF16)),
-        (A,) * 7,
+        (shape((16, PACKED_T), BF16), shape((Y, 16, PACKED_S), BF16)),
+        (A,) * 8,
         [
             pltpu.VMEM(caption_ids.shape, jnp.int32),
             pltpu.VMEM(text_states.shape[1:], BF16),
             pltpu.VMEM(w_text.shape, BF16),
             pltpu.VMEM(w_out_spatial.shape, BF16),
             pltpu.VMEM(w_out_temporal.shape, BF16),
-            pltpu.VMEM(w_qkv_spatial.shape, BF16),
-            DMA((7,)),
+            DMA((8,)),
         ],
         vmem=VMEM_WHOLE,
     )(
@@ -370,54 +393,50 @@
         w_text,
         w_out_spatial,
         w_out_temporal,
+        w_video,
         w_qkv_spatial,
     )
     barrier = lax.optimization_barrier
     gather = functools.partial(lax.all_gather, axis_name="dp", axis=0, tiled=True)
     own = send_all(own, ROWS_OF_Y)
     packed = gather(packed, axis_index_groups=ROWS_OF_X)
-    own, packed, w_video = barrier((own, packed, w_video))
-    early = gather(packed, axis_index_groups=ROWS_OF_YC).reshape(Y, 2, X, 16, PACKED)
-    own = jnp.broadcast_to(own.reshape(1, Y * 16, 3 * WIDTH), (X, Y * 16, 3 * WIDTH))
-    own = send_all(own, ROWS_OF_X)
-    late = gather(w_video, axis_index_groups=ROWS_OF_X)
-    own, late, dealing = barrier((own, late, tokens.reshape(FRAMES, 32, D)))
-    late = gather(late, axis_index_groups=ROWS_OF_YC).reshape(Y, 2, X, 16, E)
-    by_patch = lax.all_to_all(dealing, "frame", 0, 0, tiled=True)
-    own = own.reshape(X * Y, 16, 3 * WIDTH)
+    own, packed = barrier((own, packed))
+    weights = gather(packed, axis_index_groups=ROWS_OF_YC).reshape(Y, 2, X, 16, PACKED_T)
+    own = jnp.broadcast_to(own.reshape(1, Y * 16, PACKED_S), (X, Y * 16, PACKED_S))
+    own = send_all(own, ROWS_OF_X).reshape(X * Y, 16, PACKED_S)
     other = lax.ppermute(own, "dp", OTHER_CORE)
 
-    mixed = call(
+    spatial = call(
         spatial_kernel,
-        shape((256, WIDTH), BF16),
-        (S, A, V, A, A),
+        shape((256, D), BF16),
+        (S, V, V, A, A),
         [
-            pltpu.VMEM((256, D), BF16),
             pltpu.VMEM((X * Y, 2, 16, 3 * WIDTH), BF16),
+            pltpu.VMEM((X * Y, 2, 16, D // 2), BF16),
             pltpu.VMEM((256, 3 * WIDTH), BF16),
-            DMA((3,)),
+            pltpu.VMEM((256, WIDTH), BF16),
+            DMA((4,)),
         ],
     )(place % 2, tokens, gain_spatial.reshape(1, D), own, other)
-    mixed, by_patch = barrier((mixed, by_patch))
-    mixed = lax.all_to_all(mixed.reshape(FRAMES, 32, WIDTH), "frame", 0, 0, tiled=True)
+    spatial = lax.all_to_all(spatial.reshape(FRAMES, 32, D), "frame", 0, 0, tiled=True)
     layer_out, pool = call(
         temporal_kernel,
         (shape((256, D), BF16), shape((FRAMES, 8, 128), F32)),
-        (V, V, V, A),
+        (V, V, A),
         [
             pltpu.VMEM(halves + (3 * WIDTH,), BF16),
-            pltpu.VMEM(halves + (D,), BF16),
+            pltpu.VMEM(halves + (D // 2,), BF16),
             pltpu.VMEM((256, 3 * WIDTH), BF16),
             pltpu.VMEM((256, WIDTH), BF16),
             DMA((2, 2 * Y)),
         ],
-    )(mixed.reshape(256, WIDTH), by_patch.reshape(256, D), gain_temporal.reshape(1, D), early)
+    )(spatial.reshape(256, D), gain_temporal.reshape(1, D), weights)
     text_pool, text_mapped, text_weight = call(
         text_kernel,
         (shape((64, DT), F32), shape((64, E), F32), shape((DT, E), BF16)),
         (V, A),
         [pltpu.VMEM(halves + (E,), BF16), DMA((2 * Y,))],
-    )(gain_text.reshape(1, DT), early)
+    )(gain_text.reshape(1, DT), weights)
     pool = lax.all_to_all(pool, "frame", 0, 0, tiled=True)
     pool = call(spread_kernel, shape((64, 8, 128), F32), (V,), [])(pool)
     pooled = lax.all_to_all(pool, "dp", 0, 0, tiled=True)
@@ -443,7 +462,7 @@
         text_weight,
         gain_video.reshape(1, D),
         gain_text.reshape(1, DT),
-        late,
+        weights,
     )
     return (layer_out.reshape(1, 8, 32, D), video_loss, text_loss, grad_pooled, grad_text)
 

time: 158 us -> 151 us (0.956)
  blocking collectives: 59.9 us -> 82.6 us
  starting transfers between devices: 38.1 us -> 17.2 us
  waiting for transfers between devices: 21.1 us -> 12.9 us
    all_to_all x1 -> x2, blocking collectives: 14.6 us -> 60.5 us  [the longest x1 32.5 us: send_all(): lax.all_to_all(copies, 'dp', 0, 0, tiled=True, axis_index_groups=groups)]
    all_gather x1 -> x0, blocking collectives: 23.5 us -> none  [on_device(): late = gather(w_video, axis_index_groups=ROWS_OF_X)]
    all_to_all x1 -> x0, waiting for transfers between devices: 14.1 us -> none  [on_device(): by_patch = lax.all_to_all(dealing, 'frame', 0, 0, tiled=True)]
    all_to_all x1 -> x0, starting transfers between devices: 10 us -> none  [on_device(): by_patch = lax.all_to_all(dealing, 'frame', 0, 0, tiled=True)]
    all_to_all x2 -> x1, starting transfers between devices: 13.5 us -> 7.66 us  [send_all(): lax.all_to_all(copies, 'dp', 0, 0, tiled=True, axis_index_groups=groups)]
    ppermute x1, waiting for transfers between devices: 0.01 us -> 3.88 us  [on_device(): other = lax.ppermute(own, 'dp', OTHER_CORE)]
    all_to_all x1, starting transfers between devices: 8.35 us -> 5.74 us  [on_device(): pooled = lax.all_to_all(pool, 'dp', 0, 0, tiled=True)]
    ppermute x1, starting transfers between devices: 6.1 us -> 3.81 us  [on_device(): other = lax.ppermute(own, 'dp', OTHER_CORE)]
  transfers between devices with their start and end apart: 7 -> 4, of which waited for: 2 -> 3; matrix products, arithmetic and copies ran while one was open for 1% -> 0% of each run, Pallas kernels for 10% -> 6%
where the time goes in v6:
time: 151 us; the launch traced here: 150 us
  blocking collectives  82.6 us (55%)
  Pallas kernels  22.2 us (15%)
  starting transfers between devices  17.2 us (11%)
  between operations  14.8 us (10%)
  waiting for transfers between devices  12.9 us (9%)
    all_to_all x1, blocking collectives, send_all(): lax.all_to_all(copies, 'dp', 0, 0, tiled=True, axis_index_groups=groups)  32.5 us
    all_to_all x1, blocking collectives, on_device(): lax.all_to_all(spatial.reshape(FRAMES, 32, D), 'frame', 0, 0, tiled=True)  28 us
    all_gather x1, blocking collectives, on_device(): packed = gather(packed, axis_index_groups=ROWS_OF_X)  12.8 us
    all_to_all x1, blocking collectives, on_device(): pool = lax.all_to_all(pool, 'frame', 0, 0, tiled=True)  9.27 us
    all_to_all x1, starting transfers between devices, send_all(): lax.all_to_all(copies, 'dp', 0, 0, tiled=True, axis_index_groups=groups)  7.66 us
    all_to_all x1, waiting for transfers between devices, on_device(): pooled = lax.all_to_all(pool, 'dp', 0, 0, tiled=True)  7.02 us
    pallas_call x1, Pallas kernels, on_device(): call(temporal_kernel, (shape((256, D), BF16), shape((FRAMES, 8, 128), F32...  5.77 us
    all_to_all x1, starting transfers between devices, on_device(): pooled = lax.all_to_all(pool, 'dp', 0, 0, tiled=True)  5.74 us
  transfers between devices with their start and end apart: 4, of which 3 were waited for; matrix products, arithmetic and copies ran while one was open for 0% of the time, Pallas kernels for 6%

profile of v6, /device:TPU:1, one launch (start us, length us, event | category | flops | bytes accessed | tf_op | source)
XLA Modules:
  0.0 150.1 jit_solution(10346996411423164336)
XLA Ops:
  7.2 2.1 %shard_map.182 = (bf16[16,3584]{1,0:T(8,128)(2,1)}, bf16[8,16,2048]{2,1,0:T(8,128)(2,1)}) custom-call(s32[1,77]{1,0:T(1,128)} %ids_ref.1, bf16[77,768]{1,0:T(8,128)(2,1)} %bitcast.25, bf16[16,1536]{1,0:T(8,128)(2,1)} %qkv_ref.1, bf16[12,768]{1,0:T(8,128)(2,1)} %text_ref.1, bf16[8,1024]{1,0:T(8,128)(2,1)} %out_s_ref.1, bf16[8,1024]{1,0:T(8,128)(2,1)} %out_t_ref.1, ...), custom_call_target="tpu_custom_call" | custom-call | tf_op jit(solution)/shard_map/pallas_call | solution.py:376
  9.3 7.7 %all-to-all-start = ((bf16[8,16,2048]{2,1,0:T(8,128)(2,1)}), bf16[8,16,2048]{2,1,0:T(8,128)(2,1)S(1)}, u32[]{:S(2)}, u32[]{:S(2)}) async-start(bf16[8,16,2048]{2,1,0:T(8,128)(2,1)} %get-tuple-element.18), calls=%async_computation | async-start | bytes 1048576 | tf_op jit(solution)/shard_map/all_to_all | solution.py:351
  16.9 0.0 all-gather.2.cloned.1.call-start
  17.0 12.8 %all_gather.6 = bf16[64,3584]{1,0:T(8,128)(2,1)} all-gather(bf16[16,3584]{1,0:T(8,128)(2,1)} %get-tuple-element.19), channel_id=1, replica_groups={{0,128,256,384},{8,136,264,392},{16,144,272,400},{24,152,280,408},{32,1..., dimensions={0}, use_global_device_ids=true | all-gather | bytes 573440 | tf_op jit(solution)/shard_map/all_gather | solution.py:402
  29.7 1.9 %all-to-all-done = bf16[8,16,2048]{2,1,0:T(8,128)(2,1)S(1)} async-done(((bf16[8,16,2048]{2,1,0:T(8,128)(2,1)}), bf16[8,16,2048]{2,1,0:T(8,128)(2,1)S(1)}, u32[]{:S(2)}, u32[]{:S(2)}) %all-to-all-start) | async-done | bytes 524320 | tf_op jit(solution)/shard_map/all_to_all | solution.py:351
  31.7 0.0 all-gather.2.cloned.1.call-update
  31.7 0.2 broadcast_in_dim.8
  32.0 0.0 copy-start
  32.0 0.0 copy-start.2
  32.0 32.5 %all_to_all.25 = bf16[4,128,2048]{2,1,0:T(8,128)(2,1)S(1)} all-to-all(bf16[4,128,2048]{2,1,0:T(8,128)(2,1)S(1)} %broadcast_in_dim.8), channel_id=1, replica_groups={{0,128,256,384},{8,136,264,392},{16,144,272,400},{24,152,280,408},{32,1..., dimensions={0} | all-to-all | bytes 4194304 | tf_op jit(solution)/shard_map/all_to_all | solution.py:351
  64.5 3.8 %collective-permute-start = (bf16[32,16,2048]{2,1,0:T(8,128)(2,1)S(1)}, bf16[32,16,2048]{2,1,0:T(8,128)(2,1)}, u32[]{:S(2)}, u32[]{:S(2)}) collective-permute-start(bf16[32,16,2048]{2,1,0:T(8,128)(2,1)S(1)} %bitcast.13), channel_id=1, source_target_pairs={{0,8},{8,0},{16,24},{24,16},{32,40},{40,32},{48,56},{56,48},{64,72... | collective-permute-start | bytes 6291464 | tf_op jit(solution)/shard_map/ppermute | solution.py:407
  68.3 3.9 %collective-permute-done.other_ref = bf16[32,16,2048]{2,1,0:T(8,128)(2,1)} collective-permute-done((bf16[32,16,2048]{2,1,0:T(8,128)(2,1)S(1)}, bf16[32,16,2048]{2,1,0:T(8,128)(2,1)}, u32[]{:S(2)}, u32[]{:S(2)}) %collective-permute-start) | collective-permute-done | bytes 2097184 | tf_op jit(solution)/shard_map/ppermute | solution.py:407
  72.2 0.0 copy-done
  72.2 0.0 copy-done.2
  72.2 0.0 copy-start.1
  72.2 4.5 %shard_map.183 = bf16[256,1024]{1,0:T(8,128)(2,1)S(1)} custom-call(s32[1]{0:T(128)S(6)} %select_n.7.core_ref, bf16[256,1024]{1,0:T(8,128)(2,1)S(1)} %bitcast.17, f32[1,1024]{1,0:T(1,128)S(1)} %bitcast.19, bf16[32,16,2048]{2,1,0:T(8,128)(2,1)S(1)} %bitcast.14, bf16[32,16,2048]{2,1,0:T(8,128)(2,1)} %collective-permute-done.other_ref), custom_call_target="tpu_custom_call" | custom-call | tf_op jit(solution)/shard_map/pallas_call | solution.py:409
  76.8 28.0 %all_to_all.26 = bf16[8,32,1024]{2,1,0:T(8,128)(2,1)S(1)} all-to-all(bf16[8,32,1024]{2,1,0:T(8,128)(2,1)S(1)} %bitcast.16), channel_id=1, replica_groups=mesh['dp'=64,'frame'=8] {'frame'}, dimensions={0} | all-to-all | bytes 1048576 | tf_op jit(solution)/shard_map/all_to_all | solution.py:421
  104.8 0.0 all-gather.2.cloned.1.call-done
  104.8 0.0 copy-done.1
  104.8 0.0 copy-start.5
  104.8 0.0 copy-start.4
  104.8 5.8 %shard_map.184 = (bf16[256,1024]{1,0:T(8,128)(2,1)}, f32[8,8,128]{2,1,0:T(8,128)S(1)}) custom-call(bf16[256,1024]{1,0:T(8,128)(2,1)S(1)} %bitcast.15, f32[1,1024]{1,0:T(1,128)S(1)} %bitcast.18, bf16[8,2,4,16,3584]{4,3,2,1,0:T(8,128)(2,1)} %bitcast.21), custom_call_target="tpu_custom_call" | custom-call | tf_op jit(solution)/shard_map/pallas_call | solution.py:422
  110.6 9.3 %all_to_all.27.parts_ref = f32[8,8,128]{2,1,0:T(8,128)S(1)} all-to-all(f32[8,8,128]{2,1,0:T(8,128)S(1)} %get-tuple-element.23), channel_id=1, replica_groups=mesh['dp'=64,'frame'=8] {'frame'}, dimensions={0} | all-to-all | bytes 65536 | tf_op jit(solution)/shard_map/all_to_all | solution.py:440
  119.9 0.7 shard_map.185
  120.6 5.7 %all-to-all-start.4 = ((f32[64,8,128]{2,1,0:T(8,128)}), f32[64,8,128]{2,1,0:T(8,128)S(1)}, u32[]{:S(2)}, u32[]{:S(2)}) async-start(f32[64,8,128]{2,1,0:T(8,128)} %shard_map.185), calls=%async_computation.4 | async-start | bytes 524288 | tf_op jit(solution)/shard_map/all_to_all | solution.py:442
  127.0 0.0 copy-done.5
  127.0 0.1 copy.20.pairs_ref
  127.1 0.0 copy-done.4
  127.1 0.0 copy-start.3
  127.1 4.2 %shard_map.186 = (f32[64,768]{1,0:T(8,128)S(1)}, f32[64,768]{1,0:T(8,128)S(1)}, bf16[768,768]{1,0:T(8,128)(2,1)S(1)}) custom-call(f32[1,768]{1,0:T(1,128)S(1)} %reshape.65.gain_ref.gain_text_ref, bf16[8,2,4,16,3584]{4,3,2,1,0:T(8,128)(2,1)} %bitcast.22), custom_call_target="tpu_custom_call" | custom-call | tf_op jit(solution)/shard_map/pallas_call | solution.py:434
  131.3 7.0 %all-to-all-done.4.pooled_ref = f32[64,8,128]{2,1,0:T(8,128)S(1)} async-done(((f32[64,8,128]{2,1,0:T(8,128)}), f32[64,8,128]{2,1,0:T(8,128)S(1)}, u32[]{:S(2)}, u32[]{:S(2)}) %all-to-all-start.4) | async-done | bytes 262176 | tf_op jit(solution)/shard_map/all_to_all | solution.py:442
  138.4 0.0 copy-done.3
  138.4 4.8 %shard_map.187 = (f32[1]{0:T(128)}, f32[1]{0:T(128)}, f32[1,1024]{1,0:T(1,128)}, f32[1,768]{1,0:T(1,128)}) custom-call(s32[1]{0:T(128)} %bitcast.place_ref, f32[1]{0:T(128)S(6)} %copy.21.scale_ref, s32[64,1]{1,0:T(8,128)S(1)} %copy.20.pairs_ref, f32[64,8,128]{2,1,0:T(8,128)S(1)} %all-to-all-done.4.pooled_ref, f32[64,768]{1,0:T(8,128)S(1)} %get-tuple-element.24.text_pool_ref, ...), custom_call_target="tpu_custom_call" | custom-call | tf_op jit(solution)/shard_map/pallas_call | solution.py:443
  (1 shorter events, 0.0 us)
Async XLA Ops:
  9.3 22.4 %all-to-all-start = ((bf16[8,16,2048]{2,1,0:T(8,128)(2,1)}), bf16[8,16,2048]{2,1,0:T(8,128)(2,1)S(1)}, u32[]{:S(2)}, u32[]{:S(2)}) async-start(bf16[8,16,2048]{2,1,0:T(8,128)(2,1)} %get-tuple-element.18), calls=%async_computation | async-start | bytes 1048576 | tf_op jit(solution)/shard_map/all_to_all | solution.py:351
  16.9 87.9 %all-gather.2.cloned.1.call-start = ((), (), s32[]{:S(2)}) async-start(), calls=%async_computation.5 | async-start | bytes 7798784 | tf_op jit(solution)/shard_map/all_gather | solution.py:404
  32.0 40.3 %copy-start = (bf16[1,1,256,1024]{3,2,1,0:T(8,128)(2,1)S(1)}, bf16[1,1,256,1024]{3,2,1,0:T(8,128)(2,1)}, u32[]{:S(2)}) copy-start(bf16[1,1,256,1024]{3,2,1,0:T(8,128)(2,1)} %param.15) | copy-start | bytes 1572868
  32.0 40.3 %copy-start.2 = (f32[1024]{0:T(1024)S(1)}, f32[1024]{0:T(1024)}, u32[]{:S(2)}) copy-start(f32[1024]{0:T(1024)} %param.20) | copy-start | bytes 12292
  64.5 7.7 %collective-permute-start = (bf16[32,16,2048]{2,1,0:T(8,128)(2,1)S(1)}, bf16[32,16,2048]{2,1,0:T(8,128)(2,1)}, u32[]{:S(2)}, u32[]{:S(2)}) collective-permute-start(bf16[32,16,2048]{2,1,0:T(8,128)(2,1)S(1)} %bitcast.13), channel_id=1, source_target_pairs={{0,8},{8,0},{16,24},{24,16},{32,40},{40,32},{48,56},{56,48},{64,72... | collective-permute-start | bytes 6291464 | tf_op jit(solution)/shard_map/ppermute | solution.py:407
  72.2 32.6 %copy-start.1 = (f32[1024]{0:T(1024)S(1)}, f32[1024]{0:T(1024)}, u32[]{:S(2)}) copy-start(f32[1024]{0:T(1024)} %param.21) | copy-start | bytes 12292
  104.8 22.2 %copy-start.5 = (s32[64]{0:T(128)S(1)}, s32[64]{0:T(128)}, u32[]{:S(2)}) copy-start(s32[64]{0:T(128)} %param.18) | copy-start | bytes 772
  104.8 22.3 %copy-start.4 = (f32[768]{0:T(1024)S(1)}, f32[768]{0:T(1024)}, u32[]{:S(2)}) copy-start(f32[768]{0:T(1024)} %param.23) | copy-start | bytes 9220
  120.6 17.8 %all-to-all-start.4 = ((f32[64,8,128]{2,1,0:T(8,128)}), f32[64,8,128]{2,1,0:T(8,128)S(1)}, u32[]{:S(2)}, u32[]{:S(2)}) async-start(f32[64,8,128]{2,1,0:T(8,128)} %shard_map.185), calls=%async_computation.4 | async-start | bytes 524288 | tf_op jit(solution)/shard_map/all_to_all | solution.py:442
  127.1 11.3 %copy-start.3 = (f32[1024]{0:T(1024)S(1)}, f32[1024]{0:T(1024)}, u32[]{:S(2)}) copy-start(f32[1024]{0:T(1024)} %param.22) | copy-start | bytes 12292
Sparse Core Ops, SparseCore 0:
  31.8 57.3 all-gather.1

commit v7 on v6

--- a/solution.py
+++ b/solution.py
@@ -20,7 +20,7 @@
 MIB = 1024 * 1024
 VMEM_LIMIT = 48 * MIB
 VMEM_WHOLE = 63 * MIB
-VMEM_MOST = 52 * MIB
+VMEM_SMALL = 24 * MIB
 
 QKV = 0
 OUT = 1536
@@ -98,32 +98,36 @@
     return [halves[:, side].reshape(WIDTH, D // 2).astype(BF16) for side in range(2)]
 
 
+def norm_kernel(core_ref, tokens_ref, gain_ref, own_ref, other_ref):
+    normed = layer_norm(tokens_ref[...].astype(F32), gain_ref[...]).astype(BF16)
+    for half, target in enumerate((own_ref, other_ref)):
+        core = core_ref[0] if half == 0 else 1 - core_ref[0]
+        row = lax.broadcasted_iota(jnp.int32, (D, D // 2), 0)
+        column = lax.broadcasted_iota(jnp.int32, (D, D // 2), 1)
+        pick = row == (column // 16) * 32 + core * 16 + column % 16
+        target[...] = dot(normed, pick.astype(BF16)).astype(BF16)
+
+
+def own_kernel(normed_ref, own_ref, part_ref):
+    part_ref[...] = dot(
+        normed_ref[...], own_ref[:, :, QKV : QKV + 3 * WIDTH].reshape(D // 2, 3 * WIDTH)
+    )
+
+
 def spatial_kernel(
-    core_ref, tokens_ref, gain_ref, own_ref, other_ref, spatial_ref, qkv, outs, packed, mixed, sems
-):
-    core = core_ref[0]
-    copies = []
-    for half, (ref, place) in enumerate(((own_ref, core), (other_ref, 1 - core))):
-        for part, (first, target) in enumerate(((QKV, qkv), (OUT, outs))):
-            copies.append(
-                pltpu.make_async_copy(
-                    ref.at[:, :, first : first + target.shape[-1]],
-                    target.at[:, place],
-                    sems.at[2 * half + part],
-                )
-            )
-    for copy in copies:
-        copy.start()
-    tokens = tokens_ref[...].astype(F32)
-    normed = layer_norm(tokens, gain_ref[...]).astype(BF16)
-    copies[0].wait()
-    copies[2].wait()
-    packed[...] = dot(normed, qkv[...].reshape(D, 3 * WIDTH)).astype(BF16)
+    core_ref, tokens_ref, normed_ref, part_ref, own_ref, other_ref, spatial_ref, packed, mixed
+):
+    other = other_ref[:, :, QKV : QKV + 3 * WIDTH].reshape(D // 2, 3 * WIDTH)
+    packed[...] = (part_ref[...] + dot(normed_ref[...], other)).astype(BF16)
     attend(packed, mixed, None)
-    copies[1].wait()
-    copies[3].wait()
-    for side, weight in enumerate(out_halves(outs[...])):
+    halves = (X * Y, 2, 8, D // 2)
+    own = own_ref[:, :, OUT : OUT + D // 2].astype(F32).reshape(halves)
+    other = other_ref[:, :, OUT : OUT + D // 2].astype(F32).reshape(halves)
+    first = core_ref[0] == 0
+    outs = jnp.stack([jnp.where(first, own, other), jnp.where(first, other, own)], axis=1)
+    for side in range(2):
         columns = slice(side * (D // 2), (side + 1) * (D // 2))
+        weight = outs[:, :, side].reshape(WIDTH, D // 2).astype(BF16)
         spatial_ref[:, columns] = (
             tokens_ref[:, columns].astype(F32) + dot(mixed[...], weight)
         ).astype(BF16)
@@ -214,10 +218,11 @@
 
 
 def text_kernel(
-    gain_ref, weights_ref, pool_ref, mapped_ref, weight_ref, gathered, sems
-):
-    copies = gather_rows(weights_ref, W_TEXT, gathered, sems)
-    for copy in copies:
+    gain_ref, weights_ref, pool_ref, mapped_ref, weight_ref, video_ref, gathered, sems
+):
+    copies = gather_rows(weights_ref, W_TEXT, gathered, sems.at[0])
+    copies_video = gather_rows(weights_ref, W_VIDEO, video_ref, sems.at[1])
+    for copy in copies + copies_video:
         copy.start()
     for copy in copies:
         copy.wait()
@@ -233,6 +238,8 @@
     pool = dot(pick, packed)
     pool_ref[...] = pool
     mapped_ref[...] = exact(dot, layer_norm(pool, gain_ref[...]), weight)
+    for copy in copies_video:
+        copy.wait()
 
 
 def unit_rows(values):
@@ -264,29 +271,20 @@
     text_weight_ref,
     gain_video_ref,
     gain_text_ref,
-    weights_ref,
+    video_weight_ref,
     video_loss_ref,
     text_loss_ref,
     grad_pooled_ref,
     grad_text_ref,
-    gathered,
-    text_weight,
     pooled_all,
-    sems,
 ):
     me = place_ref[0]
-    copies = gather_rows(weights_ref, W_VIDEO, gathered, sems)
-    copy_text = pltpu.make_async_copy(text_weight_ref, text_weight, sems.at[2 * Y])
-    for copy in copies + [copy_text]:
-        copy.start()
     scale = scale_ref[0]
     for chunk in range(D // 128):
         pooled_all[:, chunk * 128 : (chunk + 1) * 128] = pooled_ref[:, chunk, :]
     gain = gain_video_ref[...]
     normed = layer_norm(pooled_all[...], gain)
-    for copy in copies:
-        copy.wait()
-    weight = gathered[...].reshape(D, E)
+    weight = video_weight_ref[...].reshape(D, E)
     mapped = exact(dot, normed, weight)
     video = unit_rows(mapped)
     text_mapped = text_mapped_ref[...]
@@ -324,12 +322,11 @@
     mine_text_pool = jnp.sum(jnp.where(mine_row, text_pool_ref[...], 0.0), axis=0, keepdims=True)
     back = exact_row(dot_t, unit_back(mine_mapped, grad_video), weight)
     grad_pooled_ref[...] = norm_back(mine_pooled, gain, back)
-    copy_text.wait()
-    back = exact_row(dot_t, unit_back(mine_text_mapped, grad_caption), text_weight[...])
+    back = exact_row(dot_t, unit_back(mine_text_mapped, grad_caption), text_weight_ref[...])
     grad_text_ref[...] = norm_back(mine_text_pool, gain_text_ref[...], back)
 
 
-def call(kernel, out_shape, in_spaces, scratch, out_spaces=None, vmem=VMEM_LIMIT):
+def call(kernel, out_shape, in_spaces, scratch, out_spaces=None, vmem=VMEM_LIMIT, flops=0):
     many = isinstance(out_shape, (tuple, list))
     out_spaces = out_spaces or ([pltpu.VMEM] * (len(out_shape) if many else 1))
     out_specs = [pl.BlockSpec(memory_space=space) for space in out_spaces]
@@ -340,6 +337,7 @@
         out_specs=out_specs if many else out_specs[0],
         scratch_shapes=scratch,
         compiler_params=pltpu.CompilerParams(vmem_limit_bytes=vmem),
+        cost_estimate=pl.CostEstimate(flops=flops, bytes_accessed=0, transcendentals=0),
     )
 
 
@@ -404,20 +402,23 @@
     weights = gather(packed, axis_index_groups=ROWS_OF_YC).reshape(Y, 2, X, 16, PACKED_T)
     own = jnp.broadcast_to(own.reshape(1, Y * 16, PACKED_S), (X, Y * 16, PACKED_S))
     own = send_all(own, ROWS_OF_X).reshape(X * Y, 16, PACKED_S)
+
+    core = place % 2
+    normed = call(
+        norm_kernel, (shape((256, D // 2), BF16),) * 2, (S, V, V), [], flops=1 << 30
+    )(core, tokens, gain_spatial.reshape(1, D))
+    own, normed = barrier((own, normed))
     other = lax.ppermute(own, "dp", OTHER_CORE)
-
+    part = call(own_kernel, shape((256, 3 * WIDTH), F32), (V, V), [], vmem=VMEM_SMALL, flops=1 << 30)(
+        normed[0], own
+    )
     spatial = call(
         spatial_kernel,
         shape((256, D), BF16),
-        (S, V, V, A, A),
-        [
-            pltpu.VMEM((X * Y, 2, 16, 3 * WIDTH), BF16),
-            pltpu.VMEM((X * Y, 2, 16, D // 2), BF16),
-            pltpu.VMEM((256, 3 * WIDTH), BF16),
-            pltpu.VMEM((256, WIDTH), BF16),
-            DMA((4,)),
-        ],
-    )(place % 2, tokens, gain_spatial.reshape(1, D), own, other)
+        (S, V, V, V, V, V),
+        [pltpu.VMEM((256, 3 * WIDTH), BF16), pltpu.VMEM((256, WIDTH), BF16)],
+        vmem=VMEM_SMALL,
+    )(core, tokens, normed[1], part, own, other)
     spatial = lax.all_to_all(spatial.reshape(FRAMES, 32, D), "frame", 0, 0, tiled=True)
     layer_out, pool = call(
         temporal_kernel,
@@ -431,11 +432,16 @@
             DMA((2, 2 * Y)),
         ],
     )(spatial.reshape(256, D), gain_temporal.reshape(1, D), weights)
-    text_pool, text_mapped, text_weight = call(
+    text_pool, text_mapped, text_weight, video_weight = call(
         text_kernel,
-        (shape((64, DT), F32), shape((64, E), F32), shape((DT, E), BF16)),
+        (
+            shape((64, DT), F32),
+            shape((64, E), F32),
+            shape((DT, E), BF16),
+            shape(halves + (E,), BF16),
+        ),
         (V, A),
-        [pltpu.VMEM(halves + (E,), BF16), DMA((2 * Y,))],
+        [pltpu.VMEM(halves + (E,), BF16), DMA((2, 2 * Y))],
     )(gain_text.reshape(1, DT), weights)
     pool = lax.all_to_all(pool, "frame", 0, 0, tiled=True)
     pool = call(spread_kernel, shape((64, 8, 128), F32), (V,), [])(pool)
@@ -443,15 +449,10 @@
     video_loss, text_loss, grad_pooled, grad_text = call(
         loss_kernel,
         (shape((1,), F32), shape((1,), F32), shape((1, D), F32), shape((1, DT), F32)),
-        (S, S, V, V, V, V, A, V, V, A),
-        [
-            pltpu.VMEM(halves + (E,), BF16),
-            pltpu.VMEM((DT, E), BF16),
-            pltpu.VMEM((64, D), F32),
-            DMA((2 * Y + 1,)),
-        ],
+        (S, S, V, V, V, V, V, V, V, V),
+        [pltpu.VMEM((64, D), F32)],
         (S, S, V, V),
-        vmem=VMEM_MOST,
+        vmem=VMEM_SMALL,
     )(
         place,
         logit_scale,
@@ -462,7 +463,7 @@
         text_weight,
         gain_video.reshape(1, D),
         gain_text.reshape(1, DT),
-        weights,
+        video_weight,
     )
     return (layer_out.reshape(1, 8, 32, D), video_loss, text_loss, grad_pooled, grad_text)
 

time: 151 us -> 148 us (0.980)
  blocking collectives: 82.6 us -> 49 us
  waiting for transfers between devices: 12.9 us -> 36.5 us
  starting transfers between devices: 17.2 us -> 25.6 us
  Pallas kernels: 22.2 us -> 20.1 us
    all_to_all x1 -> x0, blocking collectives: 32.5 us -> none  [send_all(): lax.all_to_all(copies, 'dp', 0, 0, tiled=True, axis_index_groups=groups)]
    all_to_all x1 -> x2, waiting for transfers between devices: 1.94 us -> 26.5 us  [send_all(): lax.all_to_all(copies, 'dp', 0, 0, tiled=True, axis_index_groups=groups)]
    all_to_all x1 -> x2, starting transfers between devices: 7.66 us -> 15 us  [send_all(): lax.all_to_all(copies, 'dp', 0, 0, tiled=True, axis_index_groups=groups)]
    pallas_call x1, Pallas kernels: 4.84 us -> 3.26 us  [on_device(): call(loss_kernel, (shape((1,), F32), shape((1,), F32), shape((1, D), F32)...]
    pallas_call x1 -> x3, Pallas kernels: 4.53 us -> 3.88 us  [the longest x1 2.18 us: on_device(): call(spatial_kernel, shape((256, D), BF16), (S, V, V, V, V, V), [pltpu.VM...]
  transfers between devices with their start and end apart: 4 -> 5, of which waited for: 3 -> 4; matrix products, arithmetic and copies ran while one was open for 0% -> 1% of each run, Pallas kernels for 6% -> 6%
where the time goes in v7:
time: 148 us
  blocking collectives  49 us (33%)
  waiting for transfers between devices  36.5 us (25%)
  starting transfers between devices  25.6 us (17%)
  Pallas kernels  20.1 us (14%)
  between operations  14.8 us (10%)
  local copies, waits for them, and re-layouts  1.81 us (1%)
    all_to_all x1, blocking collectives, on_device(): lax.all_to_all(spatial.reshape(FRAMES, 32, D), 'frame', 0, 0, tiled=True)  27 us
    all_to_all x2, waiting for transfers between devices, send_all(): lax.all_to_all(copies, 'dp', 0, 0, tiled=True, axis_index_groups=groups)  26.5 us
    all_to_all x2, starting transfers between devices, send_all(): lax.all_to_all(copies, 'dp', 0, 0, tiled=True, axis_index_groups=groups)  15 us
    all_gather x1, blocking collectives, on_device(): packed = gather(packed, axis_index_groups=ROWS_OF_X)  12.8 us
    all_to_all x1, blocking collectives, on_device(): pool = lax.all_to_all(pool, 'frame', 0, 0, tiled=True)  9.25 us
    all_to_all x1, starting transfers between devices, on_device(): pooled = lax.all_to_all(pool, 'dp', 0, 0, tiled=True)  6.94 us
    all_to_all x1, waiting for transfers between devices, on_device(): pooled = lax.all_to_all(pool, 'dp', 0, 0, tiled=True)  6.83 us
    pallas_call x1, Pallas kernels, on_device(): call(temporal_kernel, (shape((256, D), BF16), shape((FRAMES, 8, 128), F32...  5.77 us
  transfers between devices with their start and end apart: 5, of which 4 were waited for; matrix products, arithmetic and copies ran while one was open for 1% of the time, Pallas kernels for 6%

profile of v7, /device:TPU:1, one launch (start us, length us, event | category | flops | bytes accessed | tf_op | source)
XLA Modules:
  0.0 147.8 jit_solution(4985543726036473861)
XLA Ops:
  7.2 2.1 %shard_map.182 = (bf16[16,3584]{1,0:T(8,128)(2,1)}, bf16[8,16,2048]{2,1,0:T(8,128)(2,1)}) custom-call(s32[1,77]{1,0:T(1,128)} %ids_ref.1, bf16[77,768]{1,0:T(8,128)(2,1)} %bitcast.26, bf16[16,1536]{1,0:T(8,128)(2,1)} %qkv_ref.1, bf16[12,768]{1,0:T(8,128)(2,1)} %text_ref.1, bf16[8,1024]{1,0:T(8,128)(2,1)} %out_s_ref.1, bf16[8,1024]{1,0:T(8,128)(2,1)} %out_t_ref.1, ...), custom_call_target="tpu_custom_call" | custom-call | tf_op jit(solution)/shard_map/pallas_call | solution.py:374
  9.3 7.7 %all-to-all-start = ((bf16[8,16,2048]{2,1,0:T(8,128)(2,1)}), bf16[8,16,2048]{2,1,0:T(8,128)(2,1)S(1)}, u32[]{:S(2)}, u32[]{:S(2)}) async-start(bf16[8,16,2048]{2,1,0:T(8,128)(2,1)} %get-tuple-element.24), calls=%async_computation | async-start | bytes 1048576 | tf_op jit(solution)/shard_map/all_to_all | solution.py:349
  16.9 0.0 all-gather.2.cloned.1.call-start
  17.0 12.8 %all_gather.6 = bf16[64,3584]{1,0:T(8,128)(2,1)} all-gather(bf16[16,3584]{1,0:T(8,128)(2,1)} %get-tuple-element.25), channel_id=1, replica_groups={{0,128,256,384},{8,136,264,392},{16,144,272,400},{24,152,280,408},{32,1..., dimensions={0}, use_global_device_ids=true | all-gather | bytes 573440 | tf_op jit(solution)/shard_map/all_gather | solution.py:400
  29.7 2.0 %all-to-all-done = bf16[8,16,2048]{2,1,0:T(8,128)(2,1)S(1)} async-done(((bf16[8,16,2048]{2,1,0:T(8,128)(2,1)}), bf16[8,16,2048]{2,1,0:T(8,128)(2,1)S(1)}, u32[]{:S(2)}, u32[]{:S(2)}) %all-to-all-start) | async-done | bytes 524320 | tf_op jit(solution)/shard_map/all_to_all | solution.py:349
  31.7 0.0 all-gather.2.cloned.1.call-update
  31.7 1.7 %broadcast_in_dim.8 = bf16[4,128,2048]{2,1,0:T(8,128)(2,1)} broadcast(bf16[128,2048]{1,0:T(8,128)(2,1)S(1)} %bitcast.25), dimensions={1,2} | broadcast | bytes 2621440 | tf_op jit(solution)/shard_map/broadcast_in_dim | solution.py:403
  33.4 0.0 copy-start
  33.4 0.0 copy-start.3
  33.4 7.4 %all-to-all-start.1 = ((bf16[4,128,2048]{2,1,0:T(8,128)(2,1)}), bf16[4,128,2048]{2,1,0:T(8,128)(2,1)S(1)}, u32[]{:S(2)}, u32[]{:S(2)}) async-start(bf16[4,128,2048]{2,1,0:T(8,128)(2,1)} %broadcast_in_dim.8), calls=%async_computation.1 | async-start | bytes 4194304 | tf_op jit(solution)/shard_map/all_to_all | solution.py:349
  40.7 0.0 copy-done
  40.8 0.0 copy-done.3
  40.8 1.1 shard_map.183
  41.9 24.5 %all-to-all-done.1 = bf16[4,128,2048]{2,1,0:T(8,128)(2,1)S(1)} async-done(((bf16[4,128,2048]{2,1,0:T(8,128)(2,1)}), bf16[4,128,2048]{2,1,0:T(8,128)(2,1)S(1)}, u32[]{:S(2)}, u32[]{:S(2)}) %all-to-all-start.1) | async-done | bytes 2097184 | tf_op jit(solution)/shard_map/all_to_all | solution.py:349
  66.4 3.6 %collective-permute-start = (bf16[32,16,2048]{2,1,0:T(8,128)(2,1)S(1)}, bf16[32,16,2048]{2,1,0:T(8,128)(2,1)S(1)}, u32[]{:S(2)}, u32[]{:S(2)}) collective-permute-start(bf16[32,16,2048]{2,1,0:T(8,128)(2,1)S(1)} %bitcast.13), channel_id=1, source_target_pairs={{0,8},{8,0},{16,24},{24,16},{32,40},{40,32},{48,56},{56,48},{64,72... | collective-permute-start | bytes 6291464 | tf_op jit(solution)/shard_map/ppermute | solution.py:411
  69.9 0.6 shard_map.184.part_ref
  70.5 0.0 copy-start.1
  70.5 3.2 %collective-permute-done.other_ref = bf16[32,16,2048]{2,1,0:T(8,128)(2,1)S(1)} collective-permute-done((bf16[32,16,2048]{2,1,0:T(8,128)(2,1)S(1)}, bf16[32,16,2048]{2,1,0:T(8,128)(2,1)S(1)}, u32[]{:S(2)}, u32[]{:S(2)}) %collective-permute-start) | collective-permute-done | bytes 2097184 | tf_op jit(solution)/shard_map/ppermute | solution.py:411
  73.7 2.2 %shard_map.185 = bf16[256,1024]{1,0:T(8,128)(2,1)S(1)} custom-call(s32[1]{0:T(128)S(6)} %select_n.7.core_ref, bf16[256,1024]{1,0:T(8,128)(2,1)S(1)} %bitcast.19, bf16[256,512]{1,0:T(8,128)(2,1)S(1)} %get-tuple-element.29.normed_ref, f32[256,1536]{1,0:T(8,128)S(1)} %shard_map.184.part_ref, bf16[32,16,2048]{2,1,0:T(8,128)(2,1)S(1)} %bitcast.15, ...), custom_call_target="tpu_custom_call" | custom-call | tf_op jit(solution)/shard_map/pallas_call | solution.py:415
  75.9 27.0 %all_to_all.25 = bf16[8,32,1024]{2,1,0:T(8,128)(2,1)S(1)} all-to-all(bf16[8,32,1024]{2,1,0:T(8,128)(2,1)S(1)} %bitcast.16), channel_id=1, replica_groups=mesh['dp'=64,'frame'=8] {'frame'}, dimensions={0} | all-to-all | bytes 1048576 | tf_op jit(solution)/shard_map/all_to_all | solution.py:422
  102.9 0.0 all-gather.2.cloned.1.call-done
  102.9 0.0 copy-done.1
  102.9 0.0 copy-start.4
  102.9 0.0 copy-start.5
  102.9 5.8 %shard_map.186 = (bf16[256,1024]{1,0:T(8,128)(2,1)}, f32[8,8,128]{2,1,0:T(8,128)S(1)}) custom-call(bf16[256,1024]{1,0:T(8,128)(2,1)S(1)} %bitcast.17, f32[1,1024]{1,0:T(1,128)S(1)} %bitcast.20, bf16[8,2,4,16,3584]{4,3,2,1,0:T(8,128)(2,1)} %bitcast.23), custom_call_target="tpu_custom_call" | custom-call | tf_op jit(solution)/shard_map/pallas_call | solution.py:423
  108.7 9.2 %all_to_all.26.parts_ref = f32[8,8,128]{2,1,0:T(8,128)S(1)} all-to-all(f32[8,8,128]{2,1,0:T(8,128)S(1)} %get-tuple-element.34), channel_id=1, replica_groups=mesh['dp'=64,'frame'=8] {'frame'}, dimensions={0} | all-to-all | bytes 65536 | tf_op jit(solution)/shard_map/all_to_all | solution.py:446
  118.0 0.7 shard_map.187
  118.7 6.9 %all-to-all-start.4 = ((f32[64,8,128]{2,1,0:T(8,128)}), f32[64,8,128]{2,1,0:T(8,128)S(1)}, u32[]{:S(2)}, u32[]{:S(2)}) async-start(f32[64,8,128]{2,1,0:T(8,128)} %shard_map.187), calls=%async_computation.4 | async-start | bytes 524288 | tf_op jit(solution)/shard_map/all_to_all | solution.py:448
  125.6 0.0 copy-done.4
  125.7 0.0 copy-done.5
  125.7 0.1 copy.20.pairs_ref
  126.4 0.0 copy-start.2
  126.4 4.4 %shard_map.188 = (f32[64,768]{1,0:T(8,128)S(1)}, f32[64,768]{1,0:T(8,128)S(1)}, bf16[768,768]{1,0:T(8,128)(2,1)S(1)}, bf16[4,8,2,16,768]{4,3,2,1,0:T(8,128)(2,1)S(1)}) custom-call(f32[1,768]{1,0:T(1,128)S(1)} %reshape.65.gain_ref.gain_text_ref, bf16[8,2,4,16,3584]{4,3,2,1,0:T(8,128)(2,1)} %bitcast.24), custom_call_target="tpu_custom_call" | custom-call | tf_op jit(solution)/shard_map/pallas_call | solution.py:435
  130.8 6.8 %all-to-all-done.4.pooled_ref = f32[64,8,128]{2,1,0:T(8,128)S(1)} async-done(((f32[64,8,128]{2,1,0:T(8,128)}), f32[64,8,128]{2,1,0:T(8,128)S(1)}, u32[]{:S(2)}, u32[]{:S(2)}) %all-to-all-start.4) | async-done | bytes 262176 | tf_op jit(solution)/shard_map/all_to_all | solution.py:448
  137.7 0.0 copy-done.2
  137.7 3.3 %shard_map.189 = (f32[1]{0:T(128)}, f32[1]{0:T(128)}, f32[1,1024]{1,0:T(1,128)}, f32[1,768]{1,0:T(1,128)}) custom-call(s32[1]{0:T(128)} %bitcast.place_ref, f32[1]{0:T(128)S(6)} %copy.21.scale_ref, s32[64,1]{1,0:T(8,128)S(1)} %copy.20.pairs_ref, f32[64,8,128]{2,1,0:T(8,128)S(1)} %all-to-all-done.4.pooled_ref, f32[64,768]{1,0:T(8,128)S(1)} %get-tuple-element.35.text_pool_ref, ...), custom_call_target="tpu_custom_call" | custom-call | tf_op jit(solution)/shard_map/pallas_call | solution.py:449
  (1 shorter events, 0.0 us)
Async XLA Ops:
  9.3 22.4 %all-to-all-start = ((bf16[8,16,2048]{2,1,0:T(8,128)(2,1)}), bf16[8,16,2048]{2,1,0:T(8,128)(2,1)S(1)}, u32[]{:S(2)}, u32[]{:S(2)}) async-start(bf16[8,16,2048]{2,1,0:T(8,128)(2,1)} %get-tuple-element.24), calls=%async_computation | async-start | bytes 1048576 | tf_op jit(solution)/shard_map/all_to_all | solution.py:349
  16.9 86.0 %all-gather.2.cloned.1.call-start = ((), (), s32[]{:S(2)}) async-start(), calls=%async_computation.5 | async-start | bytes 7798784 | tf_op jit(solution)/shard_map/all_gather | solution.py:402
  33.4 7.4 %copy-start = (bf16[1,1,256,1024]{3,2,1,0:T(8,128)(2,1)S(1)}, bf16[1,1,256,1024]{3,2,1,0:T(8,128)(2,1)}, u32[]{:S(2)}) copy-start(bf16[1,1,256,1024]{3,2,1,0:T(8,128)(2,1)} %param.15) | copy-start | bytes 1572868
  33.4 7.4 %copy-start.3 = (f32[1024]{0:T(1024)S(1)}, f32[1024]{0:T(1024)}, u32[]{:S(2)}) copy-start(f32[1024]{0:T(1024)} %param.20) | copy-start | bytes 12292
  33.4 33.0 %all-to-all-start.1 = ((bf16[4,128,2048]{2,1,0:T(8,128)(2,1)}), bf16[4,128,2048]{2,1,0:T(8,128)(2,1)S(1)}, u32[]{:S(2)}, u32[]{:S(2)}) async-start(bf16[4,128,2048]{2,1,0:T(8,128)(2,1)} %broadcast_in_dim.8), calls=%async_computation.1 | async-start | bytes 4194304 | tf_op jit(solution)/shard_map/all_to_all | solution.py:349
  66.4 7.4 %collective-permute-start = (bf16[32,16,2048]{2,1,0:T(8,128)(2,1)S(1)}, bf16[32,16,2048]{2,1,0:T(8,128)(2,1)S(1)}, u32[]{:S(2)}, u32[]{:S(2)}) collective-permute-start(bf16[32,16,2048]{2,1,0:T(8,128)(2,1)S(1)} %bitcast.13), channel_id=1, source_target_pairs={{0,8},{8,0},{16,24},{24,16},{32,40},{40,32},{48,56},{56,48},{64,72... | collective-permute-start | bytes 6291464 | tf_op jit(solution)/shard_map/ppermute | solution.py:411
  70.5 32.4 %copy-start.1 = (f32[1024]{0:T(1024)S(1)}, f32[1024]{0:T(1024)}, u32[]{:S(2)}) copy-start(f32[1024]{0:T(1024)} %param.21) | copy-start | bytes 12292
  102.9 22.7 %copy-start.4 = (f32[768]{0:T(1024)S(1)}, f32[768]{0:T(1024)}, u32[]{:S(2)}) copy-start(f32[768]{0:T(1024)} %param.23) | copy-start | bytes 9220
  102.9 22.7 %copy-start.5 = (s32[64]{0:T(128)S(1)}, s32[64]{0:T(128)}, u32[]{:S(2)}) copy-start(s32[64]{0:T(128)} %param.18) | copy-start | bytes 772
  118.7 19.0 %all-to-all-start.4 = ((f32[64,8,128]{2,1,0:T(8,128)}), f32[64,8,128]{2,1,0:T(8,128)S(1)}, u32[]{:S(2)}, u32[]{:S(2)}) async-start(f32[64,8,128]{2,1,0:T(8,128)} %shard_map.187), calls=%async_computation.4 | async-start | bytes 524288 | tf_op jit(solution)/shard_map/all_to_all | solution.py:448
  126.4 11.2 %copy-start.2 = (f32[1024]{0:T(1024)S(1)}, f32[1024]{0:T(1024)}, u32[]{:S(2)}) copy-start(f32[1024]{0:T(1024)} %param.22) | copy-start | bytes 12292
Sparse Core Ops, SparseCore 0:
  31.8 57.3 all-gather.1

commit v8 on v7

--- a/solution.py
+++ b/solution.py
@@ -34,6 +34,10 @@
 ROWS_OF_Y = [[(x * Y + y) * 2 + c for y in range(Y)] for x in range(X) for c in range(2)]
 ROWS_OF_YC = [[(x * Y + y) * 2 + c for y in range(Y) for c in range(2)] for x in range(X)]
 OTHER_CORE = [(i, i ^ 1) for i in range(2 * X * Y)]
+X_UP = [(i, (i + 2 * Y) % (2 * X * Y)) for i in range(2 * X * Y)]
+X_DOWN = [(i, (i - 2 * Y) % (2 * X * Y)) for i in range(2 * X * Y)]
+STEPS = (0, X - 1, 1, 2)
+BLOCK = Y * 16
 FRAMES = 8
 
 
@@ -98,38 +102,55 @@
     return [halves[:, side].reshape(WIDTH, D // 2).astype(BF16) for side in range(2)]
 
 
-def norm_kernel(core_ref, tokens_ref, gain_ref, own_ref, other_ref):
+def sorted_rows(place_ref, half, depth, column):
+    block = column // (Y * depth)
+    step = jnp.zeros_like(block)
+    for number, value in enumerate(STEPS):
+        step = jnp.where(block == number, value, step)
+    x = (place_ref[0] + step) % X
+    core = place_ref[1] if half == 0 else 1 - place_ref[1]
+    y = column // depth % Y
+    return ((x * Y + y) * 2 + core) * depth + column % depth
+
+
+def norm_kernel(place_ref, tokens_ref, gain_ref, own_ref, other_ref, pick_ref):
     normed = layer_norm(tokens_ref[...].astype(F32), gain_ref[...]).astype(BF16)
     for half, target in enumerate((own_ref, other_ref)):
-        core = core_ref[0] if half == 0 else 1 - core_ref[0]
         row = lax.broadcasted_iota(jnp.int32, (D, D // 2), 0)
         column = lax.broadcasted_iota(jnp.int32, (D, D // 2), 1)
-        pick = row == (column // 16) * 32 + core * 16 + column % 16
+        pick = row == sorted_rows(place_ref, half, 16, column)
         target[...] = dot(normed, pick.astype(BF16)).astype(BF16)
-
-
-def own_kernel(normed_ref, own_ref, part_ref):
-    part_ref[...] = dot(
-        normed_ref[...], own_ref[:, :, QKV : QKV + 3 * WIDTH].reshape(D // 2, 3 * WIDTH)
-    )
-
-
-def spatial_kernel(
-    core_ref, tokens_ref, normed_ref, part_ref, own_ref, other_ref, spatial_ref, packed, mixed
-):
-    other = other_ref[:, :, QKV : QKV + 3 * WIDTH].reshape(D // 2, 3 * WIDTH)
-    packed[...] = (part_ref[...] + dot(normed_ref[...], other)).astype(BF16)
+        row = lax.broadcasted_iota(jnp.int32, (WIDTH, WIDTH // 2), 0)
+        column = lax.broadcasted_iota(jnp.int32, (WIDTH, WIDTH // 2), 1)
+        pick = row == sorted_rows(place_ref, half, 8, column)
+        pick_ref[:, half * (WIDTH // 2) : (half + 1) * (WIDTH // 2)] = pick.astype(BF16)
+
+
+def blocks_product(normed_refs, first, block_refs):
+    total, starts = None, [first, first]
+    for number, ref in enumerate(block_refs):
+        half, depth = number % 2, ref.shape[0]
+        rows = slice(starts[half], starts[half] + depth)
+        starts[half] += depth
+        part = dot(normed_refs[half][:, rows], ref[:, QKV : QKV + 3 * WIDTH])
+        total = part if total is None else total + part
+    return total
+
+
+def spatial_kernel(tokens_ref, own_ref, other_ref, pick_ref, *rest):
+    block_refs, (spatial_ref, packed, mixed) = rest[:-3], rest[-3:]
+    packed[...] = blocks_product((own_ref, other_ref), 0, block_refs).astype(BF16)
     attend(packed, mixed, None)
-    halves = (X * Y, 2, 8, D // 2)
-    own = own_ref[:, :, OUT : OUT + D // 2].astype(F32).reshape(halves)
-    other = other_ref[:, :, OUT : OUT + D // 2].astype(F32).reshape(halves)
-    first = core_ref[0] == 0
-    outs = jnp.stack([jnp.where(first, own, other), jnp.where(first, other, own)], axis=1)
+    sorted_mixed = dot(mixed[...], pick_ref[...]).astype(BF16)
+    halves = [
+        ref[:, OUT : OUT + D // 2].astype(F32).reshape(ref.shape[0] // 16, 2, 8, D // 2)
+        for ref in block_refs[0::2] + block_refs[1::2]
+    ]
     for side in range(2):
         columns = slice(side * (D // 2), (side + 1) * (D // 2))
-        weight = outs[:, :, side].reshape(WIDTH, D // 2).astype(BF16)
+        weight = jnp.concatenate([half[:, side].reshape(-1, D // 2) for half in halves], axis=0)
         spatial_ref[:, columns] = (
-            tokens_ref[:, columns].astype(F32) + dot(mixed[...], weight)
+            tokens_ref[:, columns].astype(F32) + dot(sorted_mixed, weight.astype(BF16))
         ).astype(BF16)
 
 
@@ -400,25 +421,34 @@
     packed = gather(packed, axis_index_groups=ROWS_OF_X)
     own, packed = barrier((own, packed))
     weights = gather(packed, axis_index_groups=ROWS_OF_YC).reshape(Y, 2, X, 16, PACKED_T)
-    own = jnp.broadcast_to(own.reshape(1, Y * 16, PACKED_S), (X, Y * 16, PACKED_S))
-    own = send_all(own, ROWS_OF_X).reshape(X * Y, 16, PACKED_S)
-
-    core = place % 2
-    normed = call(
-        norm_kernel, (shape((256, D // 2), BF16),) * 2, (S, V, V), [], flops=1 << 30
-    )(core, tokens, gain_spatial.reshape(1, D))
-    own, normed = barrier((own, normed))
-    other = lax.ppermute(own, "dp", OTHER_CORE)
-    part = call(own_kernel, shape((256, 3 * WIDTH), F32), (V, V), [], vmem=VMEM_SMALL, flops=1 << 30)(
-        normed[0], own
-    )
+    permute = functools.partial(lax.ppermute, axis_name="dp")
+    mine, late_tokens = barrier((own.reshape(BLOCK, PACKED_S), tokens))
+    below, above = permute(mine, perm=X_UP), permute(mine, perm=X_DOWN)
+    mine_other = permute(mine, perm=OTHER_CORE)
+    where = jnp.concatenate([place // (2 * Y), place % 2])
+    *normed, pick = call(
+        norm_kernel,
+        (shape((256, D // 2), BF16),) * 2 + (shape((WIDTH, WIDTH), BF16),),
+        (S, V, V),
+        [],
+        flops=1 << 30,
+    )(where, late_tokens, gain_spatial.reshape(1, D))
+    below, above, low, high, normed, pick = barrier(
+        (below, above, below[: BLOCK // 2], above[BLOCK // 2 :], normed, pick)
+    )
+    low, high = permute(low, perm=X_UP), permute(high, perm=X_DOWN)
+    near, far = [mine, mine_other], []
+    for block in (below, above):
+        near += [block, permute(block, perm=OTHER_CORE)]
+    for block in (low, high):
+        far += [block, permute(block, perm=OTHER_CORE)]
     spatial = call(
         spatial_kernel,
         shape((256, D), BF16),
-        (S, V, V, V, V, V),
+        (V,) * 14,
         [pltpu.VMEM((256, 3 * WIDTH), BF16), pltpu.VMEM((256, WIDTH), BF16)],
         vmem=VMEM_SMALL,
-    )(core, tokens, normed[1], part, own, other)
+    )(tokens, *normed, pick, *near, *far)
     spatial = lax.all_to_all(spatial.reshape(FRAMES, 32, D), "frame", 0, 0, tiled=True)
     layer_out, pool = call(
         temporal_kernel,

time: 148 us -> 147 us (level)
  waiting for transfers between devices: 36.5 us -> 16.8 us
  starting transfers between devices: 25.6 us -> 42.9 us
  Pallas kernels: 20.1 us -> 22 us
  local copies, waits for them, and re-layouts: 1.81 us -> 0.16 us
    ppermute x1 -> x9, starting transfers between devices: 3.56 us -> 29.4 us  [the longest x2 9.52 us: on_device(): below, above = (permute(mine, perm=X_UP), permute(mine, perm=X_DOWN))]
    all_to_all x2 -> x1, waiting for transfers between devices: 26.5 us -> 1.95 us  [send_all(): lax.all_to_all(copies, 'dp', 0, 0, tiled=True, axis_index_groups=groups)]
    all_to_all x2 -> x1, starting transfers between devices: 15 us -> 7.66 us  [send_all(): lax.all_to_all(copies, 'dp', 0, 0, tiled=True, axis_index_groups=groups)]
    ppermute x1 -> x9, waiting for transfers between devices: 3.19 us -> 8.04 us  [the longest x2 6.46 us: on_device(): below, above = (permute(mine, perm=X_UP), permute(mine, perm=X_DOWN))]
    pallas_call x3 -> x2, Pallas kernels: 3.88 us -> 5.71 us  [the longest x1 3.99 us: on_device(): call(spatial_kernel, shape((256, D), BF16), (V,) * 14, [pltpu.VMEM((256,...]
    broadcast_in_dim x1 -> x0, local copies, waits for them, and re-layouts: 1.69 us -> none  [on_device(): jnp.broadcast_to(own.reshape(1, Y * 16, PACKED_S), (X, Y * 16, PACKED_S))]
  transfers between devices with their start and end apart: 5 -> 12, of which waited for: 4 -> 5; matrix products, arithmetic and copies ran while one was open for 1% -> 0% of each run, Pallas kernels for 6% -> 7%
where the time goes in v8:
time: 147 us
  blocking collectives  49.8 us (34%)
  starting transfers between devices  42.9 us (29%)
  Pallas kernels  22 us (15%)
  waiting for transfers between devices  16.8 us (11%)
  between operations  15 us (10%)
    all_to_all x1, blocking collectives, on_device(): lax.all_to_all(spatial.reshape(FRAMES, 32, D), 'frame', 0, 0, tiled=True)  27.8 us
    all_gather x1, blocking collectives, on_device(): packed = gather(packed, axis_index_groups=ROWS_OF_X)  12.8 us
    ppermute x2, starting transfers between devices, on_device(): below, above = (permute(mine, perm=X_UP), permute(mine, perm=X_DOWN))  9.52 us
    all_to_all x1, blocking collectives, on_device(): pool = lax.all_to_all(pool, 'frame', 0, 0, tiled=True)  9.26 us
    all_to_all x1, starting transfers between devices, send_all(): lax.all_to_all(copies, 'dp', 0, 0, tiled=True, axis_index_groups=groups)  7.66 us
    all_to_all x1, waiting for transfers between devices, on_device(): pooled = lax.all_to_all(pool, 'dp', 0, 0, tiled=True)  6.83 us
    ppermute x2, starting transfers between devices, on_device(): low, high = (permute(low, perm=X_UP), permute(high, perm=X_DOWN))  6.49 us
    ppermute x2, waiting for transfers between devices, on_device(): below, above = (permute(mine, perm=X_UP), permute(mine, perm=X_DOWN))  6.46 us
  transfers between devices with their start and end apart: 12, of which 5 were waited for; matrix products, arithmetic and copies ran while one was open for 0% of the time, Pallas kernels for 7%

profile of v8, /device:TPU:1, one launch (start us, length us, event | category | flops | bytes accessed | tf_op | source)
XLA Modules:
  0.0 146.7 jit_solution(9273182774523321385)
XLA Ops:
  7.2 0.0 copy-start
  7.2 0.0 copy-start.3
  7.2 2.1 %shard_map.182 = (bf16[16,3584]{1,0:T(8,128)(2,1)}, bf16[8,16,2048]{2,1,0:T(8,128)(2,1)}) custom-call(s32[1,77]{1,0:T(1,128)} %ids_ref.1, bf16[77,768]{1,0:T(8,128)(2,1)} %bitcast.25, bf16[16,1536]{1,0:T(8,128)(2,1)} %qkv_ref.1, bf16[12,768]{1,0:T(8,128)(2,1)} %text_ref.1, bf16[8,1024]{1,0:T(8,128)(2,1)} %out_s_ref.1, bf16[8,1024]{1,0:T(8,128)(2,1)} %out_t_ref.1, ...), custom_call_target="tpu_custom_call" | custom-call | tf_op jit(solution)/shard_map/pallas_call | solution.py:395
  9.3 7.7 %all-to-all-start = ((bf16[8,16,2048]{2,1,0:T(8,128)(2,1)}), bf16[8,16,2048]{2,1,0:T(8,128)(2,1)S(1)}, u32[]{:S(2)}, u32[]{:S(2)}) async-start(bf16[8,16,2048]{2,1,0:T(8,128)(2,1)} %get-tuple-element.31), calls=%async_computation | async-start | bytes 1048576 | tf_op jit(solution)/shard_map/all_to_all | solution.py:370
  17.0 0.0 all-gather.2.cloned.1.call-start
  17.0 12.8 %all_gather.6 = bf16[64,3584]{1,0:T(8,128)(2,1)} all-gather(bf16[16,3584]{1,0:T(8,128)(2,1)} %get-tuple-element.32), channel_id=1, replica_groups={{0,128,256,384},{8,136,264,392},{16,144,272,400},{24,152,280,408},{32,1..., dimensions={0}, use_global_device_ids=true | all-gather | bytes 573440 | tf_op jit(solution)/shard_map/all_gather | solution.py:421
  29.8 2.0 %all-to-all-done = bf16[8,16,2048]{2,1,0:T(8,128)(2,1)S(1)} async-done(((bf16[8,16,2048]{2,1,0:T(8,128)(2,1)}), bf16[8,16,2048]{2,1,0:T(8,128)(2,1)S(1)}, u32[]{:S(2)}, u32[]{:S(2)}) %all-to-all-start) | async-done | bytes 524320 | tf_op jit(solution)/shard_map/all_to_all | solution.py:370
  31.7 0.0 all-gather.2.cloned.1.call-update
  31.8 6.3 %collective-permute-start = (bf16[128,2048]{1,0:T(8,128)(2,1)S(1)}, bf16[128,2048]{1,0:T(8,128)(2,1)S(1)}, u32[]{:S(2)}, u32[]{:S(2)}) collective-permute-start(bf16[128,2048]{1,0:T(8,128)(2,1)S(1)} %bitcast.12), channel_id=1, source_target_pairs={{0,128},{8,136},{16,144},{24,152},{32,160},{40,168},{48,176},{56,1... | collective-permute-start | bytes 1572872 | tf_op jit(solution)/shard_map/ppermute | solution.py:426
  38.1 3.2 %collective-permute-start.1 = (bf16[128,2048]{1,0:T(8,128)(2,1)S(1)}, bf16[128,2048]{1,0:T(8,128)(2,1)S(1)}, u32[]{:S(2)}, u32[]{:S(2)}) collective-permute-start(bf16[128,2048]{1,0:T(8,128)(2,1)S(1)} %bitcast.13), channel_id=1, source_target_pairs={{0,384},{8,392},{16,400},{24,408},{32,416},{40,424},{48,432},{56,4... | collective-permute-start | bytes 1572872 | tf_op jit(solution)/shard_map/ppermute | solution.py:426
  41.3 0.1 pad_add_fusion.place_ref
  41.4 3.1 %collective-permute-start.2 = (bf16[128,2048]{1,0:T(8,128)(2,1)S(1)}, bf16[128,2048]{1,0:T(8,128)(2,1)S(1)}, u32[]{:S(2)}, u32[]{:S(2)}) collective-permute-start(bf16[128,2048]{1,0:T(8,128)(2,1)S(1)} %bitcast.14), channel_id=1, source_target_pairs={{0,8},{8,0},{16,24},{24,16},{32,40},{40,32},{48,56},{56,48},{64,72... | collective-permute-start | bytes 1572872 | tf_op jit(solution)/shard_map/ppermute | solution.py:427
  44.5 0.0 copy-done
  44.6 0.0 copy-done.3
  44.6 1.7 %shard_map.183 = (bf16[256,512]{1,0:T(8,128)(2,1)S(1)}, bf16[256,512]{1,0:T(8,128)(2,1)S(1)}, bf16[512,512]{1,0:T(8,128)(2,1)S(1)}) custom-call(s32[2]{0:T(128)S(1)} %pad_add_fusion.place_ref, bf16[256,1024]{1,0:T(8,128)(2,1)S(1)} %bitcast.18, f32[1,1024]{1,0:T(1,128)S(1)} %bitcast.22), custom_call_target="tpu_custom_call" | custom-call | flops 1073741824 | tf_op jit(solution)/shard_map/pallas_call | solution.py:429
  46.3 4.4 %collective-permute-done.rest_2_ = bf16[128,2048]{1,0:T(8,128)(2,1)S(1)} collective-permute-done((bf16[128,2048]{1,0:T(8,128)(2,1)S(1)}, bf16[128,2048]{1,0:T(8,128)(2,1)S(1)}, u32[]{:S(2)}, u32[]{:S(2)}) %collective-permute-start) | collective-permute-done | bytes 524320 | tf_op jit(solution)/shard_map/ppermute | solution.py:426
  50.7 2.1 %collective-permute-done.1.rest_4_ = bf16[128,2048]{1,0:T(8,128)(2,1)S(1)} collective-permute-done((bf16[128,2048]{1,0:T(8,128)(2,1)S(1)}, bf16[128,2048]{1,0:T(8,128)(2,1)S(1)}, u32[]{:S(2)}, u32[]{:S(2)}) %collective-permute-start.1) | collective-permute-done | bytes 524320 | tf_op jit(solution)/shard_map/ppermute | solution.py:426
  52.8 0.0 copy-start.1
  52.8 3.1 %collective-permute-start.5 = (bf16[64,2048]{1,0:T(8,128)(2,1)S(1)}, bf16[64,2048]{1,0:T(8,128)(2,1)S(1)}, u32[]{:S(2)}, u32[]{:S(2)}) collective-permute-start(bf16[64,2048]{1,0:T(8,128)(2,1)S(1)} %slice.8), channel_id=1, source_target_pairs={{0,128},{8,136},{16,144},{24,152},{32,160},{40,168},{48,176},{56,1... | collective-permute-start | bytes 786440 | tf_op jit(solution)/shard_map/ppermute | solution.py:439
  55.9 3.4 %collective-permute-start.7 = (bf16[64,2048]{1,0:T(8,128)(2,1)S(1)}, bf16[64,2048]{1,0:T(8,128)(2,1)S(1)}, u32[]{:S(2)}, u32[]{:S(2)}) collective-permute-start(bf16[64,2048]{1,0:T(8,128)(2,1)S(1)} %slice.9), channel_id=1, source_target_pairs={{0,384},{8,392},{16,400},{24,408},{32,416},{40,424},{48,432},{56,4... | collective-permute-start | bytes 786440 | tf_op jit(solution)/shard_map/ppermute | solution.py:439
  59.3 4.0 %collective-permute-start.3 = (bf16[128,2048]{1,0:T(8,128)(2,1)S(1)}, bf16[128,2048]{1,0:T(8,128)(2,1)S(1)}, u32[]{:S(2)}, u32[]{:S(2)}) collective-permute-start(bf16[128,2048]{1,0:T(8,128)(2,1)S(1)} %collective-permute-done.rest_2_), channel_id=1, source_target_pairs={{0,8},{8,0},{16,24},{24,16},{32,40},{40,32},{48,56},{56,48},{64,72... | collective-permute-start | bytes 1572872 | tf_op jit(solution)/shard_map/ppermute | solution.py:442
  63.4 1.9 %collective-permute-start.4 = (bf16[128,2048]{1,0:T(8,128)(2,1)S(1)}, bf16[128,2048]{1,0:T(8,128)(2,1)S(1)}, u32[]{:S(2)}, u32[]{:S(2)}) collective-permute-start(bf16[128,2048]{1,0:T(8,128)(2,1)S(1)} %collective-permute-done.1.rest_4_), channel_id=1, source_target_pairs={{0,8},{8,0},{16,24},{24,16},{32,40},{40,32},{48,56},{56,48},{64,72... | collective-permute-start | bytes 1572872 | tf_op jit(solution)/shard_map/ppermute | solution.py:442
  65.3 0.0 collective-permute-done.5.rest_6_
  65.3 2.4 %collective-permute-start.6 = (bf16[64,2048]{1,0:T(8,128)(2,1)S(1)}, bf16[64,2048]{1,0:T(8,128)(2,1)S(1)}, u32[]{:S(2)}, u32[]{:S(2)}) collective-permute-start(bf16[64,2048]{1,0:T(8,128)(2,1)S(1)} %collective-permute-done.5.rest_6_), channel_id=1, source_target_pairs={{0,8},{8,0},{16,24},{24,16},{32,40},{40,32},{48,56},{56,48},{64,72... | collective-permute-start | bytes 786440 | tf_op jit(solution)/shard_map/ppermute | solution.py:444
  67.7 0.0 collective-permute-done.7.rest_8_
  67.7 1.9 %collective-permute-start.8 = (bf16[64,2048]{1,0:T(8,128)(2,1)S(1)}, bf16[64,2048]{1,0:T(8,128)(2,1)S(1)}, u32[]{:S(2)}, u32[]{:S(2)}) collective-permute-start(bf16[64,2048]{1,0:T(8,128)(2,1)S(1)} %collective-permute-done.7.rest_8_), channel_id=1, source_target_pairs={{0,8},{8,0},{16,24},{24,16},{32,40},{40,32},{48,56},{56,48},{64,72... | collective-permute-start | bytes 786440 | tf_op jit(solution)/shard_map/ppermute | solution.py:444
  69.6 0.0 collective-permute-done.2.rest_1_
  69.7 0.0 collective-permute-done.6.rest_7_
  69.7 1.6 %collective-permute-done.8.rest_9_ = bf16[64,2048]{1,0:T(8,128)(2,1)S(1)} collective-permute-done((bf16[64,2048]{1,0:T(8,128)(2,1)S(1)}, bf16[64,2048]{1,0:T(8,128)(2,1)S(1)}, u32[]{:S(2)}, u32[]{:S(2)}) %collective-permute-start.8) | collective-permute-done | bytes 262176 | tf_op jit(solution)/shard_map/ppermute | solution.py:444
  71.2 0.0 collective-permute-done.3.rest_3_
  71.2 0.0 collective-permute-done.4.rest_5_
  71.2 4.0 %shard_map.184 = bf16[256,1024]{1,0:T(8,128)(2,1)S(1)} custom-call(bf16[256,1024]{1,0:T(8,128)(2,1)S(1)} %bitcast.19, bf16[256,512]{1,0:T(8,128)(2,1)S(1)} %get-tuple-element.39.own_ref, bf16[256,512]{1,0:T(8,128)(2,1)S(1)} %get-tuple-element.40.other_ref, bf16[512,512]{1,0:T(8,128)(2,1)S(1)} %get-tuple-element.41.pick_ref, bf16[128,2048]{1,0:T(8,128)(2,1)S(1)} %bitcast.15, ...), custom_call_target="tpu_custom_call" | custom-call | tf_op jit(solution)/shard_map/pallas_call | solution.py:445
  75.2 27.8 %all_to_all.20 = bf16[8,32,1024]{2,1,0:T(8,128)(2,1)S(1)} all-to-all(bf16[8,32,1024]{2,1,0:T(8,128)(2,1)S(1)} %bitcast.16), channel_id=1, replica_groups=mesh['dp'=64,'frame'=8] {'frame'}, dimensions={0} | all-to-all | bytes 1048576 | tf_op jit(solution)/shard_map/all_to_all | solution.py:452
  103.0 0.0 all-gather.2.cloned.1.call-done
  103.0 0.0 copy-done.1
  103.0 0.0 copy-start.4
  103.0 0.0 copy-start.5
  103.0 5.8 %shard_map.185 = (bf16[256,1024]{1,0:T(8,128)(2,1)}, f32[8,8,128]{2,1,0:T(8,128)S(1)}) custom-call(bf16[256,1024]{1,0:T(8,128)(2,1)S(1)} %bitcast.17, f32[1,1024]{1,0:T(1,128)S(1)} %bitcast.20, bf16[8,2,4,16,3584]{4,3,2,1,0:T(8,128)(2,1)} %bitcast.23), custom_call_target="tpu_custom_call" | custom-call | tf_op jit(solution)/shard_map/pallas_call | solution.py:453
  108.8 9.3 %all_to_all.21.parts_ref = f32[8,8,128]{2,1,0:T(8,128)S(1)} all-to-all(f32[8,8,128]{2,1,0:T(8,128)S(1)} %get-tuple-element.48), channel_id=1, replica_groups=mesh['dp'=64,'frame'=8] {'frame'}, dimensions={0} | all-to-all | bytes 65536 | tf_op jit(solution)/shard_map/all_to_all | solution.py:476
  118.0 0.7 shard_map.186
  118.8 5.7 %all-to-all-start.3 = ((f32[64,8,128]{2,1,0:T(8,128)}), f32[64,8,128]{2,1,0:T(8,128)S(1)}, u32[]{:S(2)}, u32[]{:S(2)}) async-start(f32[64,8,128]{2,1,0:T(8,128)} %shard_map.186), calls=%async_computation.3 | async-start | bytes 524288 | tf_op jit(solution)/shard_map/all_to_all | solution.py:478
  124.5 0.0 copy-done.4
  124.5 0.0 copy-done.5
  124.6 0.1 copy.20.pairs_ref
  125.3 0.0 copy-start.2
  125.3 4.4 %shard_map.187 = (f32[64,768]{1,0:T(8,128)S(1)}, f32[64,768]{1,0:T(8,128)S(1)}, bf16[768,768]{1,0:T(8,128)(2,1)S(1)}, bf16[4,8,2,16,768]{4,3,2,1,0:T(8,128)(2,1)S(1)}) custom-call(f32[1,768]{1,0:T(1,128)S(1)} %reshape.67.gain_ref.gain_text_ref, bf16[8,2,4,16,3584]{4,3,2,1,0:T(8,128)(2,1)} %bitcast.24), custom_call_target="tpu_custom_call" | custom-call | tf_op jit(solution)/shard_map/pallas_call | solution.py:465
  129.7 6.8 %all-to-all-done.3.pooled_ref = f32[64,8,128]{2,1,0:T(8,128)S(1)} async-done(((f32[64,8,128]{2,1,0:T(8,128)}), f32[64,8,128]{2,1,0:T(8,128)S(1)}, u32[]{:S(2)}, u32[]{:S(2)}) %all-to-all-start.3) | async-done | bytes 262176 | tf_op jit(solution)/shard_map/all_to_all | solution.py:478
  136.5 0.0 copy-done.2
  136.5 3.2 %shard_map.188 = (f32[1]{0:T(128)}, f32[1]{0:T(128)}, f32[1,1024]{1,0:T(1,128)}, f32[1,768]{1,0:T(1,128)}) custom-call(s32[1]{0:T(128)} %bitcast.3.place_ref, f32[1]{0:T(128)S(6)} %copy.21.scale_ref, s32[64,1]{1,0:T(8,128)S(1)} %copy.20.pairs_ref, f32[64,8,128]{2,1,0:T(8,128)S(1)} %all-to-all-done.3.pooled_ref, ...), custom_call_target="tpu_custom_call" | custom-call | tf_op jit(solution)/shard_map/pallas_call | solution.py:479
  (3 shorter events, 0.0 us)
Async XLA Ops:
  7.2 37.4 %copy-start = (bf16[1,1,256,1024]{3,2,1,0:T(8,128)(2,1)S(1)}, bf16[1,1,256,1024]{3,2,1,0:T(8,128)(2,1)}, u32[]{:S(2)}) copy-start(bf16[1,1,256,1024]{3,2,1,0:T(8,128)(2,1)} %param.15) | copy-start | bytes 1572868
  7.2 37.4 %copy-start.3 = (f32[1024]{0:T(1024)S(1)}, f32[1024]{0:T(1024)}, u32[]{:S(2)}) copy-start(f32[1024]{0:T(1024)} %param.20) | copy-start | bytes 12292
  9.3 22.4 %all-to-all-start = ((bf16[8,16,2048]{2,1,0:T(8,128)(2,1)}), bf16[8,16,2048]{2,1,0:T(8,128)(2,1)S(1)}, u32[]{:S(2)}, u32[]{:S(2)}) async-start(bf16[8,16,2048]{2,1,0:T(8,128)(2,1)} %get-tuple-element.31), calls=%async_computation | async-start | bytes 1048576 | tf_op jit(solution)/shard_map/all_to_all | solution.py:370
  17.0 86.0 %all-gather.2.cloned.1.call-start = ((), (), s32[]{:S(2)}) async-start(), calls=%async_computation.4 | async-start | bytes 7798784 | tf_op jit(solution)/shard_map/all_gather | solution.py:423
  31.8 18.9 %collective-permute-start = (bf16[128,2048]{1,0:T(8,128)(2,1)S(1)}, bf16[128,2048]{1,0:T(8,128)(2,1)S(1)}, u32[]{:S(2)}, u32[]{:S(2)}) collective-permute-start(bf16[128,2048]{1,0:T(8,128)(2,1)S(1)} %bitcast.12), channel_id=1, source_target_pairs={{0,128},{8,136},{16,144},{24,152},{32,160},{40,168},{48,176},{56,1... | collective-permute-start | bytes 1572872 | tf_op jit(solution)/shard_map/ppermute | solution.py:426
  38.1 14.7 %collective-permute-start.1 = (bf16[128,2048]{1,0:T(8,128)(2,1)S(1)}, bf16[128,2048]{1,0:T(8,128)(2,1)S(1)}, u32[]{:S(2)}, u32[]{:S(2)}) collective-permute-start(bf16[128,2048]{1,0:T(8,128)(2,1)S(1)} %bitcast.13), channel_id=1, source_target_pairs={{0,384},{8,392},{16,400},{24,408},{32,416},{40,424},{48,432},{56,4... | collective-permute-start | bytes 1572872 | tf_op jit(solution)/shard_map/ppermute | solution.py:426
  41.4 28.3 %collective-permute-start.2 = (bf16[128,2048]{1,0:T(8,128)(2,1)S(1)}, bf16[128,2048]{1,0:T(8,128)(2,1)S(1)}, u32[]{:S(2)}, u32[]{:S(2)}) collective-permute-start(bf16[128,2048]{1,0:T(8,128)(2,1)S(1)} %bitcast.14), channel_id=1, source_target_pairs={{0,8},{8,0},{16,24},{24,16},{32,40},{40,32},{48,56},{56,48},{64,72... | collective-permute-start | bytes 1572872 | tf_op jit(solution)/shard_map/ppermute | solution.py:427
  52.8 50.2 %copy-start.1 = (f32[1024]{0:T(1024)S(1)}, f32[1024]{0:T(1024)}, u32[]{:S(2)}) copy-start(f32[1024]{0:T(1024)} %param.21) | copy-start | bytes 12292
  52.8 12.5 %collective-permute-start.5 = (bf16[64,2048]{1,0:T(8,128)(2,1)S(1)}, bf16[64,2048]{1,0:T(8,128)(2,1)S(1)}, u32[]{:S(2)}, u32[]{:S(2)}) collective-permute-start(bf16[64,2048]{1,0:T(8,128)(2,1)S(1)} %slice.8), channel_id=1, source_target_pairs={{0,128},{8,136},{16,144},{24,152},{32,160},{40,168},{48,176},{56,1... | collective-permute-start | bytes 786440 | tf_op jit(solution)/shard_map/ppermute | solution.py:439
  55.9 11.8 %collective-permute-start.7 = (bf16[64,2048]{1,0:T(8,128)(2,1)S(1)}, bf16[64,2048]{1,0:T(8,128)(2,1)S(1)}, u32[]{:S(2)}, u32[]{:S(2)}) collective-permute-start(bf16[64,2048]{1,0:T(8,128)(2,1)S(1)} %slice.9), channel_id=1, source_target_pairs={{0,384},{8,392},{16,400},{24,408},{32,416},{40,424},{48,432},{56,4... | collective-permute-start | bytes 786440 | tf_op jit(solution)/shard_map/ppermute | solution.py:439
  59.3 11.9 %collective-permute-start.3 = (bf16[128,2048]{1,0:T(8,128)(2,1)S(1)}, bf16[128,2048]{1,0:T(8,128)(2,1)S(1)}, u32[]{:S(2)}, u32[]{:S(2)}) collective-permute-start(bf16[128,2048]{1,0:T(8,128)(2,1)S(1)} %collective-permute-done.rest_2_), channel_id=1, source_target_pairs={{0,8},{8,0},{16,24},{24,16},{32,40},{40,32},{48,56},{56,48},{64,72... | collective-permute-start | bytes 1572872 | tf_op jit(solution)/shard_map/ppermute | solution.py:442
  63.4 7.9 %collective-permute-start.4 = (bf16[128,2048]{1,0:T(8,128)(2,1)S(1)}, bf16[128,2048]{1,0:T(8,128)(2,1)S(1)}, u32[]{:S(2)}, u32[]{:S(2)}) collective-permute-start(bf16[128,2048]{1,0:T(8,128)(2,1)S(1)} %collective-permute-done.1.rest_4_), channel_id=1, source_target_pairs={{0,8},{8,0},{16,24},{24,16},{32,40},{40,32},{48,56},{56,48},{64,72... | collective-permute-start | bytes 1572872 | tf_op jit(solution)/shard_map/ppermute | solution.py:442
  65.3 4.4 %collective-permute-start.6 = (bf16[64,2048]{1,0:T(8,128)(2,1)S(1)}, bf16[64,2048]{1,0:T(8,128)(2,1)S(1)}, u32[]{:S(2)}, u32[]{:S(2)}) collective-permute-start(bf16[64,2048]{1,0:T(8,128)(2,1)S(1)} %collective-permute-done.5.rest_6_), channel_id=1, source_target_pairs={{0,8},{8,0},{16,24},{24,16},{32,40},{40,32},{48,56},{56,48},{64,72... | collective-permute-start | bytes 786440 | tf_op jit(solution)/shard_map/ppermute | solution.py:444
  67.7 3.5 %collective-permute-start.8 = (bf16[64,2048]{1,0:T(8,128)(2,1)S(1)}, bf16[64,2048]{1,0:T(8,128)(2,1)S(1)}, u32[]{:S(2)}, u32[]{:S(2)}) collective-permute-start(bf16[64,2048]{1,0:T(8,128)(2,1)S(1)} %collective-permute-done.7.rest_8_), channel_id=1, source_target_pairs={{0,8},{8,0},{16,24},{24,16},{32,40},{40,32},{48,56},{56,48},{64,72... | collective-permute-start | bytes 786440 | tf_op jit(solution)/shard_map/ppermute | solution.py:444
  103.0 21.5 %copy-start.4 = (f32[768]{0:T(1024)S(1)}, f32[768]{0:T(1024)}, u32[]{:S(2)}) copy-start(f32[768]{0:T(1024)} %param.23) | copy-start | bytes 9220
  103.0 21.6 %copy-start.5 = (s32[64]{0:T(128)S(1)}, s32[64]{0:T(128)}, u32[]{:S(2)}) copy-start(s32[64]{0:T(128)} %param.18) | copy-start | bytes 772
  118.8 17.8 %all-to-all-start.3 = ((f32[64,8,128]{2,1,0:T(8,128)}), f32[64,8,128]{2,1,0:T(8,128)S(1)}, u32[]{:S(2)}, u32[]{:S(2)}) async-start(f32[64,8,128]{2,1,0:T(8,128)} %shard_map.186), calls=%async_computation.3 | async-start | bytes 524288 | tf_op jit(solution)/shard_map/all_to_all | solution.py:478
  125.3 11.2 %copy-start.2 = (f32[1024]{0:T(1024)S(1)}, f32[1024]{0:T(1024)}, u32[]{:S(2)}) copy-start(f32[1024]{0:T(1024)} %param.22) | copy-start | bytes 12292
Sparse Core Ops, SparseCore 0:
  31.9 57.3 all-gather.1

commit v9 on v8

--- a/solution.py
+++ b/solution.py
@@ -126,25 +126,17 @@
         pick_ref[:, half * (WIDTH // 2) : (half + 1) * (WIDTH // 2)] = pick.astype(BF16)
 
 
-def blocks_product(normed_refs, first, block_refs):
-    total, starts = None, [first, first]
-    for number, ref in enumerate(block_refs):
-        half, depth = number % 2, ref.shape[0]
-        rows = slice(starts[half], starts[half] + depth)
-        starts[half] += depth
-        part = dot(normed_refs[half][:, rows], ref[:, QKV : QKV + 3 * WIDTH])
-        total = part if total is None else total + part
-    return total
-
-
 def spatial_kernel(tokens_ref, own_ref, other_ref, pick_ref, *rest):
     block_refs, (spatial_ref, packed, mixed) = rest[:-3], rest[-3:]
-    packed[...] = blocks_product((own_ref, other_ref), 0, block_refs).astype(BF16)
+    block_refs = block_refs[0::2] + block_refs[1::2]
+    normed = jnp.concatenate([own_ref[...], other_ref[...]], axis=1)
+    weight = jnp.concatenate([ref[:, QKV : QKV + 3 * WIDTH] for ref in block_refs], axis=0)
+    packed[...] = dot(normed, weight).astype(BF16)
     attend(packed, mixed, None)
     sorted_mixed = dot(mixed[...], pick_ref[...]).astype(BF16)
     halves = [
         ref[:, OUT : OUT + D // 2].astype(F32).reshape(ref.shape[0] // 16, 2, 8, D // 2)
-        for ref in block_refs[0::2] + block_refs[1::2]
+        for ref in block_refs
     ]
     for side in range(2):
         columns = slice(side * (D // 2), (side + 1) * (D // 2))
@@ -433,9 +425,8 @@
         [],
         flops=1 << 30,
     )(where, late_tokens, gain_spatial.reshape(1, D))
-    below, above, low, high, normed, pick = barrier(
-        (below, above, below[: BLOCK // 2], above[BLOCK // 2 :], normed, pick)
-    )
+    below, low, normed, pick = barrier((below, below[: BLOCK // 2], normed, pick))
+    above, high = barrier((above, above[BLOCK // 2 :]))
     low, high = permute(low, perm=X_UP), permute(high, perm=X_DOWN)
     near, far = [mine, mine_other], []
     for block in (below, above):

time: 147 us -> 144 us (0.980)
  waiting for transfers between devices: 16.8 us -> 14.7 us
    ppermute x2, waiting for transfers between devices: 6.46 us -> 4.39 us  [on_device(): below, above = (permute(mine, perm=X_UP), permute(mine, perm=X_DOWN))]
  transfers between devices with their start and end apart: 12 -> 12, of which waited for: 5 -> 4; matrix products, arithmetic and copies ran while one was open for 0% -> 0% of each run, Pallas kernels for 7% -> 6%
where the time goes in v9:
time: 144 us; the launch traced here: 143 us
  blocking collectives  50 us (35%)
  starting transfers between devices  42.9 us (30%)
  Pallas kernels  20.7 us (14%)
  between operations  15 us (10%)
  waiting for transfers between devices  14.7 us (10%)
    all_to_all x1, blocking collectives, on_device(): lax.all_to_all(spatial.reshape(FRAMES, 32, D), 'frame', 0, 0, tiled=True)  28 us
    all_gather x1, blocking collectives, on_device(): packed = gather(packed, axis_index_groups=ROWS_OF_X)  12.8 us
    ppermute x2, starting transfers between devices, on_device(): below, above = (permute(mine, perm=X_UP), permute(mine, perm=X_DOWN))  9.52 us
    all_to_all x1, blocking collectives, on_device(): pool = lax.all_to_all(pool, 'frame', 0, 0, tiled=True)  9.26 us
    all_to_all x1, starting transfers between devices, send_all(): lax.all_to_all(copies, 'dp', 0, 0, tiled=True, axis_index_groups=groups)  7.66 us
    all_to_all x1, waiting for transfers between devices, on_device(): pooled = lax.all_to_all(pool, 'dp', 0, 0, tiled=True)  6.83 us
    ppermute x2, starting transfers between devices, on_device(): low, high = (permute(low, perm=X_UP), permute(high, perm=X_DOWN))  6.49 us
    ppermute x2, starting transfers between devices, on_device(): near += [block, permute(block, perm=OTHER_CORE)]  5.94 us
  transfers between devices with their start and end apart: 12, of which 4 were waited for; matrix products, arithmetic and copies ran while one was open for 0% of the time, Pallas kernels for 6%

profile of v9, /device:TPU:1, one launch (start us, length us, event | category | flops | bytes accessed | tf_op | source)
XLA Modules:
  0.0 143.5 jit_solution(9378056458570647721)
XLA Ops:
  7.2 0.0 copy-start
  7.2 0.0 copy-start.3
  7.2 2.1 %shard_map.182 = (bf16[16,3584]{1,0:T(8,128)(2,1)}, bf16[8,16,2048]{2,1,0:T(8,128)(2,1)}) custom-call(s32[1,77]{1,0:T(1,128)} %ids_ref.1, bf16[77,768]{1,0:T(8,128)(2,1)} %bitcast.25, bf16[16,1536]{1,0:T(8,128)(2,1)} %qkv_ref.1, bf16[12,768]{1,0:T(8,128)(2,1)} %text_ref.1, bf16[8,1024]{1,0:T(8,128)(2,1)} %out_s_ref.1, bf16[8,1024]{1,0:T(8,128)(2,1)} %out_t_ref.1, ...), custom_call_target="tpu_custom_call" | custom-call | tf_op jit(solution)/shard_map/pallas_call | solution.py:387
  9.3 7.7 %all-to-all-start = ((bf16[8,16,2048]{2,1,0:T(8,128)(2,1)}), bf16[8,16,2048]{2,1,0:T(8,128)(2,1)S(1)}, u32[]{:S(2)}, u32[]{:S(2)}) async-start(bf16[8,16,2048]{2,1,0:T(8,128)(2,1)} %get-tuple-element.31), calls=%async_computation | async-start | bytes 1048576 | tf_op jit(solution)/shard_map/all_to_all | solution.py:362
  17.0 0.0 all-gather.2.cloned.1.call-start
  17.0 12.8 %all_gather.6 = bf16[64,3584]{1,0:T(8,128)(2,1)} all-gather(bf16[16,3584]{1,0:T(8,128)(2,1)} %get-tuple-element.32), channel_id=1, replica_groups={{0,128,256,384},{8,136,264,392},{16,144,272,400},{24,152,280,408},{32,1..., dimensions={0}, use_global_device_ids=true | all-gather | bytes 573440 | tf_op jit(solution)/shard_map/all_gather | solution.py:413
  29.8 2.0 %all-to-all-done = bf16[8,16,2048]{2,1,0:T(8,128)(2,1)S(1)} async-done(((bf16[8,16,2048]{2,1,0:T(8,128)(2,1)}), bf16[8,16,2048]{2,1,0:T(8,128)(2,1)S(1)}, u32[]{:S(2)}, u32[]{:S(2)}) %all-to-all-start) | async-done | bytes 524320 | tf_op jit(solution)/shard_map/all_to_all | solution.py:362
  31.7 0.0 all-gather.2.cloned.1.call-update
  31.8 6.3 %collective-permute-start = (bf16[128,2048]{1,0:T(8,128)(2,1)S(1)}, bf16[128,2048]{1,0:T(8,128)(2,1)S(1)}, u32[]{:S(2)}, u32[]{:S(2)}) collective-permute-start(bf16[128,2048]{1,0:T(8,128)(2,1)S(1)} %bitcast.12), channel_id=1, source_target_pairs={{0,128},{8,136},{16,144},{24,152},{32,160},{40,168},{48,176},{56,1... | collective-permute-start | bytes 1572872 | tf_op jit(solution)/shard_map/ppermute | solution.py:418
  38.1 3.2 %collective-permute-start.3 = (bf16[128,2048]{1,0:T(8,128)(2,1)S(1)}, bf16[128,2048]{1,0:T(8,128)(2,1)S(1)}, u32[]{:S(2)}, u32[]{:S(2)}) collective-permute-start(bf16[128,2048]{1,0:T(8,128)(2,1)S(1)} %bitcast.13), channel_id=1, source_target_pairs={{0,384},{8,392},{16,400},{24,408},{32,416},{40,424},{48,432},{56,4... | collective-permute-start | bytes 1572872 | tf_op jit(solution)/shard_map/ppermute | solution.py:418
  41.3 0.1 pad_add_fusion.place_ref
  41.4 3.1 %collective-permute-start.1 = (bf16[128,2048]{1,0:T(8,128)(2,1)S(1)}, bf16[128,2048]{1,0:T(8,128)(2,1)S(1)}, u32[]{:S(2)}, u32[]{:S(2)}) collective-permute-start(bf16[128,2048]{1,0:T(8,128)(2,1)S(1)} %bitcast.14), channel_id=1, source_target_pairs={{0,8},{8,0},{16,24},{24,16},{32,40},{40,32},{48,56},{56,48},{64,72... | collective-permute-start | bytes 1572872 | tf_op jit(solution)/shard_map/ppermute | solution.py:419
  44.5 0.0 copy-done
  44.6 0.0 copy-done.3
  44.6 1.7 %shard_map.183 = (bf16[256,512]{1,0:T(8,128)(2,1)S(1)}, bf16[256,512]{1,0:T(8,128)(2,1)S(1)}, bf16[512,512]{1,0:T(8,128)(2,1)S(1)}) custom-call(s32[2]{0:T(128)S(1)} %pad_add_fusion.place_ref, bf16[256,1024]{1,0:T(8,128)(2,1)S(1)} %bitcast.18, f32[1,1024]{1,0:T(1,128)S(1)} %bitcast.22), custom_call_target="tpu_custom_call" | custom-call | flops 1073741824 | tf_op jit(solution)/shard_map/pallas_call | solution.py:421
  46.3 4.4 %collective-permute-done.rest_2_ = bf16[128,2048]{1,0:T(8,128)(2,1)S(1)} collective-permute-done((bf16[128,2048]{1,0:T(8,128)(2,1)S(1)}, bf16[128,2048]{1,0:T(8,128)(2,1)S(1)}, u32[]{:S(2)}, u32[]{:S(2)}) %collective-permute-start) | collective-permute-done | bytes 524320 | tf_op jit(solution)/shard_map/ppermute | solution.py:418
  50.7 2.3 %collective-permute-start.5 = (bf16[64,2048]{1,0:T(8,128)(2,1)S(1)}, bf16[64,2048]{1,0:T(8,128)(2,1)S(1)}, u32[]{:S(2)}, u32[]{:S(2)}) collective-permute-start(bf16[64,2048]{1,0:T(8,128)(2,1)S(1)} %slice.8), channel_id=1, source_target_pairs={{0,128},{8,136},{16,144},{24,152},{32,160},{40,168},{48,176},{56,1... | collective-permute-start | bytes 786440 | tf_op jit(solution)/shard_map/ppermute | solution.py:430
  53.0 0.0 collective-permute-done.3.rest_4_
  53.1 0.0 copy-start.1
  53.1 4.2 %collective-permute-start.7 = (bf16[64,2048]{1,0:T(8,128)(2,1)S(1)}, bf16[64,2048]{1,0:T(8,128)(2,1)S(1)}, u32[]{:S(2)}, u32[]{:S(2)}) collective-permute-start(bf16[64,2048]{1,0:T(8,128)(2,1)S(1)} %slice.9), channel_id=1, source_target_pairs={{0,384},{8,392},{16,400},{24,408},{32,416},{40,424},{48,432},{56,4... | collective-permute-start | bytes 786440 | tf_op jit(solution)/shard_map/ppermute | solution.py:430
  57.3 4.0 %collective-permute-start.2 = (bf16[128,2048]{1,0:T(8,128)(2,1)S(1)}, bf16[128,2048]{1,0:T(8,128)(2,1)S(1)}, u32[]{:S(2)}, u32[]{:S(2)}) collective-permute-start(bf16[128,2048]{1,0:T(8,128)(2,1)S(1)} %collective-permute-done.rest_2_), channel_id=1, source_target_pairs={{0,8},{8,0},{16,24},{24,16},{32,40},{40,32},{48,56},{56,48},{64,72... | collective-permute-start | bytes 1572872 | tf_op jit(solution)/shard_map/ppermute | solution.py:433
  61.3 1.9 %collective-permute-start.4 = (bf16[128,2048]{1,0:T(8,128)(2,1)S(1)}, bf16[128,2048]{1,0:T(8,128)(2,1)S(1)}, u32[]{:S(2)}, u32[]{:S(2)}) collective-permute-start(bf16[128,2048]{1,0:T(8,128)(2,1)S(1)} %collective-permute-done.3.rest_4_), channel_id=1, source_target_pairs={{0,8},{8,0},{16,24},{24,16},{32,40},{40,32},{48,56},{56,48},{64,72... | collective-permute-start | bytes 1572872 | tf_op jit(solution)/shard_map/ppermute | solution.py:433
  63.2 0.0 collective-permute-done.5.rest_6_
  63.2 2.4 %collective-permute-start.6 = (bf16[64,2048]{1,0:T(8,128)(2,1)S(1)}, bf16[64,2048]{1,0:T(8,128)(2,1)S(1)}, u32[]{:S(2)}, u32[]{:S(2)}) collective-permute-start(bf16[64,2048]{1,0:T(8,128)(2,1)S(1)} %collective-permute-done.5.rest_6_), channel_id=1, source_target_pairs={{0,8},{8,0},{16,24},{24,16},{32,40},{40,32},{48,56},{56,48},{64,72... | collective-permute-start | bytes 786440 | tf_op jit(solution)/shard_map/ppermute | solution.py:435
  65.6 0.0 collective-permute-done.7.rest_8_
  65.7 1.9 %collective-permute-start.8 = (bf16[64,2048]{1,0:T(8,128)(2,1)S(1)}, bf16[64,2048]{1,0:T(8,128)(2,1)S(1)}, u32[]{:S(2)}, u32[]{:S(2)}) collective-permute-start(bf16[64,2048]{1,0:T(8,128)(2,1)S(1)} %collective-permute-done.7.rest_8_), channel_id=1, source_target_pairs={{0,8},{8,0},{16,24},{24,16},{32,40},{40,32},{48,56},{56,48},{64,72... | collective-permute-start | bytes 786440 | tf_op jit(solution)/shard_map/ppermute | solution.py:435
  67.6 0.0 collective-permute-done.1.rest_1_
  67.6 0.0 collective-permute-done.6.rest_7_
  67.6 1.5 %collective-permute-done.8.rest_9_ = bf16[64,2048]{1,0:T(8,128)(2,1)S(1)} collective-permute-done((bf16[64,2048]{1,0:T(8,128)(2,1)S(1)}, bf16[64,2048]{1,0:T(8,128)(2,1)S(1)}, u32[]{:S(2)}, u32[]{:S(2)}) %collective-permute-start.8) | collective-permute-done | bytes 262176 | tf_op jit(solution)/shard_map/ppermute | solution.py:435
  69.1 0.0 collective-permute-done.2.rest_3_
  69.1 0.0 collective-permute-done.4.rest_5_
  69.1 2.7 %shard_map.184 = bf16[256,1024]{1,0:T(8,128)(2,1)S(1)} custom-call(bf16[256,1024]{1,0:T(8,128)(2,1)S(1)} %bitcast.19, bf16[256,512]{1,0:T(8,128)(2,1)S(1)} %get-tuple-element.39.own_ref, bf16[256,512]{1,0:T(8,128)(2,1)S(1)} %get-tuple-element.40.other_ref, bf16[512,512]{1,0:T(8,128)(2,1)S(1)} %get-tuple-element.41.pick_ref, bf16[128,2048]{1,0:T(8,128)(2,1)S(1)} %bitcast.15, ...), custom_call_target="tpu_custom_call" | custom-call | tf_op jit(solution)/shard_map/pallas_call | solution.py:436
  71.8 28.0 %all_to_all.20 = bf16[8,32,1024]{2,1,0:T(8,128)(2,1)S(1)} all-to-all(bf16[8,32,1024]{2,1,0:T(8,128)(2,1)S(1)} %bitcast.16), channel_id=1, replica_groups=mesh['dp'=64,'frame'=8] {'frame'}, dimensions={0} | all-to-all | bytes 1048576 | tf_op jit(solution)/shard_map/all_to_all | solution.py:443
  99.8 0.0 all-gather.2.cloned.1.call-done
  99.8 0.0 copy-done.1
  99.8 0.0 copy-start.4
  99.8 0.0 copy-start.5
  99.8 5.8 %shard_map.185 = (bf16[256,1024]{1,0:T(8,128)(2,1)}, f32[8,8,128]{2,1,0:T(8,128)S(1)}) custom-call(bf16[256,1024]{1,0:T(8,128)(2,1)S(1)} %bitcast.17, f32[1,1024]{1,0:T(1,128)S(1)} %bitcast.20, bf16[8,2,4,16,3584]{4,3,2,1,0:T(8,128)(2,1)} %bitcast.23), custom_call_target="tpu_custom_call" | custom-call | tf_op jit(solution)/shard_map/pallas_call | solution.py:444
  105.6 9.3 %all_to_all.21.parts_ref = f32[8,8,128]{2,1,0:T(8,128)S(1)} all-to-all(f32[8,8,128]{2,1,0:T(8,128)S(1)} %get-tuple-element.48), channel_id=1, replica_groups=mesh['dp'=64,'frame'=8] {'frame'}, dimensions={0} | all-to-all | bytes 65536 | tf_op jit(solution)/shard_map/all_to_all | solution.py:467
  114.8 0.7 shard_map.186
  115.6 5.7 %all-to-all-start.3 = ((f32[64,8,128]{2,1,0:T(8,128)}), f32[64,8,128]{2,1,0:T(8,128)S(1)}, u32[]{:S(2)}, u32[]{:S(2)}) async-start(f32[64,8,128]{2,1,0:T(8,128)} %shard_map.186), calls=%async_computation.3 | async-start | bytes 524288 | tf_op jit(solution)/shard_map/all_to_all | solution.py:469
  121.3 0.0 copy-done.4
  121.4 0.0 copy-done.5
  121.4 0.1 copy.20.pairs_ref
  122.1 0.0 copy-start.2
  122.1 4.4 %shard_map.187 = (f32[64,768]{1,0:T(8,128)S(1)}, f32[64,768]{1,0:T(8,128)S(1)}, bf16[768,768]{1,0:T(8,128)(2,1)S(1)}, bf16[4,8,2,16,768]{4,3,2,1,0:T(8,128)(2,1)S(1)}) custom-call(f32[1,768]{1,0:T(1,128)S(1)} %reshape.67.gain_ref.gain_text_ref, bf16[8,2,4,16,3584]{4,3,2,1,0:T(8,128)(2,1)} %bitcast.24), custom_call_target="tpu_custom_call" | custom-call | tf_op jit(solution)/shard_map/pallas_call | solution.py:456
  126.5 6.8 %all-to-all-done.3.pooled_ref = f32[64,8,128]{2,1,0:T(8,128)S(1)} async-done(((f32[64,8,128]{2,1,0:T(8,128)}), f32[64,8,128]{2,1,0:T(8,128)S(1)}, u32[]{:S(2)}, u32[]{:S(2)}) %all-to-all-start.3) | async-done | bytes 262176 | tf_op jit(solution)/shard_map/all_to_all | solution.py:469
  133.4 0.0 copy-done.2
  133.4 3.2 %shard_map.188 = (f32[1]{0:T(128)}, f32[1]{0:T(128)}, f32[1,1024]{1,0:T(1,128)}, f32[1,768]{1,0:T(1,128)}) custom-call(s32[1]{0:T(128)} %bitcast.3.place_ref, f32[1]{0:T(128)S(6)} %copy.21.scale_ref, s32[64,1]{1,0:T(8,128)S(1)} %copy.20.pairs_ref, f32[64,8,128]{2,1,0:T(8,128)S(1)} %all-to-all-done.3.pooled_ref, ...), custom_call_target="tpu_custom_call" | custom-call | tf_op jit(solution)/shard_map/pallas_call | solution.py:470
  (3 shorter events, 0.0 us)
Async XLA Ops:
  7.2 37.4 %copy-start = (bf16[1,1,256,1024]{3,2,1,0:T(8,128)(2,1)S(1)}, bf16[1,1,256,1024]{3,2,1,0:T(8,128)(2,1)}, u32[]{:S(2)}) copy-start(bf16[1,1,256,1024]{3,2,1,0:T(8,128)(2,1)} %param.15) | copy-start | bytes 1572868
  7.2 37.4 %copy-start.3 = (f32[1024]{0:T(1024)S(1)}, f32[1024]{0:T(1024)}, u32[]{:S(2)}) copy-start(f32[1024]{0:T(1024)} %param.20) | copy-start | bytes 12292
  9.3 22.4 %all-to-all-start = ((bf16[8,16,2048]{2,1,0:T(8,128)(2,1)}), bf16[8,16,2048]{2,1,0:T(8,128)(2,1)S(1)}, u32[]{:S(2)}, u32[]{:S(2)}) async-start(bf16[8,16,2048]{2,1,0:T(8,128)(2,1)} %get-tuple-element.31), calls=%async_computation | async-start | bytes 1048576 | tf_op jit(solution)/shard_map/all_to_all | solution.py:362
  17.0 82.8 %all-gather.2.cloned.1.call-start = ((), (), s32[]{:S(2)}) async-start(), calls=%async_computation.4 | async-start | bytes 7798784 | tf_op jit(solution)/shard_map/all_gather | solution.py:415
  31.8 18.9 %collective-permute-start = (bf16[128,2048]{1,0:T(8,128)(2,1)S(1)}, bf16[128,2048]{1,0:T(8,128)(2,1)S(1)}, u32[]{:S(2)}, u32[]{:S(2)}) collective-permute-start(bf16[128,2048]{1,0:T(8,128)(2,1)S(1)} %bitcast.12), channel_id=1, source_target_pairs={{0,128},{8,136},{16,144},{24,152},{32,160},{40,168},{48,176},{56,1... | collective-permute-start | bytes 1572872 | tf_op jit(solution)/shard_map/ppermute | solution.py:418
  38.1 14.9 %collective-permute-start.3 = (bf16[128,2048]{1,0:T(8,128)(2,1)S(1)}, bf16[128,2048]{1,0:T(8,128)(2,1)S(1)}, u32[]{:S(2)}, u32[]{:S(2)}) collective-permute-start(bf16[128,2048]{1,0:T(8,128)(2,1)S(1)} %bitcast.13), channel_id=1, source_target_pairs={{0,384},{8,392},{16,400},{24,408},{32,416},{40,424},{48,432},{56,4... | collective-permute-start | bytes 1572872 | tf_op jit(solution)/shard_map/ppermute | solution.py:418
  41.4 26.2 %collective-permute-start.1 = (bf16[128,2048]{1,0:T(8,128)(2,1)S(1)}, bf16[128,2048]{1,0:T(8,128)(2,1)S(1)}, u32[]{:S(2)}, u32[]{:S(2)}) collective-permute-start(bf16[128,2048]{1,0:T(8,128)(2,1)S(1)} %bitcast.14), channel_id=1, source_target_pairs={{0,8},{8,0},{16,24},{24,16},{32,40},{40,32},{48,56},{56,48},{64,72... | collective-permute-start | bytes 1572872 | tf_op jit(solution)/shard_map/ppermute | solution.py:419
  50.7 12.5 %collective-permute-start.5 = (bf16[64,2048]{1,0:T(8,128)(2,1)S(1)}, bf16[64,2048]{1,0:T(8,128)(2,1)S(1)}, u32[]{:S(2)}, u32[]{:S(2)}) collective-permute-start(bf16[64,2048]{1,0:T(8,128)(2,1)S(1)} %slice.8), channel_id=1, source_target_pairs={{0,128},{8,136},{16,144},{24,152},{32,160},{40,168},{48,176},{56,1... | collective-permute-start | bytes 786440 | tf_op jit(solution)/shard_map/ppermute | solution.py:430
  53.1 46.7 %copy-start.1 = (f32[1024]{0:T(1024)S(1)}, f32[1024]{0:T(1024)}, u32[]{:S(2)}) copy-start(f32[1024]{0:T(1024)} %param.21) | copy-start | bytes 12292
  53.1 12.6 %collective-permute-start.7 = (bf16[64,2048]{1,0:T(8,128)(2,1)S(1)}, bf16[64,2048]{1,0:T(8,128)(2,1)S(1)}, u32[]{:S(2)}, u32[]{:S(2)}) collective-permute-start(bf16[64,2048]{1,0:T(8,128)(2,1)S(1)} %slice.9), channel_id=1, source_target_pairs={{0,384},{8,392},{16,400},{24,408},{32,416},{40,424},{48,432},{56,4... | collective-permute-start | bytes 786440 | tf_op jit(solution)/shard_map/ppermute | solution.py:430
  57.3 11.8 %collective-permute-start.2 = (bf16[128,2048]{1,0:T(8,128)(2,1)S(1)}, bf16[128,2048]{1,0:T(8,128)(2,1)S(1)}, u32[]{:S(2)}, u32[]{:S(2)}) collective-permute-start(bf16[128,2048]{1,0:T(8,128)(2,1)S(1)} %collective-permute-done.rest_2_), channel_id=1, source_target_pairs={{0,8},{8,0},{16,24},{24,16},{32,40},{40,32},{48,56},{56,48},{64,72... | collective-permute-start | bytes 1572872 | tf_op jit(solution)/shard_map/ppermute | solution.py:433
  61.3 7.8 %collective-permute-start.4 = (bf16[128,2048]{1,0:T(8,128)(2,1)S(1)}, bf16[128,2048]{1,0:T(8,128)(2,1)S(1)}, u32[]{:S(2)}, u32[]{:S(2)}) collective-permute-start(bf16[128,2048]{1,0:T(8,128)(2,1)S(1)} %collective-permute-done.3.rest_4_), channel_id=1, source_target_pairs={{0,8},{8,0},{16,24},{24,16},{32,40},{40,32},{48,56},{56,48},{64,72... | collective-permute-start | bytes 1572872 | tf_op jit(solution)/shard_map/ppermute | solution.py:433
  63.2 4.4 %collective-permute-start.6 = (bf16[64,2048]{1,0:T(8,128)(2,1)S(1)}, bf16[64,2048]{1,0:T(8,128)(2,1)S(1)}, u32[]{:S(2)}, u32[]{:S(2)}) collective-permute-start(bf16[64,2048]{1,0:T(8,128)(2,1)S(1)} %collective-permute-done.5.rest_6_), channel_id=1, source_target_pairs={{0,8},{8,0},{16,24},{24,16},{32,40},{40,32},{48,56},{56,48},{64,72... | collective-permute-start | bytes 786440 | tf_op jit(solution)/shard_map/ppermute | solution.py:435
  65.7 3.4 %collective-permute-start.8 = (bf16[64,2048]{1,0:T(8,128)(2,1)S(1)}, bf16[64,2048]{1,0:T(8,128)(2,1)S(1)}, u32[]{:S(2)}, u32[]{:S(2)}) collective-permute-start(bf16[64,2048]{1,0:T(8,128)(2,1)S(1)} %collective-permute-done.7.rest_8_), channel_id=1, source_target_pairs={{0,8},{8,0},{16,24},{24,16},{32,40},{40,32},{48,56},{56,48},{64,72... | collective-permute-start | bytes 786440 | tf_op jit(solution)/shard_map/ppermute | solution.py:435
  99.8 21.5 %copy-start.4 = (f32[768]{0:T(1024)S(1)}, f32[768]{0:T(1024)}, u32[]{:S(2)}) copy-start(f32[768]{0:T(1024)} %param.23) | copy-start | bytes 9220
  99.8 21.6 %copy-start.5 = (s32[64]{0:T(128)S(1)}, s32[64]{0:T(128)}, u32[]{:S(2)}) copy-start(s32[64]{0:T(128)} %param.18) | copy-start | bytes 772
  115.6 17.8 %all-to-all-start.3 = ((f32[64,8,128]{2,1,0:T(8,128)}), f32[64,8,128]{2,1,0:T(8,128)S(1)}, u32[]{:S(2)}, u32[]{:S(2)}) async-start(f32[64,8,128]{2,1,0:T(8,128)} %shard_map.186), calls=%async_computation.3 | async-start | bytes 524288 | tf_op jit(solution)/shard_map/all_to_all | solution.py:469
  122.1 11.2 %copy-start.2 = (f32[1024]{0:T(1024)S(1)}, f32[1024]{0:T(1024)}, u32[]{:S(2)}) copy-start(f32[1024]{0:T(1024)} %param.22) | copy-start | bytes 12292
Sparse Core Ops, SparseCore 0:
  31.9 57.3 all-gather.1

commit v10 on v9

--- a/solution.py
+++ b/solution.py
@@ -126,24 +126,21 @@
         pick_ref[:, half * (WIDTH // 2) : (half + 1) * (WIDTH // 2)] = pick.astype(BF16)
 
 
-def spatial_kernel(tokens_ref, own_ref, other_ref, pick_ref, *rest):
-    block_refs, (spatial_ref, packed, mixed) = rest[:-3], rest[-3:]
+def spatial_kernel(own_ref, other_ref, pick_ref, *rest):
+    block_refs, (mixed_ref, weight_ref, packed, mixed) = rest[:-4], rest[-4:]
     block_refs = block_refs[0::2] + block_refs[1::2]
     normed = jnp.concatenate([own_ref[...], other_ref[...]], axis=1)
     weight = jnp.concatenate([ref[:, QKV : QKV + 3 * WIDTH] for ref in block_refs], axis=0)
     packed[...] = dot(normed, weight).astype(BF16)
     attend(packed, mixed, None)
-    sorted_mixed = dot(mixed[...], pick_ref[...]).astype(BF16)
+    mixed_ref[...] = dot(mixed[...], pick_ref[...]).astype(BF16)
     halves = [
         ref[:, OUT : OUT + D // 2].astype(F32).reshape(ref.shape[0] // 16, 2, 8, D // 2)
         for ref in block_refs
     ]
     for side in range(2):
-        columns = slice(side * (D // 2), (side + 1) * (D // 2))
         weight = jnp.concatenate([half[:, side].reshape(-1, D // 2) for half in halves], axis=0)
-        spatial_ref[:, columns] = (
-            tokens_ref[:, columns].astype(F32) + dot(sorted_mixed, weight.astype(BF16))
-        ).astype(BF16)
+        weight_ref[:, side * (D // 2) : (side + 1) * (D // 2)] = weight.astype(BF16)
 
 
 def gather_rows(weights_ref, first, target, sems):
@@ -196,15 +193,17 @@
 
 
 def temporal_kernel(
-    spatial_ref, gain_ref, weights_ref, out_ref, pool_ref, qkv, outs, packed, mixed, sems
+    tokens_ref, mixed_ref, weight_ref, gain_ref, weights_ref, out_ref, pool_ref,
+    qkv, outs, spatial_ref, packed, mixed, sems,
 ):
     copies_qkv = gather_rows(weights_ref, QKV, qkv, sems.at[0])
     copies_out = gather_rows(weights_ref, OUT, outs, sems.at[1])
     for copy in copies_qkv + copies_out:
         copy.start()
-    rows = spatial_ref.shape[0]
-    spatial = spatial_ref[...].astype(F32)
-    normed = layer_norm(spatial, gain_ref[...]).astype(BF16)
+    rows = tokens_ref.shape[0]
+    spatial = tokens_ref[...].astype(F32) + dot(mixed_ref[...], weight_ref[...])
+    spatial_ref[...] = spatial.astype(BF16)
+    normed = layer_norm(spatial_ref[...].astype(F32), gain_ref[...]).astype(BF16)
     for copy in copies_qkv:
         copy.wait()
     packed[...] = dot(normed, qkv[...].reshape(D, 3 * WIDTH)).astype(BF16)
@@ -417,6 +416,7 @@
     mine, late_tokens = barrier((own.reshape(BLOCK, PACKED_S), tokens))
     below, above = permute(mine, perm=X_UP), permute(mine, perm=X_DOWN)
     mine_other = permute(mine, perm=OTHER_CORE)
+    by_patch = lax.all_to_all(late_tokens.reshape(FRAMES, 32, D), "frame", 0, 0, tiled=True)
     where = jnp.concatenate([place // (2 * Y), place % 2])
     *normed, pick = call(
         norm_kernel,
@@ -433,26 +433,34 @@
         near += [block, permute(block, perm=OTHER_CORE)]
     for block in (low, high):
         far += [block, permute(block, perm=OTHER_CORE)]
-    spatial = call(
+    mixed, out_spatial = call(
         spatial_kernel,
-        shape((256, D), BF16),
-        (V,) * 14,
+        (shape((256, WIDTH), BF16), shape((WIDTH, D), BF16)),
+        (V,) * 13,
         [pltpu.VMEM((256, 3 * WIDTH), BF16), pltpu.VMEM((256, WIDTH), BF16)],
         vmem=VMEM_SMALL,
-    )(tokens, *normed, pick, *near, *far)
-    spatial = lax.all_to_all(spatial.reshape(FRAMES, 32, D), "frame", 0, 0, tiled=True)
+    )(*normed, pick, *near, *far)
+    mixed, by_patch = barrier((mixed, by_patch))
+    mixed = lax.all_to_all(mixed.reshape(FRAMES, 32, WIDTH), "frame", 0, 0, tiled=True)
     layer_out, pool = call(
         temporal_kernel,
         (shape((256, D), BF16), shape((FRAMES, 8, 128), F32)),
-        (V, V, A),
+        (V, V, V, V, A),
         [
             pltpu.VMEM(halves + (3 * WIDTH,), BF16),
             pltpu.VMEM(halves + (D // 2,), BF16),
+            pltpu.VMEM((256, D), BF16),
             pltpu.VMEM((256, 3 * WIDTH), BF16),
             pltpu.VMEM((256, WIDTH), BF16),
             DMA((2, 2 * Y)),
         ],
-    )(spatial.reshape(256, D), gain_temporal.reshape(1, D), weights)
+    )(
+        by_patch.reshape(256, D),
+        mixed.reshape(256, WIDTH),
+        out_spatial,
+        gain_temporal.reshape(1, D),
+        weights,
+    )
     text_pool, text_mapped, text_weight, video_weight = call(
         text_kernel,
         (

time: 144 us -> 143 us (level)
  starting transfers between devices: 42.9 us -> 54.9 us
  blocking collectives: 50 us -> 41 us
  waiting for transfers between devices: 14.7 us -> 10.4 us
    all_to_all x0 -> x1, starting transfers between devices: none -> 10.2 us  [on_device(): lax.all_to_all(late_tokens.reshape(FRAMES, 32, D), 'frame', 0, 0, tiled=T...]
    all_to_all x1, blocking collectives: 28 us -> 19 us  [on_device(): lax.all_to_all(mixed.reshape(FRAMES, 32, WIDTH), 'frame', 0, 0, tiled=True)]
    ppermute x2, waiting for transfers between devices: 4.39 us -> 0.01 us  [on_device(): below, above = (permute(mine, perm=X_UP), permute(mine, perm=X_DOWN))]
    all_to_all x1, starting transfers between devices: 5.74 us -> 8.83 us  [on_device(): pooled = lax.all_to_all(pool, 'dp', 0, 0, tiled=True)]
    ppermute x2, starting transfers between devices: 5.94 us -> 4.39 us  [on_device(): near += [block, permute(block, perm=OTHER_CORE)]]
  transfers between devices with their start and end apart: 12 -> 13, of which waited for: 4 -> 4; matrix products, arithmetic and copies ran while one was open for 0% -> 0% of each run, Pallas kernels for 6% -> 6%
where the time goes in v10:
time: 143 us; the launch traced here: 142 us
  starting transfers between devices  54.9 us (38%)
  blocking collectives  41 us (29%)
  Pallas kernels  20.9 us (15%)
  between operations  15 us (10%)
  waiting for transfers between devices  10.4 us (7%)
    all_to_all x1, blocking collectives, on_device(): lax.all_to_all(mixed.reshape(FRAMES, 32, WIDTH), 'frame', 0, 0, tiled=True)  19 us
    all_gather x1, blocking collectives, on_device(): packed = gather(packed, axis_index_groups=ROWS_OF_X)  12.8 us
    all_to_all x1, starting transfers between devices, on_device(): lax.all_to_all(late_tokens.reshape(FRAMES, 32, D), 'frame', 0, 0, tiled=T...  10.2 us
    ppermute x2, starting transfers between devices, on_device(): below, above = (permute(mine, perm=X_UP), permute(mine, perm=X_DOWN))  9.52 us
    all_to_all x1, blocking collectives, on_device(): pool = lax.all_to_all(pool, 'frame', 0, 0, tiled=True)  9.27 us
    all_to_all x1, starting transfers between devices, on_device(): pooled = lax.all_to_all(pool, 'dp', 0, 0, tiled=True)  8.83 us
    all_to_all x1, starting transfers between devices, send_all(): lax.all_to_all(copies, 'dp', 0, 0, tiled=True, axis_index_groups=groups)  7.66 us
    all_to_all x1, waiting for transfers between devices, on_device(): pooled = lax.all_to_all(pool, 'dp', 0, 0, tiled=True)  6.8 us
  transfers between devices with their start and end apart: 13, of which 4 were waited for; matrix products, arithmetic and copies ran while one was open for 0% of the time, Pallas kernels for 6%

profile of v10, /device:TPU:1, one launch (start us, length us, event | category | flops | bytes accessed | tf_op | source)
XLA Modules:
  0.0 142.4 jit_solution(340530046071265905)
XLA Ops:
  7.2 2.1 %shard_map.182 = (bf16[16,3584]{1,0:T(8,128)(2,1)}, bf16[8,16,2048]{2,1,0:T(8,128)(2,1)}) custom-call(s32[1,77]{1,0:T(1,128)} %ids_ref.1, bf16[77,768]{1,0:T(8,128)(2,1)} %bitcast.26, bf16[16,1536]{1,0:T(8,128)(2,1)} %qkv_ref.1, bf16[12,768]{1,0:T(8,128)(2,1)} %text_ref.1, bf16[8,1024]{1,0:T(8,128)(2,1)} %out_s_ref.1, bf16[8,1024]{1,0:T(8,128)(2,1)} %out_t_ref.1, ...), custom_call_target="tpu_custom_call" | custom-call | tf_op jit(solution)/shard_map/pallas_call | solution.py:386
  9.3 0.0 copy-start.2
  9.3 7.7 %all-to-all-start = ((bf16[8,16,2048]{2,1,0:T(8,128)(2,1)}), bf16[8,16,2048]{2,1,0:T(8,128)(2,1)S(1)}, u32[]{:S(2)}, u32[]{:S(2)}) async-start(bf16[8,16,2048]{2,1,0:T(8,128)(2,1)} %get-tuple-element.35), calls=%async_computation | async-start | bytes 1048576 | tf_op jit(solution)/shard_map/all_to_all | solution.py:361
  16.9 0.0 all-gather.2.cloned.1.call-start
  17.0 12.8 %all_gather.6 = bf16[64,3584]{1,0:T(8,128)(2,1)} all-gather(bf16[16,3584]{1,0:T(8,128)(2,1)} %get-tuple-element.36), channel_id=1, replica_groups={{0,128,256,384},{8,136,264,392},{16,144,272,400},{24,152,280,408},{32,1..., dimensions={0}, use_global_device_ids=true | all-gather | bytes 573440 | tf_op jit(solution)/shard_map/all_gather | solution.py:412
  29.8 1.9 %all-to-all-done = bf16[8,16,2048]{2,1,0:T(8,128)(2,1)S(1)} async-done(((bf16[8,16,2048]{2,1,0:T(8,128)(2,1)}), bf16[8,16,2048]{2,1,0:T(8,128)(2,1)S(1)}, u32[]{:S(2)}, u32[]{:S(2)}) %all-to-all-start) | async-done | bytes 524320 | tf_op jit(solution)/shard_map/all_to_all | solution.py:361
  31.7 0.0 all-gather.2.cloned.1.call-update
  31.7 6.3 %collective-permute-start = (bf16[128,2048]{1,0:T(8,128)(2,1)S(1)}, bf16[128,2048]{1,0:T(8,128)(2,1)S(1)}, u32[]{:S(2)}, u32[]{:S(2)}) collective-permute-start(bf16[128,2048]{1,0:T(8,128)(2,1)S(1)} %bitcast.14), channel_id=1, source_target_pairs={{0,128},{8,136},{16,144},{24,152},{32,160},{40,168},{48,176},{56,1... | collective-permute-start | bytes 1572872 | tf_op jit(solution)/shard_map/ppermute | solution.py:417
  38.1 3.2 %collective-permute-start.3 = (bf16[128,2048]{1,0:T(8,128)(2,1)S(1)}, bf16[128,2048]{1,0:T(8,128)(2,1)S(1)}, u32[]{:S(2)}, u32[]{:S(2)}) collective-permute-start(bf16[128,2048]{1,0:T(8,128)(2,1)S(1)} %bitcast.15), channel_id=1, source_target_pairs={{0,384},{8,392},{16,400},{24,408},{32,416},{40,424},{48,432},{56,4... | collective-permute-start | bytes 1572872 | tf_op jit(solution)/shard_map/ppermute | solution.py:417
  41.3 10.2 %all-to-all-start.1 = ((bf16[8,32,1024]{2,1,0:T(8,128)(2,1)}), bf16[8,32,1024]{2,1,0:T(8,128)(2,1)S(1)}, u32[]{:S(2)}, u32[]{:S(2)}) async-start(bf16[8,32,1024]{2,1,0:T(8,128)(2,1)} %bitcast.5), calls=%async_computation.1 | async-start | bytes 1048576 | tf_op jit(solution)/shard_map/all_to_all | solution.py:419
  51.5 0.1 pad_add_fusion.place_ref
  51.6 3.2 %collective-permute-start.1 = (bf16[128,2048]{1,0:T(8,128)(2,1)S(1)}, bf16[128,2048]{1,0:T(8,128)(2,1)S(1)}, u32[]{:S(2)}, u32[]{:S(2)}) collective-permute-start(bf16[128,2048]{1,0:T(8,128)(2,1)S(1)} %bitcast.16), channel_id=1, source_target_pairs={{0,8},{8,0},{16,24},{24,16},{32,40},{40,32},{48,56},{56,48},{64,72... | collective-permute-start | bytes 1572872 | tf_op jit(solution)/shard_map/ppermute | solution.py:418
  54.8 0.0 copy-done.2
  54.8 2.2 %shard_map.183 = (bf16[256,512]{1,0:T(8,128)(2,1)S(1)}, bf16[256,512]{1,0:T(8,128)(2,1)S(1)}, bf16[512,512]{1,0:T(8,128)(2,1)S(1)}) custom-call(s32[2]{0:T(128)S(1)} %pad_add_fusion.place_ref, bf16[256,1024]{1,0:T(8,128)(2,1)} %bitcast.2.tokens_ref, f32[1,1024]{1,0:T(1,128)S(1)} %bitcast.23), custom_call_target="tpu_custom_call" | custom-call | flops 1073741824 | tf_op jit(solution)/shard_map/pallas_call | solution.py:421
  57.1 0.0 collective-permute-done.rest_2_
  57.1 1.9 %collective-permute-start.5 = (bf16[64,2048]{1,0:T(8,128)(2,1)S(1)}, bf16[64,2048]{1,0:T(8,128)(2,1)S(1)}, u32[]{:S(2)}, u32[]{:S(2)}) collective-permute-start(bf16[64,2048]{1,0:T(8,128)(2,1)S(1)} %slice.8), channel_id=1, source_target_pairs={{0,128},{8,136},{16,144},{24,152},{32,160},{40,168},{48,176},{56,1... | collective-permute-start | bytes 786440 | tf_op jit(solution)/shard_map/ppermute | solution.py:430
  59.0 0.0 collective-permute-done.3.rest_4_
  59.1 0.0 copy-start
  59.1 4.6 %collective-permute-start.7 = (bf16[64,2048]{1,0:T(8,128)(2,1)S(1)}, bf16[64,2048]{1,0:T(8,128)(2,1)S(1)}, u32[]{:S(2)}, u32[]{:S(2)}) collective-permute-start(bf16[64,2048]{1,0:T(8,128)(2,1)S(1)} %slice.9), channel_id=1, source_target_pairs={{0,384},{8,392},{16,400},{24,408},{32,416},{40,424},{48,432},{56,4... | collective-permute-start | bytes 786440 | tf_op jit(solution)/shard_map/ppermute | solution.py:430
  63.7 2.5 %collective-permute-start.2 = (bf16[128,2048]{1,0:T(8,128)(2,1)S(1)}, bf16[128,2048]{1,0:T(8,128)(2,1)S(1)}, u32[]{:S(2)}, u32[]{:S(2)}) collective-permute-start(bf16[128,2048]{1,0:T(8,128)(2,1)S(1)} %collective-permute-done.rest_2_), channel_id=1, source_target_pairs={{0,8},{8,0},{16,24},{24,16},{32,40},{40,32},{48,56},{56,48},{64,72... | collective-permute-start | bytes 1572872 | tf_op jit(solution)/shard_map/ppermute | solution.py:433
  66.1 1.9 %collective-permute-start.4 = (bf16[128,2048]{1,0:T(8,128)(2,1)S(1)}, bf16[128,2048]{1,0:T(8,128)(2,1)S(1)}, u32[]{:S(2)}, u32[]{:S(2)}) collective-permute-start(bf16[128,2048]{1,0:T(8,128)(2,1)S(1)} %collective-permute-done.3.rest_4_), channel_id=1, source_target_pairs={{0,8},{8,0},{16,24},{24,16},{32,40},{40,32},{48,56},{56,48},{64,72... | collective-permute-start | bytes 1572872 | tf_op jit(solution)/shard_map/ppermute | solution.py:433
  68.1 0.2 collective-permute-done.5.rest_6_
  68.2 2.6 %collective-permute-start.6 = (bf16[64,2048]{1,0:T(8,128)(2,1)S(1)}, bf16[64,2048]{1,0:T(8,128)(2,1)S(1)}, u32[]{:S(2)}, u32[]{:S(2)}) collective-permute-start(bf16[64,2048]{1,0:T(8,128)(2,1)S(1)} %collective-permute-done.5.rest_6_), channel_id=1, source_target_pairs={{0,8},{8,0},{16,24},{24,16},{32,40},{40,32},{48,56},{56,48},{64,72... | collective-permute-start | bytes 786440 | tf_op jit(solution)/shard_map/ppermute | solution.py:435
  70.8 0.0 collective-permute-done.7.rest_8_
  70.8 1.9 %collective-permute-start.8 = (bf16[64,2048]{1,0:T(8,128)(2,1)S(1)}, bf16[64,2048]{1,0:T(8,128)(2,1)S(1)}, u32[]{:S(2)}, u32[]{:S(2)}) collective-permute-start(bf16[64,2048]{1,0:T(8,128)(2,1)S(1)} %collective-permute-done.7.rest_8_), channel_id=1, source_target_pairs={{0,8},{8,0},{16,24},{24,16},{32,40},{40,32},{48,56},{56,48},{64,72... | collective-permute-start | bytes 786440 | tf_op jit(solution)/shard_map/ppermute | solution.py:435
  72.8 0.0 collective-permute-done.1.rest_1_
  72.8 0.0 collective-permute-done.6.rest_7_
  72.8 1.5 %collective-permute-done.8.rest_9_ = bf16[64,2048]{1,0:T(8,128)(2,1)S(1)} collective-permute-done((bf16[64,2048]{1,0:T(8,128)(2,1)S(1)}, bf16[64,2048]{1,0:T(8,128)(2,1)S(1)}, u32[]{:S(2)}, u32[]{:S(2)}) %collective-permute-start.8) | collective-permute-done | bytes 262176 | tf_op jit(solution)/shard_map/ppermute | solution.py:435
  74.3 0.0 collective-permute-done.2.rest_3_
  74.3 0.0 collective-permute-done.4.rest_5_
  74.3 2.4 %shard_map.184 = (bf16[256,512]{1,0:T(8,128)(2,1)S(1)}, bf16[512,1024]{1,0:T(8,128)(2,1)S(1)}) custom-call(bf16[256,512]{1,0:T(8,128)(2,1)S(1)} %get-tuple-element.43.own_ref, bf16[256,512]{1,0:T(8,128)(2,1)S(1)} %get-tuple-element.44.other_ref, bf16[512,512]{1,0:T(8,128)(2,1)S(1)} %get-tuple-element.45.pick_ref, bf16[128,2048]{1,0:T(8,128)(2,1)S(1)} %bitcast.17, ...), custom_call_target="tpu_custom_call" | custom-call | tf_op jit(solution)/shard_map/pallas_call | solution.py:436
  76.7 0.0 all-to-all-done.1
  76.7 19.0 %all_to_all.25 = bf16[8,32,512]{2,1,0:T(8,128)(2,1)S(1)} all-to-all(bf16[8,32,512]{2,1,0:T(8,128)(2,1)S(1)} %bitcast.20), channel_id=1, replica_groups=mesh['dp'=64,'frame'=8] {'frame'}, dimensions={0} | all-to-all | bytes 524288 | tf_op jit(solution)/shard_map/all_to_all | solution.py:444
  95.7 0.0 all-gather.2.cloned.1.call-done
  95.7 0.0 copy-done
  95.7 0.0 copy-start.3
  95.7 0.0 copy-start.4
  95.7 5.7 %shard_map.185 = (bf16[256,1024]{1,0:T(8,128)(2,1)}, f32[8,8,128]{2,1,0:T(8,128)S(1)}) custom-call(bf16[256,1024]{1,0:T(8,128)(2,1)S(1)} %bitcast.18, bf16[256,512]{1,0:T(8,128)(2,1)S(1)} %bitcast.19, bf16[512,1024]{1,0:T(8,128)(2,1)S(1)} %get-tuple-element.53.weight_ref, f32[1,1024]{1,0:T(1,128)S(1)} %bitcast.21, bf16[8,2,4,16,3584]{4,3,2,1,0:T(8,128)(2,1)} %bitcast.24), custom_call_target="tpu_custom_call" | custom-call | tf_op jit(solution)/shard_map/pallas_call | solution.py:445
  101.5 9.3 %all_to_all.26.parts_ref = f32[8,8,128]{2,1,0:T(8,128)S(1)} all-to-all(f32[8,8,128]{2,1,0:T(8,128)S(1)} %get-tuple-element.56), channel_id=1, replica_groups=mesh['dp'=64,'frame'=8] {'frame'}, dimensions={0} | all-to-all | bytes 65536 | tf_op jit(solution)/shard_map/all_to_all | solution.py:475
  110.7 0.7 shard_map.186
  111.5 8.8 %all-to-all-start.4 = ((f32[64,8,128]{2,1,0:T(8,128)}), f32[64,8,128]{2,1,0:T(8,128)S(1)}, u32[]{:S(2)}, u32[]{:S(2)}) async-start(f32[64,8,128]{2,1,0:T(8,128)} %shard_map.186), calls=%async_computation.4 | async-start | bytes 524288 | tf_op jit(solution)/shard_map/all_to_all | solution.py:477
  120.3 0.0 copy-done.3
  120.3 0.0 copy-done.4
  120.3 0.1 copy.20.pairs_ref
  121.1 0.0 copy-start.1
  121.1 4.4 %shard_map.187 = (f32[64,768]{1,0:T(8,128)S(1)}, f32[64,768]{1,0:T(8,128)S(1)}, bf16[768,768]{1,0:T(8,128)(2,1)S(1)}, bf16[4,8,2,16,768]{4,3,2,1,0:T(8,128)(2,1)S(1)}) custom-call(f32[1,768]{1,0:T(1,128)S(1)} %reshape.75.gain_ref.gain_text_ref, bf16[8,2,4,16,3584]{4,3,2,1,0:T(8,128)(2,1)} %bitcast.25), custom_call_target="tpu_custom_call" | custom-call | tf_op jit(solution)/shard_map/pallas_call | solution.py:464
  125.5 6.8 %all-to-all-done.4.pooled_ref = f32[64,8,128]{2,1,0:T(8,128)S(1)} async-done(((f32[64,8,128]{2,1,0:T(8,128)}), f32[64,8,128]{2,1,0:T(8,128)S(1)}, u32[]{:S(2)}, u32[]{:S(2)}) %all-to-all-start.4) | async-done | bytes 262176 | tf_op jit(solution)/shard_map/all_to_all | solution.py:477
  132.3 0.0 copy-done.1
  132.3 3.2 %shard_map.188 = (f32[1]{0:T(128)}, f32[1]{0:T(128)}, f32[1,1024]{1,0:T(1,128)}, f32[1,768]{1,0:T(1,128)}) custom-call(s32[1]{0:T(128)} %bitcast.3.place_ref, f32[1]{0:T(128)S(6)} %copy.21.scale_ref, s32[64,1]{1,0:T(8,128)S(1)} %copy.20.pairs_ref, f32[64,8,128]{2,1,0:T(8,128)S(1)} %all-to-all-done.4.pooled_ref, ...), custom_call_target="tpu_custom_call" | custom-call | tf_op jit(solution)/shard_map/pallas_call | solution.py:478
  (3 shorter events, 0.0 us)
Async XLA Ops:
  9.3 45.5 %copy-start.2 = (f32[1024]{0:T(1024)S(1)}, f32[1024]{0:T(1024)}, u32[]{:S(2)}) copy-start(f32[1024]{0:T(1024)} %param.20) | copy-start | bytes 12292
  9.3 22.4 %all-to-all-start = ((bf16[8,16,2048]{2,1,0:T(8,128)(2,1)}), bf16[8,16,2048]{2,1,0:T(8,128)(2,1)S(1)}, u32[]{:S(2)}, u32[]{:S(2)}) async-start(bf16[8,16,2048]{2,1,0:T(8,128)(2,1)} %get-tuple-element.35), calls=%async_computation | async-start | bytes 1048576 | tf_op jit(solution)/shard_map/all_to_all | solution.py:361
  16.9 78.8 %all-gather.2.cloned.1.call-start = ((), (), s32[]{:S(2)}) async-start(), calls=%async_computation.5 | async-start | bytes 7798784 | tf_op jit(solution)/shard_map/all_gather | solution.py:414
  31.7 25.3 %collective-permute-start = (bf16[128,2048]{1,0:T(8,128)(2,1)S(1)}, bf16[128,2048]{1,0:T(8,128)(2,1)S(1)}, u32[]{:S(2)}, u32[]{:S(2)}) collective-permute-start(bf16[128,2048]{1,0:T(8,128)(2,1)S(1)} %bitcast.14), channel_id=1, source_target_pairs={{0,128},{8,136},{16,144},{24,152},{32,160},{40,168},{48,176},{56,1... | collective-permute-start | bytes 1572872 | tf_op jit(solution)/shard_map/ppermute | solution.py:417
  38.1 21.0 %collective-permute-start.3 = (bf16[128,2048]{1,0:T(8,128)(2,1)S(1)}, bf16[128,2048]{1,0:T(8,128)(2,1)S(1)}, u32[]{:S(2)}, u32[]{:S(2)}) collective-permute-start(bf16[128,2048]{1,0:T(8,128)(2,1)S(1)} %bitcast.15), channel_id=1, source_target_pairs={{0,384},{8,392},{16,400},{24,408},{32,416},{40,424},{48,432},{56,4... | collective-permute-start | bytes 1572872 | tf_op jit(solution)/shard_map/ppermute | solution.py:417
  41.3 35.4 %all-to-all-start.1 = ((bf16[8,32,1024]{2,1,0:T(8,128)(2,1)}), bf16[8,32,1024]{2,1,0:T(8,128)(2,1)S(1)}, u32[]{:S(2)}, u32[]{:S(2)}) async-start(bf16[8,32,1024]{2,1,0:T(8,128)(2,1)} %bitcast.5), calls=%async_computation.1 | async-start | bytes 1048576 | tf_op jit(solution)/shard_map/all_to_all | solution.py:419
  51.6 21.2 %collective-permute-start.1 = (bf16[128,2048]{1,0:T(8,128)(2,1)S(1)}, bf16[128,2048]{1,0:T(8,128)(2,1)S(1)}, u32[]{:S(2)}, u32[]{:S(2)}) collective-permute-start(bf16[128,2048]{1,0:T(8,128)(2,1)S(1)} %bitcast.16), channel_id=1, source_target_pairs={{0,8},{8,0},{16,24},{24,16},{32,40},{40,32},{48,56},{56,48},{64,72... | collective-permute-start | bytes 1572872 | tf_op jit(solution)/shard_map/ppermute | solution.py:418
  57.1 11.2 %collective-permute-start.5 = (bf16[64,2048]{1,0:T(8,128)(2,1)S(1)}, bf16[64,2048]{1,0:T(8,128)(2,1)S(1)}, u32[]{:S(2)}, u32[]{:S(2)}) collective-permute-start(bf16[64,2048]{1,0:T(8,128)(2,1)S(1)} %slice.8), channel_id=1, source_target_pairs={{0,128},{8,136},{16,144},{24,152},{32,160},{40,168},{48,176},{56,1... | collective-permute-start | bytes 786440 | tf_op jit(solution)/shard_map/ppermute | solution.py:430
  59.1 36.6 %copy-start = (f32[1024]{0:T(1024)S(1)}, f32[1024]{0:T(1024)}, u32[]{:S(2)}) copy-start(f32[1024]{0:T(1024)} %param.21) | copy-start | bytes 12292
  59.1 11.8 %collective-permute-start.7 = (bf16[64,2048]{1,0:T(8,128)(2,1)S(1)}, bf16[64,2048]{1,0:T(8,128)(2,1)S(1)}, u32[]{:S(2)}, u32[]{:S(2)}) collective-permute-start(bf16[64,2048]{1,0:T(8,128)(2,1)S(1)} %slice.9), channel_id=1, source_target_pairs={{0,384},{8,392},{16,400},{24,408},{32,416},{40,424},{48,432},{56,4... | collective-permute-start | bytes 786440 | tf_op jit(solution)/shard_map/ppermute | solution.py:430
  63.7 10.6 %collective-permute-start.2 = (bf16[128,2048]{1,0:T(8,128)(2,1)S(1)}, bf16[128,2048]{1,0:T(8,128)(2,1)S(1)}, u32[]{:S(2)}, u32[]{:S(2)}) collective-permute-start(bf16[128,2048]{1,0:T(8,128)(2,1)S(1)} %collective-permute-done.rest_2_), channel_id=1, source_target_pairs={{0,8},{8,0},{16,24},{24,16},{32,40},{40,32},{48,56},{56,48},{64,72... | collective-permute-start | bytes 1572872 | tf_op jit(solution)/shard_map/ppermute | solution.py:433
  66.1 8.1 %collective-permute-start.4 = (bf16[128,2048]{1,0:T(8,128)(2,1)S(1)}, bf16[128,2048]{1,0:T(8,128)(2,1)S(1)}, u32[]{:S(2)}, u32[]{:S(2)}) collective-permute-start(bf16[128,2048]{1,0:T(8,128)(2,1)S(1)} %collective-permute-done.3.rest_4_), channel_id=1, source_target_pairs={{0,8},{8,0},{16,24},{24,16},{32,40},{40,32},{48,56},{56,48},{64,72... | collective-permute-start | bytes 1572872 | tf_op jit(solution)/shard_map/ppermute | solution.py:433
  68.2 4.5 %collective-permute-start.6 = (bf16[64,2048]{1,0:T(8,128)(2,1)S(1)}, bf16[64,2048]{1,0:T(8,128)(2,1)S(1)}, u32[]{:S(2)}, u32[]{:S(2)}) collective-permute-start(bf16[64,2048]{1,0:T(8,128)(2,1)S(1)} %collective-permute-done.5.rest_6_), channel_id=1, source_target_pairs={{0,8},{8,0},{16,24},{24,16},{32,40},{40,32},{48,56},{56,48},{64,72... | collective-permute-start | bytes 786440 | tf_op jit(solution)/shard_map/ppermute | solution.py:435
  70.8 3.4 %collective-permute-start.8 = (bf16[64,2048]{1,0:T(8,128)(2,1)S(1)}, bf16[64,2048]{1,0:T(8,128)(2,1)S(1)}, u32[]{:S(2)}, u32[]{:S(2)}) collective-permute-start(bf16[64,2048]{1,0:T(8,128)(2,1)S(1)} %collective-permute-done.7.rest_8_), channel_id=1, source_target_pairs={{0,8},{8,0},{16,24},{24,16},{32,40},{40,32},{48,56},{56,48},{64,72... | collective-permute-start | bytes 786440 | tf_op jit(solution)/shard_map/ppermute | solution.py:435
  95.7 24.6 %copy-start.3 = (f32[768]{0:T(1024)S(1)}, f32[768]{0:T(1024)}, u32[]{:S(2)}) copy-start(f32[768]{0:T(1024)} %param.23) | copy-start | bytes 9220
  95.7 24.6 %copy-start.4 = (s32[64]{0:T(128)S(1)}, s32[64]{0:T(128)}, u32[]{:S(2)}) copy-start(s32[64]{0:T(128)} %param.18) | copy-start | bytes 772
  111.5 20.8 %all-to-all-start.4 = ((f32[64,8,128]{2,1,0:T(8,128)}), f32[64,8,128]{2,1,0:T(8,128)S(1)}, u32[]{:S(2)}, u32[]{:S(2)}) async-start(f32[64,8,128]{2,1,0:T(8,128)} %shard_map.186), calls=%async_computation.4 | async-start | bytes 524288 | tf_op jit(solution)/shard_map/all_to_all | solution.py:477
  121.1 11.2 %copy-start.1 = (f32[1024]{0:T(1024)S(1)}, f32[1024]{0:T(1024)}, u32[]{:S(2)}) copy-start(f32[1024]{0:T(1024)} %param.22) | copy-start | bytes 12292
Sparse Core Ops, SparseCore 0:
  31.8 57.3 all-gather.1

commit v11 on v10

--- a/solution.py
+++ b/solution.py
@@ -415,7 +415,6 @@
     permute = functools.partial(lax.ppermute, axis_name="dp")
     mine, late_tokens = barrier((own.reshape(BLOCK, PACKED_S), tokens))
     below, above = permute(mine, perm=X_UP), permute(mine, perm=X_DOWN)
-    mine_other = permute(mine, perm=OTHER_CORE)
     by_patch = lax.all_to_all(late_tokens.reshape(FRAMES, 32, D), "frame", 0, 0, tiled=True)
     where = jnp.concatenate([place // (2 * Y), place % 2])
     *normed, pick = call(
@@ -426,9 +425,9 @@
         flops=1 << 30,
     )(where, late_tokens, gain_spatial.reshape(1, D))
     below, low, normed, pick = barrier((below, below[: BLOCK // 2], normed, pick))
-    above, high = barrier((above, above[BLOCK // 2 :]))
+    above, high, swapped = barrier((above, above[BLOCK // 2 :], mine))
     low, high = permute(low, perm=X_UP), permute(high, perm=X_DOWN)
-    near, far = [mine, mine_other], []
+    near, far = [mine, permute(swapped, perm=OTHER_CORE)], []
     for block in (below, above):
         near += [block, permute(block, perm=OTHER_CORE)]
     for block in (low, high):

time: 143 us -> 142 us (level)
  transfers between devices with their start and end apart: 13 -> 13, of which waited for: 4 -> 3; matrix products, arithmetic and copies ran while one was open for 0% -> 0% of each run, Pallas kernels for 6% -> 6%
where the time goes in v11:
time: 142 us; the launch traced here: 141 us
  starting transfers between devices  54.6 us (38%)
  blocking collectives  40.1 us (28%)
  Pallas kernels  20.8 us (15%)
  between operations  14.9 us (10%)
  waiting for transfers between devices  9.96 us (7%)
    all_to_all x1, blocking collectives, on_device(): lax.all_to_all(mixed.reshape(FRAMES, 32, WIDTH), 'frame', 0, 0, tiled=True)  18.1 us
    all_gather x1, blocking collectives, on_device(): packed = gather(packed, axis_index_groups=ROWS_OF_X)  12.8 us
    all_to_all x1, starting transfers between devices, on_device(): lax.all_to_all(late_tokens.reshape(FRAMES, 32, D), 'frame', 0, 0, tiled=T...  10.2 us
    ppermute x2, starting transfers between devices, on_device(): below, above = (permute(mine, perm=X_UP), permute(mine, perm=X_DOWN))  9.52 us
    all_to_all x1, blocking collectives, on_device(): pool = lax.all_to_all(pool, 'frame', 0, 0, tiled=True)  9.25 us
    all_to_all x1, starting transfers between devices, on_device(): pooled = lax.all_to_all(pool, 'dp', 0, 0, tiled=True)  8.24 us
    all_to_all x1, starting transfers between devices, send_all(): lax.all_to_all(copies, 'dp', 0, 0, tiled=True, axis_index_groups=groups)  7.66 us
    all_to_all x1, waiting for transfers between devices, on_device(): pooled = lax.all_to_all(pool, 'dp', 0, 0, tiled=True)  6.8 us
  transfers between devices with their start and end apart: 13, of which 3 were waited for; matrix products, arithmetic and copies ran while one was open for 0% of the time, Pallas kernels for 6%

profile of v11, /device:TPU:1, one launch (start us, length us, event | category | flops | bytes accessed | tf_op | source)
XLA Modules:
  0.0 140.7 jit_solution(8080509627909075556)
XLA Ops:
  7.2 2.1 %shard_map.182 = (bf16[16,3584]{1,0:T(8,128)(2,1)}, bf16[8,16,2048]{2,1,0:T(8,128)(2,1)}) custom-call(s32[1,77]{1,0:T(1,128)} %ids_ref.1, bf16[77,768]{1,0:T(8,128)(2,1)} %bitcast.26, bf16[16,1536]{1,0:T(8,128)(2,1)} %qkv_ref.1, bf16[12,768]{1,0:T(8,128)(2,1)} %text_ref.1, bf16[8,1024]{1,0:T(8,128)(2,1)} %out_s_ref.1, bf16[8,1024]{1,0:T(8,128)(2,1)} %out_t_ref.1, ...), custom_call_target="tpu_custom_call" | custom-call | tf_op jit(solution)/shard_map/pallas_call | solution.py:386
  9.3 0.0 copy-start.2
  9.3 7.7 %all-to-all-start = ((bf16[8,16,2048]{2,1,0:T(8,128)(2,1)}), bf16[8,16,2048]{2,1,0:T(8,128)(2,1)S(1)}, u32[]{:S(2)}, u32[]{:S(2)}) async-start(bf16[8,16,2048]{2,1,0:T(8,128)(2,1)} %get-tuple-element.36), calls=%async_computation | async-start | bytes 1048576 | tf_op jit(solution)/shard_map/all_to_all | solution.py:361
  16.9 0.0 all-gather.2.cloned.1.call-start
  17.0 12.8 %all_gather.6 = bf16[64,3584]{1,0:T(8,128)(2,1)} all-gather(bf16[16,3584]{1,0:T(8,128)(2,1)} %get-tuple-element.37), channel_id=1, replica_groups={{0,128,256,384},{8,136,264,392},{16,144,272,400},{24,152,280,408},{32,1..., dimensions={0}, use_global_device_ids=true | all-gather | bytes 573440 | tf_op jit(solution)/shard_map/all_gather | solution.py:412
  29.8 1.9 %all-to-all-done = bf16[8,16,2048]{2,1,0:T(8,128)(2,1)S(1)} async-done(((bf16[8,16,2048]{2,1,0:T(8,128)(2,1)}), bf16[8,16,2048]{2,1,0:T(8,128)(2,1)S(1)}, u32[]{:S(2)}, u32[]{:S(2)}) %all-to-all-start) | async-done | bytes 524320 | tf_op jit(solution)/shard_map/all_to_all | solution.py:361
  31.7 0.0 all-gather.2.cloned.1.call-update
  31.7 6.3 %collective-permute-start = (bf16[128,2048]{1,0:T(8,128)(2,1)S(1)}, bf16[128,2048]{1,0:T(8,128)(2,1)S(1)}, u32[]{:S(2)}, u32[]{:S(2)}) collective-permute-start(bf16[128,2048]{1,0:T(8,128)(2,1)S(1)} %bitcast.14), channel_id=1, source_target_pairs={{0,128},{8,136},{16,144},{24,152},{32,160},{40,168},{48,176},{56,1... | collective-permute-start | bytes 1572872 | tf_op jit(solution)/shard_map/ppermute | solution.py:417
  38.1 3.2 %collective-permute-start.1 = (bf16[128,2048]{1,0:T(8,128)(2,1)S(1)}, bf16[128,2048]{1,0:T(8,128)(2,1)S(1)}, u32[]{:S(2)}, u32[]{:S(2)}) collective-permute-start(bf16[128,2048]{1,0:T(8,128)(2,1)S(1)} %bitcast.15), channel_id=1, source_target_pairs={{0,384},{8,392},{16,400},{24,408},{32,416},{40,424},{48,432},{56,4... | collective-permute-start | bytes 1572872 | tf_op jit(solution)/shard_map/ppermute | solution.py:417
  41.3 10.2 %all-to-all-start.1 = ((bf16[8,32,1024]{2,1,0:T(8,128)(2,1)}), bf16[8,32,1024]{2,1,0:T(8,128)(2,1)S(1)}, u32[]{:S(2)}, u32[]{:S(2)}) async-start(bf16[8,32,1024]{2,1,0:T(8,128)(2,1)} %bitcast.5), calls=%async_computation.1 | async-start | bytes 1048576 | tf_op jit(solution)/shard_map/all_to_all | solution.py:418
  51.5 0.1 pad_add_fusion.place_ref
  51.6 0.0 copy-done.2
  51.6 2.2 %shard_map.183 = (bf16[256,512]{1,0:T(8,128)(2,1)S(1)}, bf16[256,512]{1,0:T(8,128)(2,1)S(1)}, bf16[512,512]{1,0:T(8,128)(2,1)S(1)}) custom-call(s32[2]{0:T(128)S(1)} %pad_add_fusion.place_ref, bf16[256,1024]{1,0:T(8,128)(2,1)} %bitcast.2.tokens_ref, f32[1,1024]{1,0:T(1,128)S(1)} %bitcast.23), custom_call_target="tpu_custom_call" | custom-call | flops 1073741824 | tf_op jit(solution)/shard_map/pallas_call | solution.py:420
  53.8 0.0 collective-permute-done.rest_2_
  53.8 1.9 %collective-permute-start.5 = (bf16[64,2048]{1,0:T(8,128)(2,1)S(1)}, bf16[64,2048]{1,0:T(8,128)(2,1)S(1)}, u32[]{:S(2)}, u32[]{:S(2)}) collective-permute-start(bf16[64,2048]{1,0:T(8,128)(2,1)S(1)} %slice.8), channel_id=1, source_target_pairs={{0,128},{8,136},{16,144},{24,152},{32,160},{40,168},{48,176},{56,1... | collective-permute-start | bytes 786440 | tf_op jit(solution)/shard_map/ppermute | solution.py:429
  55.8 0.0 collective-permute-done.1.rest_4_
  55.8 0.0 copy-start
  55.8 4.6 %collective-permute-start.7 = (bf16[64,2048]{1,0:T(8,128)(2,1)S(1)}, bf16[64,2048]{1,0:T(8,128)(2,1)S(1)}, u32[]{:S(2)}, u32[]{:S(2)}) collective-permute-start(bf16[64,2048]{1,0:T(8,128)(2,1)S(1)} %slice.9), channel_id=1, source_target_pairs={{0,384},{8,392},{16,400},{24,408},{32,416},{40,424},{48,432},{56,4... | collective-permute-start | bytes 786440 | tf_op jit(solution)/shard_map/ppermute | solution.py:429
  60.4 3.8 %collective-permute-start.3 = (bf16[128,2048]{1,0:T(8,128)(2,1)S(1)}, bf16[128,2048]{1,0:T(8,128)(2,1)S(1)}, u32[]{:S(2)}, u32[]{:S(2)}) collective-permute-start(bf16[128,2048]{1,0:T(8,128)(2,1)S(1)} %collective-permute-done.rest_2_), channel_id=1, source_target_pairs={{0,8},{8,0},{16,24},{24,16},{32,40},{40,32},{48,56},{56,48},{64,72... | collective-permute-start | bytes 1572872 | tf_op jit(solution)/shard_map/ppermute | solution.py:432
  64.2 1.9 %collective-permute-start.4 = (bf16[128,2048]{1,0:T(8,128)(2,1)S(1)}, bf16[128,2048]{1,0:T(8,128)(2,1)S(1)}, u32[]{:S(2)}, u32[]{:S(2)}) collective-permute-start(bf16[128,2048]{1,0:T(8,128)(2,1)S(1)} %collective-permute-done.1.rest_4_), channel_id=1, source_target_pairs={{0,8},{8,0},{16,24},{24,16},{32,40},{40,32},{48,56},{56,48},{64,72... | collective-permute-start | bytes 1572872 | tf_op jit(solution)/shard_map/ppermute | solution.py:432
  66.1 2.4 %collective-permute-start.2 = (bf16[128,2048]{1,0:T(8,128)(2,1)S(1)}, bf16[128,2048]{1,0:T(8,128)(2,1)S(1)}, u32[]{:S(2)}, u32[]{:S(2)}) collective-permute-start(bf16[128,2048]{1,0:T(8,128)(2,1)S(1)} %bitcast.16), channel_id=1, source_target_pairs={{0,8},{8,0},{16,24},{24,16},{32,40},{40,32},{48,56},{56,48},{64,72... | collective-permute-start | bytes 1572872 | tf_op jit(solution)/shard_map/ppermute | solution.py:430
  68.6 0.0 collective-permute-done.5.rest_6_
  68.6 1.9 %collective-permute-start.6 = (bf16[64,2048]{1,0:T(8,128)(2,1)S(1)}, bf16[64,2048]{1,0:T(8,128)(2,1)S(1)}, u32[]{:S(2)}, u32[]{:S(2)}) collective-permute-start(bf16[64,2048]{1,0:T(8,128)(2,1)S(1)} %collective-permute-done.5.rest_6_), channel_id=1, source_target_pairs={{0,8},{8,0},{16,24},{24,16},{32,40},{40,32},{48,56},{56,48},{64,72... | collective-permute-start | bytes 786440 | tf_op jit(solution)/shard_map/ppermute | solution.py:434
  70.5 0.0 collective-permute-done.7.rest_8_
  70.5 2.4 %collective-permute-start.8 = (bf16[64,2048]{1,0:T(8,128)(2,1)S(1)}, bf16[64,2048]{1,0:T(8,128)(2,1)S(1)}, u32[]{:S(2)}, u32[]{:S(2)}) collective-permute-start(bf16[64,2048]{1,0:T(8,128)(2,1)S(1)} %collective-permute-done.7.rest_8_), channel_id=1, source_target_pairs={{0,8},{8,0},{16,24},{24,16},{32,40},{40,32},{48,56},{56,48},{64,72... | collective-permute-start | bytes 786440 | tf_op jit(solution)/shard_map/ppermute | solution.py:434
  72.9 0.0 collective-permute-done.6.rest_7_
  72.9 1.2 collective-permute-done.8.rest_9_
  74.1 0.0 collective-permute-done.3.rest_3_
  74.1 0.0 collective-permute-done.4.rest_5_
  74.1 0.0 collective-permute-done.2.rest_1_
  74.1 2.4 %shard_map.184 = (bf16[256,512]{1,0:T(8,128)(2,1)S(1)}, bf16[512,1024]{1,0:T(8,128)(2,1)S(1)}) custom-call(bf16[256,512]{1,0:T(8,128)(2,1)S(1)} %get-tuple-element.44.own_ref, bf16[256,512]{1,0:T(8,128)(2,1)S(1)} %get-tuple-element.45.other_ref, bf16[512,512]{1,0:T(8,128)(2,1)S(1)} %get-tuple-element.46.pick_ref, bf16[128,2048]{1,0:T(8,128)(2,1)S(1)} %bitcast.17, ...), custom_call_target="tpu_custom_call" | custom-call | tf_op jit(solution)/shard_map/pallas_call | solution.py:435
  76.5 0.0 all-to-all-done.1
  76.5 18.1 %all_to_all.25 = bf16[8,32,512]{2,1,0:T(8,128)(2,1)S(1)} all-to-all(bf16[8,32,512]{2,1,0:T(8,128)(2,1)S(1)} %bitcast.20), channel_id=1, replica_groups=mesh['dp'=64,'frame'=8] {'frame'}, dimensions={0} | all-to-all | bytes 524288 | tf_op jit(solution)/shard_map/all_to_all | solution.py:443
  94.6 0.0 all-gather.2.cloned.1.call-done
  94.6 0.0 copy-done
  94.6 0.0 copy-start.3
  94.6 0.0 copy-start.4
  94.6 5.7 %shard_map.185 = (bf16[256,1024]{1,0:T(8,128)(2,1)}, f32[8,8,128]{2,1,0:T(8,128)S(1)}) custom-call(bf16[256,1024]{1,0:T(8,128)(2,1)S(1)} %bitcast.18, bf16[256,512]{1,0:T(8,128)(2,1)S(1)} %bitcast.19, bf16[512,1024]{1,0:T(8,128)(2,1)S(1)} %get-tuple-element.55.weight_ref, f32[1,1024]{1,0:T(1,128)S(1)} %bitcast.21, bf16[8,2,4,16,3584]{4,3,2,1,0:T(8,128)(2,1)} %bitcast.24), custom_call_target="tpu_custom_call" | custom-call | tf_op jit(solution)/shard_map/pallas_call | solution.py:444
  100.4 9.2 %all_to_all.26.parts_ref = f32[8,8,128]{2,1,0:T(8,128)S(1)} all-to-all(f32[8,8,128]{2,1,0:T(8,128)S(1)} %get-tuple-element.58), channel_id=1, replica_groups=mesh['dp'=64,'frame'=8] {'frame'}, dimensions={0} | all-to-all | bytes 65536 | tf_op jit(solution)/shard_map/all_to_all | solution.py:474
  109.6 0.7 shard_map.186
  110.4 8.2 %all-to-all-start.4 = ((f32[64,8,128]{2,1,0:T(8,128)}), f32[64,8,128]{2,1,0:T(8,128)S(1)}, u32[]{:S(2)}, u32[]{:S(2)}) async-start(f32[64,8,128]{2,1,0:T(8,128)} %shard_map.186), calls=%async_computation.4 | async-start | bytes 524288 | tf_op jit(solution)/shard_map/all_to_all | solution.py:476
  118.6 0.0 copy-done.3
  118.6 0.0 copy-done.4
  118.6 0.1 copy.20.pairs_ref
  119.4 0.0 copy-start.1
  119.4 4.4 %shard_map.187 = (f32[64,768]{1,0:T(8,128)S(1)}, f32[64,768]{1,0:T(8,128)S(1)}, bf16[768,768]{1,0:T(8,128)(2,1)S(1)}, bf16[4,8,2,16,768]{4,3,2,1,0:T(8,128)(2,1)S(1)}) custom-call(f32[1,768]{1,0:T(1,128)S(1)} %reshape.75.gain_ref.gain_text_ref, bf16[8,2,4,16,3584]{4,3,2,1,0:T(8,128)(2,1)} %bitcast.25), custom_call_target="tpu_custom_call" | custom-call | tf_op jit(solution)/shard_map/pallas_call | solution.py:463
  123.8 6.8 %all-to-all-done.4.pooled_ref = f32[64,8,128]{2,1,0:T(8,128)S(1)} async-done(((f32[64,8,128]{2,1,0:T(8,128)}), f32[64,8,128]{2,1,0:T(8,128)S(1)}, u32[]{:S(2)}, u32[]{:S(2)}) %all-to-all-start.4) | async-done | bytes 262176 | tf_op jit(solution)/shard_map/all_to_all | solution.py:476
  130.6 0.0 copy-done.1
  130.6 3.2 %shard_map.188 = (f32[1]{0:T(128)}, f32[1]{0:T(128)}, f32[1,1024]{1,0:T(1,128)}, f32[1,768]{1,0:T(1,128)}) custom-call(s32[1]{0:T(128)} %bitcast.3.place_ref, f32[1]{0:T(128)S(6)} %copy.21.scale_ref, s32[64,1]{1,0:T(8,128)S(1)} %copy.20.pairs_ref, f32[64,8,128]{2,1,0:T(8,128)S(1)} %all-to-all-done.4.pooled_ref, ...), custom_call_target="tpu_custom_call" | custom-call | tf_op jit(solution)/shard_map/pallas_call | solution.py:477
  (3 shorter events, 0.0 us)
Async XLA Ops:
  9.3 42.3 %copy-start.2 = (f32[1024]{0:T(1024)S(1)}, f32[1024]{0:T(1024)}, u32[]{:S(2)}) copy-start(f32[1024]{0:T(1024)} %param.20) | copy-start | bytes 12292
  9.3 22.4 %all-to-all-start = ((bf16[8,16,2048]{2,1,0:T(8,128)(2,1)}), bf16[8,16,2048]{2,1,0:T(8,128)(2,1)S(1)}, u32[]{:S(2)}, u32[]{:S(2)}) async-start(bf16[8,16,2048]{2,1,0:T(8,128)(2,1)} %get-tuple-element.36), calls=%async_computation | async-start | bytes 1048576 | tf_op jit(solution)/shard_map/all_to_all | solution.py:361
  16.9 77.7 %all-gather.2.cloned.1.call-start = ((), (), s32[]{:S(2)}) async-start(), calls=%async_computation.5 | async-start | bytes 7798784 | tf_op jit(solution)/shard_map/all_gather | solution.py:414
  31.7 22.1 %collective-permute-start = (bf16[128,2048]{1,0:T(8,128)(2,1)S(1)}, bf16[128,2048]{1,0:T(8,128)(2,1)S(1)}, u32[]{:S(2)}, u32[]{:S(2)}) collective-permute-start(bf16[128,2048]{1,0:T(8,128)(2,1)S(1)} %bitcast.14), channel_id=1, source_target_pairs={{0,128},{8,136},{16,144},{24,152},{32,160},{40,168},{48,176},{56,1... | collective-permute-start | bytes 1572872 | tf_op jit(solution)/shard_map/ppermute | solution.py:417
  38.1 17.7 %collective-permute-start.1 = (bf16[128,2048]{1,0:T(8,128)(2,1)S(1)}, bf16[128,2048]{1,0:T(8,128)(2,1)S(1)}, u32[]{:S(2)}, u32[]{:S(2)}) collective-permute-start(bf16[128,2048]{1,0:T(8,128)(2,1)S(1)} %bitcast.15), channel_id=1, source_target_pairs={{0,384},{8,392},{16,400},{24,408},{32,416},{40,424},{48,432},{56,4... | collective-permute-start | bytes 1572872 | tf_op jit(solution)/shard_map/ppermute | solution.py:417
  41.3 35.3 %all-to-all-start.1 = ((bf16[8,32,1024]{2,1,0:T(8,128)(2,1)}), bf16[8,32,1024]{2,1,0:T(8,128)(2,1)S(1)}, u32[]{:S(2)}, u32[]{:S(2)}) async-start(bf16[8,32,1024]{2,1,0:T(8,128)(2,1)} %bitcast.5), calls=%async_computation.1 | async-start | bytes 1048576 | tf_op jit(solution)/shard_map/all_to_all | solution.py:418
  53.8 14.7 %collective-permute-start.5 = (bf16[64,2048]{1,0:T(8,128)(2,1)S(1)}, bf16[64,2048]{1,0:T(8,128)(2,1)S(1)}, u32[]{:S(2)}, u32[]{:S(2)}) collective-permute-start(bf16[64,2048]{1,0:T(8,128)(2,1)S(1)} %slice.8), channel_id=1, source_target_pairs={{0,128},{8,136},{16,144},{24,152},{32,160},{40,168},{48,176},{56,1... | collective-permute-start | bytes 786440 | tf_op jit(solution)/shard_map/ppermute | solution.py:429
  55.8 38.8 %copy-start = (f32[1024]{0:T(1024)S(1)}, f32[1024]{0:T(1024)}, u32[]{:S(2)}) copy-start(f32[1024]{0:T(1024)} %param.21) | copy-start | bytes 12292
  55.8 14.7 %collective-permute-start.7 = (bf16[64,2048]{1,0:T(8,128)(2,1)S(1)}, bf16[64,2048]{1,0:T(8,128)(2,1)S(1)}, u32[]{:S(2)}, u32[]{:S(2)}) collective-permute-start(bf16[64,2048]{1,0:T(8,128)(2,1)S(1)} %slice.9), channel_id=1, source_target_pairs={{0,384},{8,392},{16,400},{24,408},{32,416},{40,424},{48,432},{56,4... | collective-permute-start | bytes 786440 | tf_op jit(solution)/shard_map/ppermute | solution.py:429
  60.4 13.7 %collective-permute-start.3 = (bf16[128,2048]{1,0:T(8,128)(2,1)S(1)}, bf16[128,2048]{1,0:T(8,128)(2,1)S(1)}, u32[]{:S(2)}, u32[]{:S(2)}) collective-permute-start(bf16[128,2048]{1,0:T(8,128)(2,1)S(1)} %collective-permute-done.rest_2_), channel_id=1, source_target_pairs={{0,8},{8,0},{16,24},{24,16},{32,40},{40,32},{48,56},{56,48},{64,72... | collective-permute-start | bytes 1572872 | tf_op jit(solution)/shard_map/ppermute | solution.py:432
  64.2 9.9 %collective-permute-start.4 = (bf16[128,2048]{1,0:T(8,128)(2,1)S(1)}, bf16[128,2048]{1,0:T(8,128)(2,1)S(1)}, u32[]{:S(2)}, u32[]{:S(2)}) collective-permute-start(bf16[128,2048]{1,0:T(8,128)(2,1)S(1)} %collective-permute-done.1.rest_4_), channel_id=1, source_target_pairs={{0,8},{8,0},{16,24},{24,16},{32,40},{40,32},{48,56},{56,48},{64,72... | collective-permute-start | bytes 1572872 | tf_op jit(solution)/shard_map/ppermute | solution.py:432
  66.1 8.0 %collective-permute-start.2 = (bf16[128,2048]{1,0:T(8,128)(2,1)S(1)}, bf16[128,2048]{1,0:T(8,128)(2,1)S(1)}, u32[]{:S(2)}, u32[]{:S(2)}) collective-permute-start(bf16[128,2048]{1,0:T(8,128)(2,1)S(1)} %bitcast.16), channel_id=1, source_target_pairs={{0,8},{8,0},{16,24},{24,16},{32,40},{40,32},{48,56},{56,48},{64,72... | collective-permute-start | bytes 1572872 | tf_op jit(solution)/shard_map/ppermute | solution.py:430
  68.6 4.4 %collective-permute-start.6 = (bf16[64,2048]{1,0:T(8,128)(2,1)S(1)}, bf16[64,2048]{1,0:T(8,128)(2,1)S(1)}, u32[]{:S(2)}, u32[]{:S(2)}) collective-permute-start(bf16[64,2048]{1,0:T(8,128)(2,1)S(1)} %collective-permute-done.5.rest_6_), channel_id=1, source_target_pairs={{0,8},{8,0},{16,24},{24,16},{32,40},{40,32},{48,56},{56,48},{64,72... | collective-permute-start | bytes 786440 | tf_op jit(solution)/shard_map/ppermute | solution.py:434
  70.5 3.6 %collective-permute-start.8 = (bf16[64,2048]{1,0:T(8,128)(2,1)S(1)}, bf16[64,2048]{1,0:T(8,128)(2,1)S(1)}, u32[]{:S(2)}, u32[]{:S(2)}) collective-permute-start(bf16[64,2048]{1,0:T(8,128)(2,1)S(1)} %collective-permute-done.7.rest_8_), channel_id=1, source_target_pairs={{0,8},{8,0},{16,24},{24,16},{32,40},{40,32},{48,56},{56,48},{64,72... | collective-permute-start | bytes 786440 | tf_op jit(solution)/shard_map/ppermute | solution.py:434
  94.6 24.0 %copy-start.3 = (f32[768]{0:T(1024)S(1)}, f32[768]{0:T(1024)}, u32[]{:S(2)}) copy-start(f32[768]{0:T(1024)} %param.23) | copy-start | bytes 9220
  94.6 24.0 %copy-start.4 = (s32[64]{0:T(128)S(1)}, s32[64]{0:T(128)}, u32[]{:S(2)}) copy-start(s32[64]{0:T(128)} %param.18) | copy-start | bytes 772
  110.4 20.2 %all-to-all-start.4 = ((f32[64,8,128]{2,1,0:T(8,128)}), f32[64,8,128]{2,1,0:T(8,128)S(1)}, u32[]{:S(2)}, u32[]{:S(2)}) async-start(f32[64,8,128]{2,1,0:T(8,128)} %shard_map.186), calls=%async_computation.4 | async-start | bytes 524288 | tf_op jit(solution)/shard_map/all_to_all | solution.py:476
  119.4 11.2 %copy-start.1 = (f32[1024]{0:T(1024)S(1)}, f32[1024]{0:T(1024)}, u32[]{:S(2)}) copy-start(f32[1024]{0:T(1024)} %param.22) | copy-start | bytes 12292
Sparse Core Ops, SparseCore 0:
  31.8 57.3 all-gather.1
